TPU v7x, 32 devices: a whole 2x2x4 slice. The times are simulated.
32 devices in a mesh: lat: 8 (over z, core), lon: 4 (over y, x).
Axes of the slice: x: 2, y: 2, z: 4, core: 2. Of those that a mesh axis runs over, the one named last changes fastest.
Arguments:
- tokens: bfloat16 [4, 48, 96, 192], P(None, 'lat', 'lon'), may hold values from -6 to 6
- cotangent: bfloat16 [4, 48, 96, 192], P(None, 'lat', 'lon'), may hold values from -6 to 6
- norm_gain: float32 [192], replicated, may hold values from 0.1 to 1.9
- inproj_weight: bfloat16 [192, 576], replicated, may hold values from -0.4375 to 0.4375
- outproj_weight: bfloat16 [192, 192], replicated, may hold values from -0.4375 to 0.4375
- bias: float32 [2, 8, 6, 144, 144], P(None, 'lat'), may hold values from -4 to 4
Outputs:
- grad_input: bfloat16 [4, 48, 96, 192], P(None, 'lat', 'lon')
- bias_grad: float32 [2, 8, 6, 144, 144], P(None, 'lat', None, 'lon')
All inputs are finite; a program needn't handle non-finite values.
Results may differ from a plain program's by a relative error of at most 0.017.
Values may be sent and summed in bfloat16 or wider, within the bound.
No kernel may reach another device: no remote copies, remote signals or barrier semaphores. Data moves between devices by JAX's collectives and lax.ppermute only.
A program may use at most 64 MiB of HBM per device.

v0:
```python
import functools

import jax
import jax.numpy as jnp
import numpy as np
from jax import lax
from jax.experimental import pallas as pl
from jax.experimental.pallas import tpu as pltpu
from jax.sharding import PartitionSpec as P

WZ = 2
WH = 6
WW = 12
WT = WZ * WH * WW
HALF_ROWS = WH // 2
HALF_COLS = WW // 2
SIDE = 8
LEVEL = WH * WW
LANES = 128
LOG2E = 1.4426950408889634
epsilon = 1e-05
F32 = jnp.float32
BF16 = jnp.bfloat16
NT = (((1,), (1,)), ((), ()))


def dot(a, b):
    return jnp.dot(a, b, preferred_element_type=F32)


def dot_nt(a, b):
    return lax.dot_general(a, b, NT, preferred_element_type=F32)


def round_up(value, to):
    return (value + to - 1) // to * to


class Chunks:
    def __init__(self, parts, heads):
        self.parts, self.heads = parts, heads
        self.size = WT // parts
        self.main = self.size // 16 * 16
        self.rest = self.size - self.main
        self.rest_rows = round_up(heads * self.rest, 16)
        self.rows = self.main + self.rest_rows
        self.used = heads * self.main + self.rest_rows
        self.width = round_up(self.used, LANES)

    def queries(self):
        table = np.zeros((self.parts, self.rows, WT), np.float32)
        for j in range(self.parts):
            for i in range(self.main):
                table[j, i, j * self.size + i] = 1.0
            for h in range(self.heads):
                for i in range(self.rest):
                    table[j, self.main + h * self.rest + i, j * self.size + self.main + i] = 1.0
        return table

    def columns(self, j):
        lane = lax.broadcasted_iota(jnp.int32, (1, self.width), 1)
        low = self.heads * self.main
        main, left = lane, self.main + lane - low
        for h in range(1, self.heads):
            main -= jnp.where(lane >= h * self.main, self.main, 0)
            left -= jnp.where(lane >= low + h * self.rest, self.rest, 0)
        return j * self.size + jnp.where(lane < low, main, left)


def window_order(cols, c, narrow):
    last = c == cols // WW - 1
    part, side = HALF_ROWS * cols, HALF_ROWS * SIDE
    kept = cols - HALF_COLS if narrow else cols
    near = WZ * part + round_up(WZ * HALF_ROWS * kept, 16)
    table = np.zeros((WT, near + last * 2 * WZ * side), np.float32)
    for z in range(WZ):
        for r in range(WH):
            for w in range(WW):
                col = c * WW + w + HALF_COLS
                low, row = divmod(r, HALF_ROWS)
                if col >= cols:
                    at = near + (low * WZ + z) * side + row * SIDE + col - cols
                elif low:
                    at = WZ * part + (z * HALF_ROWS + row) * kept + col - (cols - kept)
                else:
                    at = z * part + row * cols + col
                table[(z * WH + r) * WW + w, at] = 1.0
    return table


def level_rows(field, a, base):
    levels = field.shape[0]
    at = [(a * WZ + WZ // 2 + z) % levels for z in range(WZ)]
    return [field[level, base + row].astype(F32) for level in at for row in range(HALF_ROWS)]


def send_kernel(both, inner, below, right, corner):
    cols = both.shape[2]
    kept = cols - HALF_COLS
    shape = (below.shape[1], WZ * HALF_ROWS * cols)
    row = lax.broadcasted_iota(jnp.int32, shape, 0)
    target = row + HALF_COLS
    for i in range(1, WZ * HALF_ROWS):
        target += jnp.where(row >= i * kept, HALF_COLS, 0)
    kept_rows = (lax.broadcasted_iota(jnp.int32, shape, 1) == target) & (row < WZ * HALF_ROWS * kept)
    narrow = kept_rows.astype(F32).astype(BF16)
    for a in range(inner.shape[0]):
        low, high = level_rows(both, a, 0), level_rows(both, a, HALF_ROWS)
        below[a] = dot(narrow, jnp.concatenate(low, axis=0).astype(BF16)).astype(BF16)
        inner[a] = jnp.concatenate(high, axis=0).astype(BF16)
        right[a] = jnp.concatenate([row[:SIDE] for row in high], axis=0).astype(BF16)
        corner[a] = jnp.concatenate([row[:SIDE] for row in low], axis=0).astype(BF16)


def prep_kernel(chunks, lat_count, bias, bias_t):
    level_windows = bias.shape[0]
    last_lat = lax.axis_index("lat") == lat_count - 1
    me = lax.axis_index("lon")
    parts, size, main = chunks.parts, chunks.size, chunks.main

    def labels(index, window):
        level_label = (index >= LEVEL) & (window == level_windows - 1)
        in_level = jnp.where(index >= LEVEL, index - LEVEL, index)
        row_label = (in_level >= LEVEL // 2) & last_lat
        return level_label.astype(jnp.int32) * 2 + row_label.astype(jnp.int32)

    key_index = lax.broadcasted_iota(jnp.int32, (WT, chunks.width), 0)
    for window in range(level_windows):
        key_labels = labels(key_index, window)
        for j in range(parts):
            heads = range(chunks.heads)
            low = j * size
            rows = []
            if main:
                rows += [bias[window, h, low : low + main, :] for h in heads]
            if chunks.rest:
                rows += [bias[window, h, low + main : low + size, :] for h in heads]
            spare = chunks.width - chunks.heads * size
            if spare:
                rows.append(jnp.zeros((spare, WT), F32))
            turned = jnp.transpose(jnp.concatenate(rows, axis=0)) * LOG2E
            allowed = key_labels == labels(chunks.columns(j), window)
            slot = me ^ j if parts & (parts - 1) == 0 else lax.rem(j - me + parts, parts)
            bias_t[window, slot] = jnp.where(allowed, turned, -1e30)


def head_masks(chunks, channels):
    head_dim = channels // chunks.heads
    lane_head = lax.broadcasted_iota(jnp.int32, (1, channels), 1) // head_dim
    lanes = [lane_head == h for h in range(chunks.heads)]
    rest = None
    if chunks.rest:
        row = lax.broadcasted_iota(jnp.int32, (chunks.rest_rows, channels), 0)
        lane = lax.broadcasted_iota(jnp.int32, (chunks.rest_rows, channels), 1) // head_dim
        rest = jnp.zeros((chunks.rest_rows, channels), F32)
        for h in range(chunks.heads):
            inside = (row >= h * chunks.rest) & (row < (h + 1) * chunks.rest) & (lane == h)
            rest = jnp.where(inside, 1.0, rest)
    return lanes, rest


def stack_heads(chunks, value, d, lane_masks, rest_mask):
    low = d * chunks.rows
    main = value[low : low + chunks.main]
    pieces = [main * mask for mask in lane_masks] if chunks.main else []
    if chunks.rest:
        pieces.append(value[low + chunks.main : low + chunks.rows] * rest_mask)
    if chunks.width > chunks.used:
        pieces.append(jnp.zeros((chunks.width - chunks.used, value.shape[1]), value.dtype))
    return jnp.concatenate(pieces, axis=0)


def split(inproj):
    channels = inproj.shape[0]
    return [inproj[:, part * channels : (part + 1) * channels] for part in range(3)]


def partner(me, d, parts):
    return me ^ d if parts & (parts - 1) == 0 else (me + d) % parts


def rolled(ref, parts):
    me = lax.axis_index("lon")
    return jnp.concatenate([ref[partner(me, d, parts)] for d in range(parts)], axis=0)


def scores_kernel(chunks, near, first, last, *refs):
    pieces, refs = refs[:near], refs[near:]
    gain_ref, inproj, outproj, bias_t, perm, queries, *refs = refs
    weights = split(inproj)
    before = None
    if not first:
        before, *refs = refs
    standard_out, scale_out, keys_out, query_out, up_out, p_out, ds_out, *totals = refs
    parts, width = chunks.parts, chunks.width
    channels = outproj.shape[0]
    scaling = (channels // chunks.heads) ** (-0.5)
    lanes, rest_mask = head_masks(chunks, channels)
    lanes = [mask.astype(F32).astype(BF16) for mask in lanes]
    rest_mask = rest_mask.astype(BF16) if chunks.rest else None
    choose = rolled(queries, parts)
    level_windows = pieces[0].shape[0]
    tile = channels // LANES * LANES
    from_tile = jnp.concatenate([jnp.zeros((channels, channels - tile), BF16), outproj[...]], axis=1)
    ts, us = [], []
    for a in range(level_windows):
        moved = dot(perm[...], jnp.concatenate([piece[a] for piece in pieces], axis=0))
        ts.append(moved[:, :channels])
        us.append(dot_nt(moved[:, tile:].astype(BF16), from_tile).astype(BF16))
    t = jnp.concatenate(ts, axis=0)
    centred = t - jnp.mean(t, axis=-1, keepdims=True)
    inverse_rms = lax.rsqrt(jnp.mean(centred * centred, axis=-1, keepdims=True) + epsilon)
    standard = centred * inverse_rms
    standard_out[...] = standard
    scale_out[...] = jnp.broadcast_to(inverse_rms, scale_out.shape)
    normed = (standard * gain_ref[...]).astype(BF16)
    q = dot(normed, weights[0]).astype(BF16)
    k = dot(normed, weights[1]).astype(BF16)
    v = dot(normed, weights[2]).astype(BF16)
    keys_out[...] = k
    for a in range(level_windows):
        cut = slice(a * WT, (a + 1) * WT)
        query = dot(choose, q[cut]).astype(BF16)
        up = dot(choose, us[a]).astype(BF16)
        query_out[a] = query
        up_out[a] = up
        for d in range(parts):
            at = slice(d * width, (d + 1) * width)
            s = dot_nt(k[cut], stack_heads(chunks, query, d, lanes, rest_mask))
            dp = dot_nt(v[cut], stack_heads(chunks, up, d, lanes, rest_mask))
            e = jnp.exp2(s * (scaling * LOG2E) + bias_t[a, d])
            p = e * (1.0 / jnp.sum(e, axis=0, keepdims=True))
            ds = p * (dp - jnp.sum(p * dp, axis=0, keepdims=True))
            p_out[a, :, at] = p.astype(BF16)
            ds_out[a, :, at] = ds.astype(BF16)
            if not first:
                ds += before[a, d]
            if last:
                totals[d][a] = ds.astype(BF16)
            else:
                totals[0][a, d] = ds


def tokens_kernel(chunks, near, first, *refs):
    standard_in, scale_in, keys, queries_in, ups, p_in, ds_in, gain_ref, inproj, perm_t, queries, *refs = refs
    weights = split(inproj)
    before = None
    if not first:
        before, refs = refs[:2], refs[2:]
    outs = refs
    parts, width = chunks.parts, chunks.width
    channels = keys.shape[-1]
    head_dim = channels // chunks.heads
    scaling = head_dim ** (-0.5)
    lanes, rest_mask = head_masks(chunks, channels)
    low_lanes = [mask.astype(F32).astype(BF16) for mask in lanes]
    low_rest = rest_mask.astype(BF16) if chunks.rest else None
    choose_t = jnp.transpose(rolled(queries, parts).astype(F32)).astype(BF16)
    level_windows = p_in.shape[0]
    dqs, dks, dvs = [], [], []
    for a in range(level_windows):
        query, up = queries_in[a], ups[a]
        qs = jnp.concatenate(
            [stack_heads(chunks, query, d, low_lanes, low_rest) for d in range(parts)], axis=0
        )
        us = jnp.concatenate(
            [stack_heads(chunks, up, d, low_lanes, low_rest) for d in range(parts)], axis=0
        )
        ds = ds_in[a]
        dks.append((dot(ds, qs) * scaling).astype(BF16))
        dvs.append(dot(p_in[a], us).astype(BF16))
        turned = jnp.transpose(ds)
        key = keys[a * WT : (a + 1) * WT]
        main = []
        for lane in range(0, channels, LANES):
            low = lane // head_dim
            many = min(LANES // head_dim, chunks.heads - low)
            if not chunks.main:
                break
            some = [turned[d * width + low * chunks.main :][: many * chunks.main] for d in range(parts)]
            flat = dot(jnp.concatenate(some, axis=0), key[:, lane : lane + LANES])
            tiles = []
            for d in range(parts):
                picked = flat[d * many * chunks.main :][: chunks.main]
                for h in range(1, many):
                    mask = lanes[low + h][:, lane : lane + LANES]
                    picked = jnp.where(mask, flat[(d * many + h) * chunks.main :][: chunks.main], picked)
                tiles.append(picked)
            main.append(tiles)
        if chunks.rest:
            low = chunks.heads * chunks.main
            some = [turned[d * width + low :][: chunks.rest_rows] for d in range(parts)]
            left = dot(jnp.concatenate(some, axis=0), key)
        rows = []
        for d in range(parts):
            if chunks.main:
                rows.append(jnp.concatenate([tiles[d] for tiles in main], axis=1))
            if chunks.rest:
                rows.append(left[d * chunks.rest_rows : (d + 1) * chunks.rest_rows] * rest_mask)
        picked = (jnp.concatenate(rows, axis=0) * scaling).astype(BF16)
        dqs.append(dot(choose_t, picked).astype(BF16))
    dq, dk, dv = (jnp.concatenate(parts_of, axis=0) for parts_of in (dqs, dks, dvs))
    scaled = (dot_nt(dq, weights[0]) + dot_nt(dk, weights[1]) + dot_nt(dv, weights[2])) * gain_ref[...]
    standard = standard_in[...]
    inverse_rms = scale_in[:, :1]
    grad = inverse_rms * (
        scaled
        - jnp.mean(scaled, axis=-1, keepdims=True)
        - standard * jnp.mean(scaled * standard, axis=-1, keepdims=True)
    )
    grad = grad.astype(BF16)
    lows = []
    for a in range(level_windows):
        spread = dot(perm_t[...], grad[a * WT : (a + 1) * WT])
        base = 0
        for i, out in enumerate(outs):
            rows = out.shape[-2]
            part = spread[base : base + rows]
            if not first and i < 2:
                part += before[i][a].astype(F32)
            if not first and i == 1:
                lows.append(part)
            else:
                out[a] = part.astype(BF16)
            base += rows
    if not first:
        packed = [low[:, :LANES] for low in lows] + [low[:, LANES:] for low in lows]
        outs[1][...] = jnp.concatenate(packed, axis=1).astype(BF16)


def join_kernel(corner, below, right, inner, after, grad_input):
    levels, _, cols, channels = grad_input.shape
    level_windows = levels // WZ
    whole = below[...].astype(F32)
    for a in range(level_windows):
        rest_at = level_windows * LANES + a * (channels - LANES)
        low = jnp.concatenate(
            [whole[:, a * LANES : (a + 1) * LANES], whole[:, rest_at : rest_at + channels - LANES]], axis=1
        )
        parts = ((low, corner[a].astype(F32), 0), (inner[a].astype(F32), right[a].astype(F32), HALF_ROWS))
        for z in range(WZ):
            level = (a * WZ + WZ // 2 + z) % levels
            for row in range(HALF_ROWS):
                at = z * HALF_ROWS + row
                for wide, side, base in parts:
                    first = wide[at * cols : at * cols + SIDE] + side[at * SIDE : (at + 1) * SIDE]
                    rest = wide[at * cols + SIDE : (at + 1) * cols]
                    grad_input[level, base + row] = jnp.concatenate([first, rest], axis=0).astype(BF16)


def bias_kernel(chunks, *refs):
    *arrived, bias_grad, after = refs
    after[...] = jnp.zeros(after.shape, F32)
    main, rest, heads = chunks.main, chunks.rest, chunks.heads
    for a in range(arrived[0].shape[0]):
        total = arrived[0][a].astype(F32)
        for other in arrived[1:]:
            total += other[a].astype(F32)
        turned = jnp.transpose(total)
        for h in range(heads):
            at = (a * heads + h) * chunks.size
            if main:
                bias_grad[at : at + main, 0, :] = turned[h * main : (h + 1) * main]
            if rest:
                low = heads * main + h * rest
                bias_grad[at + main : at + chunks.size, 0, :] = turned[low : low + rest]


def vmem(count):
    return [pl.BlockSpec(memory_space=pltpu.VMEM)] * count


def call(kernel, outs, args, flops=0):
    return pl.pallas_call(
        kernel,
        out_shape=outs,
        in_specs=vmem(len(args)),
        out_specs=vmem(len(outs)),
        compiler_params=pltpu.CompilerParams(vmem_limit_bytes=40 * 2**20),
        cost_estimate=pl.CostEstimate(flops=flops, bytes_accessed=0, transcendentals=0),
    )(*args)


def shift(value, rows, cols):
    lat_count, lon_count = lax.axis_size("lat"), lax.axis_size("lon")
    pairs = []
    for i in range(lat_count):
        for j in range(lon_count):
            to = (i + rows) % lat_count * lon_count + (j + cols) % lon_count
            pairs.append((i * lon_count + j, to))
    return lax.ppermute(value, ("lat", "lon"), pairs)


def local(tokens, cotangent, norm_gain, inproj_weight, outproj_weight, bias):
    levels, rows, cols, channels = tokens.shape
    level_windows, _, heads = bias.shape[:3]
    lat_count, lon_count = lax.axis_size("lat"), lax.axis_size("lon")
    chunks = Chunks(lon_count, heads)
    windows = cols // WW
    struct = jax.ShapeDtypeStruct
    half, side = WZ * HALF_ROWS * cols, WZ * HALF_ROWS * SIDE
    gain = norm_gain.reshape(1, channels)
    queries = jnp.asarray(chunks.queries(), BF16)

    bias = bias.reshape(level_windows, heads, WT, WT)
    both = jnp.concatenate([tokens, cotangent], axis=-1)
    narrow = round_up(WZ * HALF_ROWS * (cols - HALF_COLS), 16)
    inner, below, right, corner = call(
        send_kernel,
        [struct((level_windows, size, 2 * channels), BF16) for size in (half, narrow, side, side)],
        (both,),
    )
    below = shift(below, -1, 0)
    right = shift(right, 0, -1)
    corner = shift(corner, -1, -1)
    (bias_t,) = call(
        functools.partial(prep_kernel, chunks, lat_count),
        [struct((level_windows, lon_count, WT, chunks.width), F32)],
        (bias,),
    )
    per_window = []
    total = []
    for c in range(windows):
        last = c == windows - 1
        pieces = (inner, below) + ((right, corner) if last else ())
        if last:
            sums = [struct((level_windows, WT, chunks.width), BF16)] * lon_count
        else:
            sums = [struct((level_windows, lon_count, WT, chunks.width), F32)]
        order = jnp.asarray(window_order(cols, c, True), BF16)
        results = call(
            functools.partial(scores_kernel, chunks, len(pieces), c == 0, last),
            [
                struct((level_windows * WT, channels), F32),
                struct((level_windows * WT, LANES), F32),
                struct((level_windows * WT, channels), BF16),
                struct((level_windows, lon_count * chunks.rows, channels), BF16),
                struct((level_windows, lon_count * chunks.rows, channels), BF16),
                struct((level_windows, WT, lon_count * chunks.width), BF16),
                struct((level_windows, WT, lon_count * chunks.width), BF16),
            ]
            + sums,
            (*pieces, gain, inproj_weight, outproj_weight, bias_t, order, queries, *total),
            flops=10**9,
        )
        per_window.append(results[:7])
        total = results[7:]
    arrived = [total[0]]
    for d in range(1, lon_count):
        pairs = [(i, partner(i, d, lon_count)) for i in range(lon_count)]
        arrived.append(lax.ppermute(total[d], "lon", pairs))
    wide = struct((level_windows, half, channels), BF16)
    thin = struct((level_windows, side, channels), BF16)
    grads = []
    for c in reversed(range(windows)):
        last = c == windows - 1
        order = jnp.asarray(window_order(cols, c, False).T, BF16)
        results = call(
            functools.partial(tokens_kernel, chunks, 2, last),
            [wide, wide, thin, thin] if last else [wide, struct((half, level_windows * channels), BF16)],
            (*per_window[c], gain, inproj_weight, order, queries, *grads),
        )
        grads = results[:2]
        if last:
            left, corner = shift(results[2], 0, 1), shift(results[3], 1, 1)
    above = shift(grads[1], 1, 0)
    bias_grad, after = call(
        functools.partial(bias_kernel, chunks),
        [struct((level_windows * heads * chunks.size, 1, WT), F32), struct((8, LANES), F32)],
        arrived,
    )
    (grad_input,) = call(join_kernel, [struct(tokens.shape, BF16)], (corner, above, left, grads[0], after))
    bias_grad = bias_grad.reshape(level_windows, heads, chunks.size, 1, WT)
    return grad_input, jnp.transpose(bias_grad, (0, 3, 1, 2, 4))


def solution(mesh):
    placed = (
        P(None, "lat", "lon", None),
        P(None, "lat", "lon", None),
        P(),
        P(),
        P(),
        P(None, "lat", None, None, None),
    )
    return jax.shard_map(
        local,
        mesh=mesh,
        in_specs=placed,
        out_specs=(P(None, "lat", "lon", None), P(None, "lat", None, "lon", None)),
        check_vma=False,
    )
```

profile of v0, /device:TPU:0, one launch (start us, length us, event | category | flops | bytes accessed | tf_op | source)
XLA Modules:
  0.0 30.6 jit_solution(3286138319962986021)
XLA Ops:
  0.6 1.2 %pad_maximum_fusion.both = bf16[4,6,24,384]{3,2,1,0:T(8,128)(2,1)S(1)} fusion(bf16[4,6,24,192]{3,2,1,0:T(8,128)(2,1)} %param.12, bf16[4,6,24,192]{3,2,1,0:T(8,128)(2,1)} %param.11), kind=kLoop, calls=%fused_computation | loop fusion | flops 884736 | bytes 884736 | tf_op jit(solution)/shard_map/concatenate | solution.py:406
  1.8 0.2 shard_map.122
  2.1 4.5 %collective-permute-start = (bf16[2,112,384]{2,1,0:T(8,128)(2,1)S(1)}, bf16[2,112,384]{2,1,0:T(8,128)(2,1)S(1)}, u32[]{:S(2)}, u32[]{:S(2)}) collective-permute-start(bf16[2,112,384]{2,1,0:T(8,128)(2,1)S(1)} %get-tuple-element.34), channel_id=1, source_target_pairs={{0,28},{1,29},{2,30},{3,31},{4,0},{5,1},{6,2},{7,3},{8,4},{9,5},{1... | collective-permute-start | bytes 516104 | tf_op jit(solution)/shard_map/ppermute | solution.py:391
  6.6 2.4 %collective-permute-start.1 = (bf16[2,48,384]{2,1,0:T(8,128)(2,1)S(1)}, bf16[2,48,384]{2,1,0:T(8,128)(2,1)S(1)}, u32[]{:S(2)}, u32[]{:S(2)}) collective-permute-start(bf16[2,48,384]{2,1,0:T(8,128)(2,1)S(1)} %get-tuple-element.35), channel_id=1, source_target_pairs={{0,3},{1,0},{2,1},{3,2},{4,7},{5,4},{6,5},{7,6},{8,11},{9,8},{10,9... | collective-permute-start | bytes 221192 | tf_op jit(solution)/shard_map/ppermute | solution.py:391
  9.1 0.4 %collective-permute-start.2 = (bf16[2,48,384]{2,1,0:T(8,128)(2,1)S(1)}, bf16[2,48,384]{2,1,0:T(8,128)(2,1)S(1)}, u32[]{:S(2)}, u32[]{:S(2)}) collective-permute-start(bf16[2,48,384]{2,1,0:T(8,128)(2,1)S(1)} %get-tuple-element.36), channel_id=1, source_target_pairs={{0,31},{1,28},{2,29},{3,30},{4,3},{5,0},{6,1},{7,2},{8,7},{9,4},{1... | collective-permute-start | bytes 221192 | tf_op jit(solution)/shard_map/ppermute | solution.py:391
  9.4 0.0 copy-start
  9.4 1.5 %copy-done = f32[2,1,6,144,144]{4,3,2,1,0:T(8,128)S(1)} copy-done((f32[2,1,6,144,144]{4,3,2,1,0:T(8,128)S(1)}, f32[2,1,6,144,144]{4,3,2,1,0:T(8,128)}, u32[]{:S(2)}) %copy-start) | copy-done | bytes 995352
  10.9 0.0 copy-start.1
  10.9 0.0 copy-start.2
  10.9 0.0 copy-start.5
  10.9 0.0 copy-start.6
  10.9 0.0 copy-start.8
  10.9 0.6 %shard_map.123.refs_5_.refs_7_ = f32[2,4,144,256]{3,2,1,0:T(8,128)S(1)} custom-call(f32[2,6,144,144]{3,2,1,0:T(8,128)S(1)} %bitcast.3), custom_call_target="tpu_custom_call" | custom-call | tf_op jit(solution)/shard_map/pallas_call | solution.py:374
  11.5 0.0 collective-permute-done.refs_1_
  11.5 0.3 %copy-done.1 = bf16[192,576]{1,0:T(8,128)(2,1)S(1)} copy-done((bf16[192,576]{1,0:T(8,128)(2,1)S(1)}, bf16[192,576]{1,0:T(8,128)(2,1)}, u32[]{:S(2)}) %copy-start.1) | copy-done | bytes 221208
  11.8 0.1 copy-done.2
  11.9 0.0 copy-done.5
  11.9 0.1 copy-done.6
  12.0 0.0 copy-done.8
  12.0 0.0 copy-start.7
  12.0 1.7 %shard_map.124 = (f32[288,192]{1,0:T(8,128)S(1)}, f32[288,128]{1,0:T(8,128)S(1)}, bf16[288,192]{1,0:T(8,128)(2,1)S(1)}, bf16[2,256,192]{2,1,0:T(8,128)(2,1)S(1)}...) custom-call(bf16[2,144,384]{2,1,0:T(8,128)(2,1)S(1)} %get-tuple-elem, ...), custom_call_target="tpu_custom_call" | custom-call | flops 1000000000 | tf_op jit(solution)/shard_map/pallas_call | solution.py:374
  13.7 0.0 collective-permute-done.1.refs_2_
  13.7 0.0 collective-permute-done.2.refs_3_
  13.7 0.0 copy-done.7
  13.7 0.0 copy-start.3
  13.7 1.8 %shard_map.125 = (f32[288,192]{1,0:T(8,128)S(1)}, f32[288,128]{1,0:T(8,128)S(1)}, bf16[288,192]{1,0:T(8,128)(2,1)S(1)}, bf16[2,256,192]{2,1,0:T(8,128)(2,1)S(1)}...) custom-call(bf16[2,144,384]{2,1,0:T(8,128)(2,1)S(1)} %get-tuple-elem, ...), custom_call_target="tpu_custom_call" | custom-call | flops 1000000000 | tf_op jit(solution)/shard_map/pallas_call | solution.py:374
  15.5 1.6 %collective-permute-start.6 = (bf16[2,144,256]{2,1,0:T(8,128)(2,1)S(1)}, bf16[2,144,256]{2,1,0:T(8,128)(2,1)S(1)}, u32[]{:S(2)}, u32[]{:S(2)}) collective-permute-start(bf16[2,144,256]{2,1,0:T(8,128)(2,1)S(1)} %get-tuple-element.59), channel_id=1, source_target_pairs={{0,1},{1,0},{2,3},{3,2},{4,5},{5,4},{6,7},{7,6},{8,9},{9,8},{10,11... | collective-permute-start | bytes 442376 | tf_op jit(solution)/shard_map/ppermute | solution.py:451
  17.1 0.5 %collective-permute-start.7 = (bf16[2,144,256]{2,1,0:T(8,128)(2,1)S(1)}, bf16[2,144,256]{2,1,0:T(8,128)(2,1)S(1)}, u32[]{:S(2)}, u32[]{:S(2)}) collective-permute-start(bf16[2,144,256]{2,1,0:T(8,128)(2,1)S(1)} %get-tuple-element.60), channel_id=1, source_target_pairs={{0,2},{1,3},{2,0},{3,1},{4,6},{5,7},{6,4},{7,5},{8,10},{9,11},{10,... | collective-permute-start | bytes 442376 | tf_op jit(solution)/shard_map/ppermute | solution.py:451
  17.6 1.5 %collective-permute-start.8 = (bf16[2,144,256]{2,1,0:T(8,128)(2,1)S(1)}, bf16[2,144,256]{2,1,0:T(8,128)(2,1)S(1)}, u32[]{:S(2)}, u32[]{:S(2)}) collective-permute-start(bf16[2,144,256]{2,1,0:T(8,128)(2,1)S(1)} %get-tuple-element.61), channel_id=1, source_target_pairs={{0,3},{1,2},{2,1},{3,0},{4,7},{5,6},{6,5},{7,4},{8,11},{9,10},{10,... | collective-permute-start | bytes 442376 | tf_op jit(solution)/shard_map/ppermute | solution.py:451
  19.1 0.0 copy-done.3
  19.1 0.0 copy-start.4
  19.1 1.6 %shard_map.126 = (bf16[2,144,192]{2,1,0:T(8,128)(2,1)S(1)}, bf16[2,144,192]{2,1,0:T(8,128)(2,1)S(1)}, bf16[2,48,192]{2,1,0:T(8,128)(2,1)S(1)}, bf16[2,48,192]{2,1,0:T(8,128)(2,1)S(1)}) custom-call(f32[288,192]{1,0:T(8,128)S(1)} %get-tuple-element.38.refs_0_, f32[288,128]{1,0:T(8,128)S(1)} %get-tuple-element.39.refs_1_, ...), custom_call_target="tpu_custom_call" | custom-call | tf_op jit(solution)/shard_map/pallas_call | solution.py:374
  20.7 0.0 copy-done.4
  20.7 1.7 %shard_map.127 = (bf16[2,144,192]{2,1,0:T(8,128)(2,1)S(1)}, bf16[144,384]{1,0:T(8,128)(2,1)S(1)}) custom-call(f32[288,192]{1,0:T(8,128)S(1)} %get-tuple-element.46.refs_0_, f32[288,128]{1,0:T(8,128)S(1)} %get-tuple-element.47.refs_1_, bf16[288,192]{1,0:T(8,128)(2,1)S(1)} %get-tuple-element.48.refs_2_, bf16[2,256,192]{2,1,0:T(8,128)(2,1)S(1)} %get-tuple-element.49.refs_3_, ...), custom_call_target="tpu_custom_call" | custom-call | tf_op jit(solution)/shard_map/pallas_call | solution.py:374
  22.4 0.1 collective-permute-start.4
  22.5 0.6 %collective-permute-start.3 = (bf16[2,48,192]{2,1,0:T(8,128)(2,1)S(1)}, bf16[2,48,192]{2,1,0:T(8,128)(2,1)S(1)}, u32[]{:S(2)}, u32[]{:S(2)}) collective-permute-start(bf16[2,48,192]{2,1,0:T(8,128)(2,1)S(1)} %get-tuple-element.45), channel_id=1, source_target_pairs={{0,5},{1,6},{2,7},{3,4},{4,9},{5,10},{6,11},{7,8},{8,13},{9,14},{1... | collective-permute-start | bytes 110600 | tf_op jit(solution)/shard_map/ppermute | solution.py:391
  23.0 0.0 collective-permute-done.6.refs_1_
  23.1 1.0 %collective-permute-start.5 = (bf16[2,48,192]{2,1,0:T(8,128)(2,1)S(1)}, bf16[2,48,192]{2,1,0:T(8,128)(2,1)S(1)}, u32[]{:S(2)}, u32[]{:S(2)}) collective-permute-start(bf16[2,48,192]{2,1,0:T(8,128)(2,1)S(1)} %get-tuple-element.56), channel_id=1, source_target_pairs={{0,1},{1,2},{2,3},{3,0},{4,5},{5,6},{6,7},{7,4},{8,9},{9,10},{10,1... | collective-permute-start | bytes 110600 | tf_op jit(solution)/shard_map/ppermute | solution.py:391
  24.1 3.0 %collective-permute-done.7.refs_2_ = bf16[2,144,256]{2,1,0:T(8,128)(2,1)S(1)} collective-permute-done((bf16[2,144,256]{2,1,0:T(8,128)(2,1)S(1)}, bf16[2,144,256]{2,1,0:T(8,128)(2,1)S(1)}, u32[]{:S(2)}, u32[]{:S(2)}) %collective-permute-start.7) | collective-permute-done | bytes 147488 | tf_op jit(solution)/shard_map/ppermute | solution.py:451
  27.0 0.0 collective-permute-done.8.refs_3_
  27.0 1.0 %shard_map.128 = (f32[432,1,144]{2,1,0:T(1,128)}, f32[8,128]{1,0:T(8,128)S(1)}) custom-call(bf16[2,144,256]{2,1,0:T(8,128)(2,1)S(1)} %get-tuple-element.58.refs_0_, bf16[2,144,256]{2,1,0:T(8,128)(2,1)S(1)} %collective-permute-done.6.refs_1_, bf16[2,144,256]{2,1,0:T(8,128)(2,1)S(1)} %collective-permute-done.7.refs_2_, ...), custom_call_target="tpu_custom_call" | custom-call | tf_op jit(solution)/shard_map/pallas_call | solution.py:374
  28.0 1.8 %collective-permute-done.3.corner = bf16[2,48,192]{2,1,0:T(8,128)(2,1)S(1)} collective-permute-done((bf16[2,48,192]{2,1,0:T(8,128)(2,1)S(1)}, bf16[2,48,192]{2,1,0:T(8,128)(2,1)S(1)}, u32[]{:S(2)}, u32[]{:S(2)}) %collective-permute-start.3) | collective-permute-done | bytes 36896 | tf_op jit(solution)/shard_map/ppermute | solution.py:391
  29.8 0.0 collective-permute-done.5.right
  29.8 0.0 collective-permute-done.4.below
  29.8 0.8 %shard_map.129 = bf16[4,6,24,192]{3,2,1,0:T(8,128)(2,1)} custom-call(bf16[2,48,192]{2,1,0:T(8,128)(2,1)S(1)} %collective-permute-done.3.corner, bf16[144,384]{1,0:T(8,128)(2,1)S(1)} %collective-permute-done.4.below, bf16[2,48,192]{2,1,0:T(8,128)(2,1)S(1)} %collective-permute-done.5.right, bf16[2,144,192]{2,1,0:T(8,128)(2,1)S(1)} %get-tuple-element.57.inner, ...), custom_call_target="tpu_custom_call" | custom-call | tf_op jit(solution)/shard_map/pallas_call | solution.py:374
Async XLA Ops:
  2.1 9.4 %collective-permute-start = (bf16[2,112,384]{2,1,0:T(8,128)(2,1)S(1)}, bf16[2,112,384]{2,1,0:T(8,128)(2,1)S(1)}, u32[]{:S(2)}, u32[]{:S(2)}) collective-permute-start(bf16[2,112,384]{2,1,0:T(8,128)(2,1)S(1)} %get-tuple-element.34), channel_id=1, source_target_pairs={{0,28},{1,29},{2,30},{3,31},{4,0},{5,1},{6,2},{7,3},{8,4},{9,5},{1... | collective-permute-start | bytes 516104 | tf_op jit(solution)/shard_map/ppermute | solution.py:391
  6.6 7.1 %collective-permute-start.1 = (bf16[2,48,384]{2,1,0:T(8,128)(2,1)S(1)}, bf16[2,48,384]{2,1,0:T(8,128)(2,1)S(1)}, u32[]{:S(2)}, u32[]{:S(2)}) collective-permute-start(bf16[2,48,384]{2,1,0:T(8,128)(2,1)S(1)} %get-tuple-element.35), channel_id=1, source_target_pairs={{0,3},{1,0},{2,1},{3,2},{4,7},{5,4},{6,5},{7,6},{8,11},{9,8},{10,9... | collective-permute-start | bytes 221192 | tf_op jit(solution)/shard_map/ppermute | solution.py:391
  9.1 4.7 %collective-permute-start.2 = (bf16[2,48,384]{2,1,0:T(8,128)(2,1)S(1)}, bf16[2,48,384]{2,1,0:T(8,128)(2,1)S(1)}, u32[]{:S(2)}, u32[]{:S(2)}) collective-permute-start(bf16[2,48,384]{2,1,0:T(8,128)(2,1)S(1)} %get-tuple-element.36), channel_id=1, source_target_pairs={{0,31},{1,28},{2,29},{3,30},{4,3},{5,0},{6,1},{7,2},{8,7},{9,4},{1... | collective-permute-start | bytes 221192 | tf_op jit(solution)/shard_map/ppermute | solution.py:391
  9.4 1.5 %copy-start = (f32[2,1,6,144,144]{4,3,2,1,0:T(8,128)S(1)}, f32[2,1,6,144,144]{4,3,2,1,0:T(8,128)}, u32[]{:S(2)}) copy-start(f32[2,1,6,144,144]{4,3,2,1,0:T(8,128)} %param.16) | copy-start | bytes 2985988
  10.9 0.9 %copy-start.1 = (bf16[192,576]{1,0:T(8,128)(2,1)S(1)}, bf16[192,576]{1,0:T(8,128)(2,1)}, u32[]{:S(2)}) copy-start(bf16[192,576]{1,0:T(8,128)(2,1)} %refs_8_.4) | copy-start | bytes 663556
  10.9 1.0 %copy-start.2 = (bf16[4,64,144]{2,1,0:T(8,128)(2,1)S(1)}, bf16[4,64,144]{2,1,0:T(8,128)(2,1)}, u32[]{:S(2)}) copy-start(bf16[4,64,144]{2,1,0:T(8,128)(2,1)} %constant.10.clone.refs_7_.refs_9_.refs_10_) | copy-start | bytes 221188
  10.9 1.0 %copy-start.5 = (f32[192]{0:T(256)S(1)}, f32[192]{0:T(256)}, u32[]{:S(2)}) copy-start(f32[192]{0:T(256)} %param.13) | copy-start | bytes 2308
  10.9 1.1 %copy-start.6 = (bf16[192,192]{1,0:T(8,128)(2,1)S(1)}, bf16[192,192]{1,0:T(8,128)(2,1)}, u32[]{:S(2)}) copy-start(bf16[192,192]{1,0:T(8,128)(2,1)} %refs_6_.2) | copy-start | bytes 221188
  10.9 1.1 %copy-start.8 = (bf16[144,256]{1,0:T(8,128)(2,1)S(1)}, bf16[144,256]{1,0:T(8,128)(2,1)}, u32[]{:S(2)}) copy-start(bf16[144,256]{1,0:T(8,128)(2,1)} %constant.11.clone.refs_6_) | copy-start | bytes 221188
  12.0 1.7 %copy-start.7 = (bf16[144,352]{1,0:T(8,128)(2,1)S(1)}, bf16[144,352]{1,0:T(8,128)(2,1)}, u32[]{:S(2)}) copy-start(bf16[144,352]{1,0:T(8,128)(2,1)} %constant.12.clone.refs_8_) | copy-start | bytes 304132
  13.7 5.3 %copy-start.3 = (bf16[384,144]{1,0:T(8,128)(2,1)S(1)}, bf16[384,144]{1,0:T(8,128)(2,1)}, u32[]{:S(2)}) copy-start(bf16[384,144]{1,0:T(8,128)(2,1)} %constant.13.clone.refs_9_) | copy-start | bytes 331780
  15.5 7.5 %collective-permute-start.6 = (bf16[2,144,256]{2,1,0:T(8,128)(2,1)S(1)}, bf16[2,144,256]{2,1,0:T(8,128)(2,1)S(1)}, u32[]{:S(2)}, u32[]{:S(2)}) collective-permute-start(bf16[2,144,256]{2,1,0:T(8,128)(2,1)S(1)} %get-tuple-element.59), channel_id=1, source_target_pairs={{0,1},{1,0},{2,3},{3,2},{4,5},{5,4},{6,7},{7,6},{8,9},{9,8},{10,11... | collective-permute-start | bytes 442376 | tf_op jit(solution)/shard_map/ppermute | solution.py:451
  17.1 10.0 %collective-permute-start.7 = (bf16[2,144,256]{2,1,0:T(8,128)(2,1)S(1)}, bf16[2,144,256]{2,1,0:T(8,128)(2,1)S(1)}, u32[]{:S(2)}, u32[]{:S(2)}) collective-permute-start(bf16[2,144,256]{2,1,0:T(8,128)(2,1)S(1)} %get-tuple-element.60), channel_id=1, source_target_pairs={{0,2},{1,3},{2,0},{3,1},{4,6},{5,7},{6,4},{7,5},{8,10},{9,11},{10,... | collective-permute-start | bytes 442376 | tf_op jit(solution)/shard_map/ppermute | solution.py:451
  17.6 9.5 %collective-permute-start.8 = (bf16[2,144,256]{2,1,0:T(8,128)(2,1)S(1)}, bf16[2,144,256]{2,1,0:T(8,128)(2,1)S(1)}, u32[]{:S(2)}, u32[]{:S(2)}) collective-permute-start(bf16[2,144,256]{2,1,0:T(8,128)(2,1)S(1)} %get-tuple-element.61), channel_id=1, source_target_pairs={{0,3},{1,2},{2,1},{3,0},{4,7},{5,6},{6,5},{7,4},{8,11},{9,10},{10,... | collective-permute-start | bytes 442376 | tf_op jit(solution)/shard_map/ppermute | solution.py:451
  19.1 1.6 %copy-start.4 = (bf16[288,144]{1,0:T(8,128)(2,1)S(1)}, bf16[288,144]{1,0:T(8,128)(2,1)}, u32[]{:S(2)}) copy-start(bf16[288,144]{1,0:T(8,128)(2,1)} %constant.14.clone.refs_9_) | copy-start | bytes 248836
  22.4 7.4 %collective-permute-start.4 = (bf16[144,384]{1,0:T(8,128)(2,1)S(1)}, bf16[144,384]{1,0:T(8,128)(2,1)S(1)}, u32[]{:S(2)}, u32[]{:S(2)}) collective-permute-start(bf16[144,384]{1,0:T(8,128)(2,1)S(1)} %get-tuple-element.55), channel_id=1, source_target_pairs={{0,4},{1,5},{2,6},{3,7},{4,8},{5,9},{6,10},{7,11},{8,12},{9,13},{1... | collective-permute-start | bytes 331784 | tf_op jit(solution)/shard_map/ppermute | solution.py:391
  22.5 7.3 %collective-permute-start.3 = (bf16[2,48,192]{2,1,0:T(8,128)(2,1)S(1)}, bf16[2,48,192]{2,1,0:T(8,128)(2,1)S(1)}, u32[]{:S(2)}, u32[]{:S(2)}) collective-permute-start(bf16[2,48,192]{2,1,0:T(8,128)(2,1)S(1)} %get-tuple-element.45), channel_id=1, source_target_pairs={{0,5},{1,6},{2,7},{3,4},{4,9},{5,10},{6,11},{7,8},{8,13},{9,14},{1... | collective-permute-start | bytes 110600 | tf_op jit(solution)/shard_map/ppermute | solution.py:391
  23.1 6.8 %collective-permute-start.5 = (bf16[2,48,192]{2,1,0:T(8,128)(2,1)S(1)}, bf16[2,48,192]{2,1,0:T(8,128)(2,1)S(1)}, u32[]{:S(2)}, u32[]{:S(2)}) collective-permute-start(bf16[2,48,192]{2,1,0:T(8,128)(2,1)S(1)} %get-tuple-element.56), channel_id=1, source_target_pairs={{0,1},{1,2},{2,3},{3,0},{4,5},{5,6},{6,7},{7,4},{8,9},{9,10},{10,1... | collective-permute-start | bytes 110600 | tf_op jit(solution)/shard_map/ppermute | solution.py:391
where the time goes:
time: 30.8 us; the launch traced here: 30.6 us
  starting transfers between devices  12.6 us (41%)
  Pallas kernels  9.29 us (30%)
  waiting for transfers between devices  4.75 us (15%)
  local copies, waits for them, and re-layouts  2.03 us (7%)
  other arithmetic  1.21 us (4%)
  between operations  0.75 us (2%)
    pallas_call x8, Pallas kernels, call(): pl.pallas_call(kernel, out_shape=outs, in_specs=vmem(len(args)), out_spec...  9.29 us
    ppermute x6, starting transfers between devices, shift(): return lax.ppermute(value, ('lat', 'lon'), pairs)  9.03 us
    ppermute x3, starting transfers between devices, local(): arrived.append(lax.ppermute(total[d], 'lon', pairs))  3.55 us
    ppermute x3, waiting for transfers between devices, local(): arrived.append(lax.ppermute(total[d], 'lon', pairs))  2.97 us
    unnamed x18, local copies, waits for them, and re-layouts  2.03 us
    ppermute x6, waiting for transfers between devices, shift(): return lax.ppermute(value, ('lat', 'lon'), pairs)  1.77 us
    concatenate x1, other arithmetic, local(): both = jnp.concatenate([tokens, cotangent], axis=-1)  1.21 us
  transfers between devices with their start and end apart: 9, of which 2 were waited for; matrix products, arithmetic and copies ran while one was open for 0% of the time, Pallas kernels for 21%

commit v1 on v0

--- a/solution.py
+++ b/solution.py
@@ -138,7 +138,7 @@
             spare = chunks.width - chunks.heads * size
             if spare:
                 rows.append(jnp.zeros((spare, WT), F32))
-            turned = jnp.transpose(jnp.concatenate(rows, axis=0)) * LOG2E
+            turned = jnp.transpose(jnp.concatenate(rows, axis=0))
             allowed = key_labels == labels(chunks.columns(j), window)
             slot = me ^ j if parts & (parts - 1) == 0 else lax.rem(j - me + parts, parts)
             bias_t[window, slot] = jnp.where(allowed, turned, -1e30)
@@ -416,7 +416,7 @@
     (bias_t,) = call(
         functools.partial(prep_kernel, chunks, lat_count),
         [struct((level_windows, lon_count, WT, chunks.width), F32)],
-        (bias,),
+        (bias * LOG2E,),
     )
     per_window = []
     total = []

time: 30.8 us -> 31.6 us (1.026)
  local copies, waits for them, and re-layouts: 2.03 us -> 0.05 us
  other arithmetic: 1.21 us -> 2.84 us
  waiting for transfers between devices: 4.75 us -> 5.4 us
  starting transfers between devices: 12.6 us -> 13 us
    ppermute x6, waiting for transfers between devices: 1.77 us -> 4.56 us  [shift(): return lax.ppermute(value, ('lat', 'lon'), pairs)]
    ppermute x3, waiting for transfers between devices: 2.97 us -> 0.84 us  [local(): arrived.append(lax.ppermute(total[d], 'lon', pairs))]
    unnamed x18 -> x16, local copies, waits for them, and re-layouts: 2.03 us -> 0.05 us
    mul x0 -> x1, other arithmetic: none -> 1.63 us  [local(): bias * LOG2E]
    ppermute x6, starting transfers between devices: 9.03 us -> 9.46 us  [shift(): return lax.ppermute(value, ('lat', 'lon'), pairs)]
  transfers between devices with their start and end apart: 9 -> 9, of which waited for: 2 -> 3; matrix products, arithmetic and copies ran while one was open for 0% -> 5% of each run, Pallas kernels for 21% -> 21%
where the time goes in v1:
time: 31.6 us; the launch traced here: 31.4 us
  starting transfers between devices  13 us (41%)
  Pallas kernels  9.3 us (29%)
  waiting for transfers between devices  5.4 us (17%)
  other arithmetic  2.84 us (9%)
  between operations  0.82 us (3%)
    ppermute x6, starting transfers between devices, shift(): return lax.ppermute(value, ('lat', 'lon'), pairs)  9.46 us
    pallas_call x8, Pallas kernels, call(): pl.pallas_call(kernel, out_shape=outs, in_specs=vmem(len(args)), out_spec...  9.3 us
    ppermute x6, waiting for transfers between devices, shift(): return lax.ppermute(value, ('lat', 'lon'), pairs)  4.56 us
    ppermute x3, starting transfers between devices, local(): arrived.append(lax.ppermute(total[d], 'lon', pairs))  3.55 us
    mul x1, other arithmetic, local(): bias * LOG2E  1.63 us
    concatenate x1, other arithmetic, local(): both = jnp.concatenate([tokens, cotangent], axis=-1)  1.21 us
    ppermute x3, waiting for transfers between devices, local(): arrived.append(lax.ppermute(total[d], 'lon', pairs))  0.84 us
  transfers between devices with their start and end apart: 9, of which 3 were waited for; matrix products, arithmetic and copies ran while one was open for 5% of the time, Pallas kernels for 21%

profile of v1, /device:TPU:0, one launch (start us, length us, event | category | flops | bytes accessed | tf_op | source)
XLA Modules:
  0.0 31.4 jit_solution(2564705938067810656)
XLA Ops:
  0.6 1.2 %pad_maximum_fusion.both = bf16[4,6,24,384]{3,2,1,0:T(8,128)(2,1)S(1)} fusion(bf16[4,6,24,192]{3,2,1,0:T(8,128)(2,1)} %param.12, bf16[4,6,24,192]{3,2,1,0:T(8,128)(2,1)} %param.11), kind=kLoop, calls=%fused_computation.2 | loop fusion | flops 884736 | bytes 884736 | tf_op jit(solution)/shard_map/concatenate | solution.py:406
  1.8 0.2 shard_map.122
  2.1 3.9 %collective-permute-start.1 = (bf16[2,48,384]{2,1,0:T(8,128)(2,1)S(1)}, bf16[2,48,384]{2,1,0:T(8,128)(2,1)S(1)}, u32[]{:S(2)}, u32[]{:S(2)}) collective-permute-start(bf16[2,48,384]{2,1,0:T(8,128)(2,1)S(1)} %get-tuple-element.35), channel_id=1, source_target_pairs={{0,3},{1,0},{2,1},{3,2},{4,7},{5,4},{6,5},{7,6},{8,11},{9,8},{10,9... | collective-permute-start | bytes 221192 | tf_op jit(solution)/shard_map/ppermute | solution.py:391
  6.0 2.7 %collective-permute-start.2 = (bf16[2,48,384]{2,1,0:T(8,128)(2,1)S(1)}, bf16[2,48,384]{2,1,0:T(8,128)(2,1)S(1)}, u32[]{:S(2)}, u32[]{:S(2)}) collective-permute-start(bf16[2,48,384]{2,1,0:T(8,128)(2,1)S(1)} %get-tuple-element.36), channel_id=1, source_target_pairs={{0,31},{1,28},{2,29},{3,30},{4,3},{5,0},{6,1},{7,2},{8,7},{9,4},{1... | collective-permute-start | bytes 221192 | tf_op jit(solution)/shard_map/ppermute | solution.py:391
  8.7 1.1 %collective-permute-start = (bf16[2,112,384]{2,1,0:T(8,128)(2,1)S(1)}, bf16[2,112,384]{2,1,0:T(8,128)(2,1)S(1)}, u32[]{:S(2)}, u32[]{:S(2)}) collective-permute-start(bf16[2,112,384]{2,1,0:T(8,128)(2,1)S(1)} %get-tuple-element.34), channel_id=1, source_target_pairs={{0,28},{1,29},{2,30},{3,31},{4,0},{5,1},{6,2},{7,3},{8,4},{9,5},{1... | collective-permute-start | bytes 516104 | tf_op jit(solution)/shard_map/ppermute | solution.py:391
  9.9 1.6 %fusion.bias = f32[2,6,144,144]{3,2,1,0:T(8,128)S(1)} fusion(f32[2,1,6,144,144]{4,3,2,1,0:T(8,128)} %param.16), kind=kLoop, calls=%fused_computation.1 | loop fusion | flops 248832 | bytes 1990656 | tf_op jit(solution)/shard_map/mul | solution.py:419
  11.5 0.0 copy-start
  11.5 0.0 copy-start.1
  11.5 0.0 copy-start.4
  11.5 0.0 copy-start.5
  11.6 0.0 copy-start.7
  11.6 0.6 %shard_map.123.refs_5_.refs_7_ = f32[2,4,144,256]{3,2,1,0:T(8,128)S(1)} custom-call(f32[2,6,144,144]{3,2,1,0:T(8,128)S(1)} %fusion.bias), custom_call_target="tpu_custom_call" | custom-call | tf_op jit(solution)/shard_map/pallas_call | solution.py:374
  12.1 0.6 %collective-permute-done.refs_1_ = bf16[2,112,384]{2,1,0:T(8,128)(2,1)S(1)} collective-permute-done((bf16[2,112,384]{2,1,0:T(8,128)(2,1)S(1)}, bf16[2,112,384]{2,1,0:T(8,128)(2,1)S(1)}, u32[]{:S(2)}, u32[]{:S(2)}) %collective-permute-start) | collective-permute-done | bytes 172064 | tf_op jit(solution)/shard_map/ppermute | solution.py:391
  12.8 0.0 copy-done
  12.8 0.0 copy-done.1
  12.8 0.0 copy-done.4
  12.8 0.0 copy-done.5
  12.8 0.0 copy-done.7
  12.8 0.0 copy-start.6
  12.8 1.7 %shard_map.124 = (f32[288,192]{1,0:T(8,128)S(1)}, f32[288,128]{1,0:T(8,128)S(1)}, bf16[288,192]{1,0:T(8,128)(2,1)S(1)}, bf16[2,256,192]{2,1,0:T(8,128)(2,1)S(1)}...) custom-call(bf16[2,144,384]{2,1,0:T(8,128)(2,1)S(1)} %get-tuple-elem, ...), custom_call_target="tpu_custom_call" | custom-call | flops 1000000000 | tf_op jit(solution)/shard_map/pallas_call | solution.py:374
  14.5 0.0 collective-permute-done.1.refs_2_
  14.5 0.0 collective-permute-done.2.refs_3_
  14.5 0.0 copy-done.6
  14.5 0.0 copy-start.2
  14.5 1.8 %shard_map.125 = (f32[288,192]{1,0:T(8,128)S(1)}, f32[288,128]{1,0:T(8,128)S(1)}, bf16[288,192]{1,0:T(8,128)(2,1)S(1)}, bf16[2,256,192]{2,1,0:T(8,128)(2,1)S(1)}...) custom-call(bf16[2,144,384]{2,1,0:T(8,128)(2,1)S(1)} %get-tuple-elem, ...), custom_call_target="tpu_custom_call" | custom-call | flops 1000000000 | tf_op jit(solution)/shard_map/pallas_call | solution.py:374
  16.3 0.0 copy-start.3
  16.3 1.6 %collective-permute-start.6 = (bf16[2,144,256]{2,1,0:T(8,128)(2,1)S(1)}, bf16[2,144,256]{2,1,0:T(8,128)(2,1)S(1)}, u32[]{:S(2)}, u32[]{:S(2)}) collective-permute-start(bf16[2,144,256]{2,1,0:T(8,128)(2,1)S(1)} %get-tuple-element.59), channel_id=1, source_target_pairs={{0,1},{1,0},{2,3},{3,2},{4,5},{5,4},{6,7},{7,6},{8,9},{9,8},{10,11... | collective-permute-start | bytes 442376 | tf_op jit(solution)/shard_map/ppermute | solution.py:451
  17.9 0.5 %collective-permute-start.7 = (bf16[2,144,256]{2,1,0:T(8,128)(2,1)S(1)}, bf16[2,144,256]{2,1,0:T(8,128)(2,1)S(1)}, u32[]{:S(2)}, u32[]{:S(2)}) collective-permute-start(bf16[2,144,256]{2,1,0:T(8,128)(2,1)S(1)} %get-tuple-element.60), channel_id=1, source_target_pairs={{0,2},{1,3},{2,0},{3,1},{4,6},{5,7},{6,4},{7,5},{8,10},{9,11},{10,... | collective-permute-start | bytes 442376 | tf_op jit(solution)/shard_map/ppermute | solution.py:451
  18.4 1.5 %collective-permute-start.8 = (bf16[2,144,256]{2,1,0:T(8,128)(2,1)S(1)}, bf16[2,144,256]{2,1,0:T(8,128)(2,1)S(1)}, u32[]{:S(2)}, u32[]{:S(2)}) collective-permute-start(bf16[2,144,256]{2,1,0:T(8,128)(2,1)S(1)} %get-tuple-element.61), channel_id=1, source_target_pairs={{0,3},{1,2},{2,1},{3,0},{4,7},{5,6},{6,5},{7,4},{8,11},{9,10},{10,... | collective-permute-start | bytes 442376 | tf_op jit(solution)/shard_map/ppermute | solution.py:451
  19.9 0.0 copy-done.2
  19.9 1.6 %shard_map.126 = (bf16[2,144,192]{2,1,0:T(8,128)(2,1)S(1)}, bf16[2,144,192]{2,1,0:T(8,128)(2,1)S(1)}, bf16[2,48,192]{2,1,0:T(8,128)(2,1)S(1)}, bf16[2,48,192]{2,1,0:T(8,128)(2,1)S(1)}) custom-call(f32[288,192]{1,0:T(8,128)S(1)} %get-tuple-element.38.refs_0_, f32[288,128]{1,0:T(8,128)S(1)} %get-tuple-element.39.refs_1_, ...), custom_call_target="tpu_custom_call" | custom-call | tf_op jit(solution)/shard_map/pallas_call | solution.py:374
  21.5 0.0 copy-done.3
  21.5 1.7 %shard_map.127 = (bf16[2,144,192]{2,1,0:T(8,128)(2,1)S(1)}, bf16[144,384]{1,0:T(8,128)(2,1)S(1)}) custom-call(f32[288,192]{1,0:T(8,128)S(1)} %get-tuple-element.46.refs_0_, f32[288,128]{1,0:T(8,128)S(1)} %get-tuple-element.47.refs_1_, bf16[288,192]{1,0:T(8,128)(2,1)S(1)} %get-tuple-element.48.refs_2_, bf16[2,256,192]{2,1,0:T(8,128)(2,1)S(1)} %get-tuple-element.49.refs_3_, ...), custom_call_target="tpu_custom_call" | custom-call | tf_op jit(solution)/shard_map/pallas_call | solution.py:374
  23.2 0.1 collective-permute-start.4
  23.3 0.1 collective-permute-start.3
  23.3 0.0 collective-permute-done.6.refs_1_
  23.3 1.5 %collective-permute-start.5 = (bf16[2,48,192]{2,1,0:T(8,128)(2,1)S(1)}, bf16[2,48,192]{2,1,0:T(8,128)(2,1)S(1)}, u32[]{:S(2)}, u32[]{:S(2)}) collective-permute-start(bf16[2,48,192]{2,1,0:T(8,128)(2,1)S(1)} %get-tuple-element.56), channel_id=1, source_target_pairs={{0,1},{1,2},{2,3},{3,0},{4,5},{5,6},{6,7},{7,4},{8,9},{9,10},{10,1... | collective-permute-start | bytes 110600 | tf_op jit(solution)/shard_map/ppermute | solution.py:391
  24.9 0.8 %collective-permute-done.7.refs_2_ = bf16[2,144,256]{2,1,0:T(8,128)(2,1)S(1)} collective-permute-done((bf16[2,144,256]{2,1,0:T(8,128)(2,1)S(1)}, bf16[2,144,256]{2,1,0:T(8,128)(2,1)S(1)}, u32[]{:S(2)}, u32[]{:S(2)}) %collective-permute-start.7) | collective-permute-done | bytes 147488 | tf_op jit(solution)/shard_map/ppermute | solution.py:451
  25.7 0.0 collective-permute-done.8.refs_3_
  25.7 1.0 %shard_map.128 = (f32[432,1,144]{2,1,0:T(1,128)}, f32[8,128]{1,0:T(8,128)S(1)}) custom-call(bf16[2,144,256]{2,1,0:T(8,128)(2,1)S(1)} %get-tuple-element.58.refs_0_, bf16[2,144,256]{2,1,0:T(8,128)(2,1)S(1)} %collective-permute-done.6.refs_1_, bf16[2,144,256]{2,1,0:T(8,128)(2,1)S(1)} %collective-permute-done.7.refs_2_, ...), custom_call_target="tpu_custom_call" | custom-call | tf_op jit(solution)/shard_map/pallas_call | solution.py:374
  26.7 3.9 %collective-permute-done.3.corner = bf16[2,48,192]{2,1,0:T(8,128)(2,1)S(1)} collective-permute-done((bf16[2,48,192]{2,1,0:T(8,128)(2,1)S(1)}, bf16[2,48,192]{2,1,0:T(8,128)(2,1)S(1)}, u32[]{:S(2)}, u32[]{:S(2)}) %collective-permute-start.3) | collective-permute-done | bytes 36896 | tf_op jit(solution)/shard_map/ppermute | solution.py:391
  30.6 0.0 collective-permute-done.5.right
  30.6 0.0 collective-permute-done.4.below
  30.6 0.8 %shard_map.129 = bf16[4,6,24,192]{3,2,1,0:T(8,128)(2,1)} custom-call(bf16[2,48,192]{2,1,0:T(8,128)(2,1)S(1)} %collective-permute-done.3.corner, bf16[144,384]{1,0:T(8,128)(2,1)S(1)} %collective-permute-done.4.below, bf16[2,48,192]{2,1,0:T(8,128)(2,1)S(1)} %collective-permute-done.5.right, bf16[2,144,192]{2,1,0:T(8,128)(2,1)S(1)} %get-tuple-element.57.inner, ...), custom_call_target="tpu_custom_call" | custom-call | tf_op jit(solution)/shard_map/pallas_call | solution.py:374
Async XLA Ops:
  2.1 12.4 %collective-permute-start.1 = (bf16[2,48,384]{2,1,0:T(8,128)(2,1)S(1)}, bf16[2,48,384]{2,1,0:T(8,128)(2,1)S(1)}, u32[]{:S(2)}, u32[]{:S(2)}) collective-permute-start(bf16[2,48,384]{2,1,0:T(8,128)(2,1)S(1)} %get-tuple-element.35), channel_id=1, source_target_pairs={{0,3},{1,0},{2,1},{3,2},{4,7},{5,4},{6,5},{7,6},{8,11},{9,8},{10,9... | collective-permute-start | bytes 221192 | tf_op jit(solution)/shard_map/ppermute | solution.py:391
  6.0 8.5 %collective-permute-start.2 = (bf16[2,48,384]{2,1,0:T(8,128)(2,1)S(1)}, bf16[2,48,384]{2,1,0:T(8,128)(2,1)S(1)}, u32[]{:S(2)}, u32[]{:S(2)}) collective-permute-start(bf16[2,48,384]{2,1,0:T(8,128)(2,1)S(1)} %get-tuple-element.36), channel_id=1, source_target_pairs={{0,31},{1,28},{2,29},{3,30},{4,3},{5,0},{6,1},{7,2},{8,7},{9,4},{1... | collective-permute-start | bytes 221192 | tf_op jit(solution)/shard_map/ppermute | solution.py:391
  8.7 4.0 %collective-permute-start = (bf16[2,112,384]{2,1,0:T(8,128)(2,1)S(1)}, bf16[2,112,384]{2,1,0:T(8,128)(2,1)S(1)}, u32[]{:S(2)}, u32[]{:S(2)}) collective-permute-start(bf16[2,112,384]{2,1,0:T(8,128)(2,1)S(1)} %get-tuple-element.34), channel_id=1, source_target_pairs={{0,28},{1,29},{2,30},{3,31},{4,0},{5,1},{6,2},{7,3},{8,4},{9,5},{1... | collective-permute-start | bytes 516104 | tf_op jit(solution)/shard_map/ppermute | solution.py:391
  11.5 1.3 %copy-start = (bf16[192,576]{1,0:T(8,128)(2,1)S(1)}, bf16[192,576]{1,0:T(8,128)(2,1)}, u32[]{:S(2)}) copy-start(bf16[192,576]{1,0:T(8,128)(2,1)} %refs_8_.4) | copy-start | bytes 663556
  11.5 1.3 %copy-start.1 = (bf16[4,64,144]{2,1,0:T(8,128)(2,1)S(1)}, bf16[4,64,144]{2,1,0:T(8,128)(2,1)}, u32[]{:S(2)}) copy-start(bf16[4,64,144]{2,1,0:T(8,128)(2,1)} %constant.12.clone.refs_7_.refs_9_.refs_10_) | copy-start | bytes 221188
  11.5 1.3 %copy-start.4 = (f32[192]{0:T(256)S(1)}, f32[192]{0:T(256)}, u32[]{:S(2)}) copy-start(f32[192]{0:T(256)} %param.13) | copy-start | bytes 2308
  11.5 1.3 %copy-start.5 = (bf16[192,192]{1,0:T(8,128)(2,1)S(1)}, bf16[192,192]{1,0:T(8,128)(2,1)}, u32[]{:S(2)}) copy-start(bf16[192,192]{1,0:T(8,128)(2,1)} %refs_6_.2) | copy-start | bytes 221188
  11.6 1.3 %copy-start.7 = (bf16[144,256]{1,0:T(8,128)(2,1)S(1)}, bf16[144,256]{1,0:T(8,128)(2,1)}, u32[]{:S(2)}) copy-start(bf16[144,256]{1,0:T(8,128)(2,1)} %constant.13.clone.refs_6_) | copy-start | bytes 221188
  12.8 1.7 %copy-start.6 = (bf16[144,352]{1,0:T(8,128)(2,1)S(1)}, bf16[144,352]{1,0:T(8,128)(2,1)}, u32[]{:S(2)}) copy-start(bf16[144,352]{1,0:T(8,128)(2,1)} %constant.14.clone.refs_8_) | copy-start | bytes 304132
  14.5 5.4 %copy-start.2 = (bf16[384,144]{1,0:T(8,128)(2,1)S(1)}, bf16[384,144]{1,0:T(8,128)(2,1)}, u32[]{:S(2)}) copy-start(bf16[384,144]{1,0:T(8,128)(2,1)} %constant.15.clone.refs_9_) | copy-start | bytes 331780
  16.3 5.2 %copy-start.3 = (bf16[288,144]{1,0:T(8,128)(2,1)S(1)}, bf16[288,144]{1,0:T(8,128)(2,1)}, u32[]{:S(2)}) copy-start(bf16[288,144]{1,0:T(8,128)(2,1)} %constant.16.clone.refs_9_) | copy-start | bytes 248836
  16.3 7.0 %collective-permute-start.6 = (bf16[2,144,256]{2,1,0:T(8,128)(2,1)S(1)}, bf16[2,144,256]{2,1,0:T(8,128)(2,1)S(1)}, u32[]{:S(2)}, u32[]{:S(2)}) collective-permute-start(bf16[2,144,256]{2,1,0:T(8,128)(2,1)S(1)} %get-tuple-element.59), channel_id=1, source_target_pairs={{0,1},{1,0},{2,3},{3,2},{4,5},{5,4},{6,7},{7,6},{8,9},{9,8},{10,11... | collective-permute-start | bytes 442376 | tf_op jit(solution)/shard_map/ppermute | solution.py:451
  17.9 7.8 %collective-permute-start.7 = (bf16[2,144,256]{2,1,0:T(8,128)(2,1)S(1)}, bf16[2,144,256]{2,1,0:T(8,128)(2,1)S(1)}, u32[]{:S(2)}, u32[]{:S(2)}) collective-permute-start(bf16[2,144,256]{2,1,0:T(8,128)(2,1)S(1)} %get-tuple-element.60), channel_id=1, source_target_pairs={{0,2},{1,3},{2,0},{3,1},{4,6},{5,7},{6,4},{7,5},{8,10},{9,11},{10,... | collective-permute-start | bytes 442376 | tf_op jit(solution)/shard_map/ppermute | solution.py:451
  18.4 7.3 %collective-permute-start.8 = (bf16[2,144,256]{2,1,0:T(8,128)(2,1)S(1)}, bf16[2,144,256]{2,1,0:T(8,128)(2,1)S(1)}, u32[]{:S(2)}, u32[]{:S(2)}) collective-permute-start(bf16[2,144,256]{2,1,0:T(8,128)(2,1)S(1)} %get-tuple-element.61), channel_id=1, source_target_pairs={{0,3},{1,2},{2,1},{3,0},{4,7},{5,6},{6,5},{7,4},{8,11},{9,10},{10,... | collective-permute-start | bytes 442376 | tf_op jit(solution)/shard_map/ppermute | solution.py:451
  23.2 7.4 %collective-permute-start.4 = (bf16[144,384]{1,0:T(8,128)(2,1)S(1)}, bf16[144,384]{1,0:T(8,128)(2,1)S(1)}, u32[]{:S(2)}, u32[]{:S(2)}) collective-permute-start(bf16[144,384]{1,0:T(8,128)(2,1)S(1)} %get-tuple-element.55), channel_id=1, source_target_pairs={{0,4},{1,5},{2,6},{3,7},{4,8},{5,9},{6,10},{7,11},{8,12},{9,13},{1... | collective-permute-start | bytes 331784 | tf_op jit(solution)/shard_map/ppermute | solution.py:391
  23.3 7.3 %collective-permute-start.3 = (bf16[2,48,192]{2,1,0:T(8,128)(2,1)S(1)}, bf16[2,48,192]{2,1,0:T(8,128)(2,1)S(1)}, u32[]{:S(2)}, u32[]{:S(2)}) collective-permute-start(bf16[2,48,192]{2,1,0:T(8,128)(2,1)S(1)} %get-tuple-element.45), channel_id=1, source_target_pairs={{0,5},{1,6},{2,7},{3,4},{4,9},{5,10},{6,11},{7,8},{8,13},{9,14},{1... | collective-permute-start | bytes 110600 | tf_op jit(solution)/shard_map/ppermute | solution.py:391
  23.3 7.3 %collective-permute-start.5 = (bf16[2,48,192]{2,1,0:T(8,128)(2,1)S(1)}, bf16[2,48,192]{2,1,0:T(8,128)(2,1)S(1)}, u32[]{:S(2)}, u32[]{:S(2)}) collective-permute-start(bf16[2,48,192]{2,1,0:T(8,128)(2,1)S(1)} %get-tuple-element.56), channel_id=1, source_target_pairs={{0,1},{1,2},{2,3},{3,0},{4,5},{5,6},{6,7},{7,4},{8,9},{9,10},{10,1... | collective-permute-start | bytes 110600 | tf_op jit(solution)/shard_map/ppermute | solution.py:391

commit v2 on v0

--- a/solution.py
+++ b/solution.py
@@ -47,16 +47,6 @@
         self.used = heads * self.main + self.rest_rows
         self.width = round_up(self.used, LANES)
 
-    def queries(self):
-        table = np.zeros((self.parts, self.rows, WT), np.float32)
-        for j in range(self.parts):
-            for i in range(self.main):
-                table[j, i, j * self.size + i] = 1.0
-            for h in range(self.heads):
-                for i in range(self.rest):
-                    table[j, self.main + h * self.rest + i, j * self.size + self.main + i] = 1.0
-        return table
-
     def columns(self, j):
         lane = lax.broadcasted_iota(jnp.int32, (1, self.width), 1)
         low = self.heads * self.main
@@ -71,7 +61,9 @@
     last = c == cols // WW - 1
     part, side = HALF_ROWS * cols, HALF_ROWS * SIDE
     kept = cols - HALF_COLS if narrow else cols
-    near = WZ * part + round_up(WZ * HALF_ROWS * kept, 16)
+    tail = narrow and last
+    inner = WZ * (side if tail else part)
+    near = inner + round_up(WZ * HALF_ROWS * kept, 16)
     table = np.zeros((WT, near + last * 2 * WZ * side), np.float32)
     for z in range(WZ):
         for r in range(WH):
@@ -81,7 +73,9 @@
                 if col >= cols:
                     at = near + (low * WZ + z) * side + row * SIDE + col - cols
                 elif low:
-                    at = WZ * part + (z * HALF_ROWS + row) * kept + col - (cols - kept)
+                    at = inner + (z * HALF_ROWS + row) * kept + col - (cols - kept)
+                elif tail:
+                    at = z * side + row * SIDE + col - (cols - SIDE)
                 else:
                     at = z * part + row * cols + col
                 table[(z * WH + r) * WW + w, at] = 1.0
@@ -94,7 +88,7 @@
     return [field[level, base + row].astype(F32) for level in at for row in range(HALF_ROWS)]
 
 
-def send_kernel(both, inner, below, right, corner):
+def send_kernel(both, inner, below, right, corner, tail):
     cols = both.shape[2]
     kept = cols - HALF_COLS
     shape = (below.shape[1], WZ * HALF_ROWS * cols)
@@ -109,13 +103,13 @@
         below[a] = dot(narrow, jnp.concatenate(low, axis=0).astype(BF16)).astype(BF16)
         inner[a] = jnp.concatenate(high, axis=0).astype(BF16)
         right[a] = jnp.concatenate([row[:SIDE] for row in high], axis=0).astype(BF16)
+        tail[a] = jnp.concatenate([row[cols - SIDE :] for row in high], axis=0).astype(BF16)
         corner[a] = jnp.concatenate([row[:SIDE] for row in low], axis=0).astype(BF16)
 
 
 def prep_kernel(chunks, lat_count, bias, bias_t):
     level_windows = bias.shape[0]
     last_lat = lax.axis_index("lat") == lat_count - 1
-    me = lax.axis_index("lon")
     parts, size, main = chunks.parts, chunks.size, chunks.main
 
     def labels(index, window):
@@ -140,8 +134,7 @@
                 rows.append(jnp.zeros((spare, WT), F32))
             turned = jnp.transpose(jnp.concatenate(rows, axis=0)) * LOG2E
             allowed = key_labels == labels(chunks.columns(j), window)
-            slot = me ^ j if parts & (parts - 1) == 0 else lax.rem(j - me + parts, parts)
-            bias_t[window, slot] = jnp.where(allowed, turned, -1e30)
+            bias_t[window, j] = jnp.where(allowed, turned, -1e30)
 
 
 def head_masks(chunks, channels):
@@ -159,14 +152,20 @@
     return lanes, rest
 
 
-def stack_heads(chunks, value, d, lane_masks, rest_mask):
-    low = d * chunks.rows
-    main = value[low : low + chunks.main]
-    pieces = [main * mask for mask in lane_masks] if chunks.main else []
+def stack_heads(chunks, value, j, lane_masks, rest_mask):
+    low = j * chunks.size
+    pieces = []
+    if chunks.main:
+        main = value[low : low + chunks.main].astype(BF16)
+        pieces += [main * mask for mask in lane_masks]
     if chunks.rest:
-        pieces.append(value[low + chunks.main : low + chunks.rows] * rest_mask)
+        rows = [value[low + chunks.main : low + chunks.size]] * chunks.heads
+        spare = chunks.rest_rows - chunks.heads * chunks.rest
+        if spare:
+            rows.append(jnp.zeros((spare, value.shape[1]), F32))
+        pieces.append(jnp.concatenate(rows, axis=0).astype(BF16) * rest_mask)
     if chunks.width > chunks.used:
-        pieces.append(jnp.zeros((chunks.width - chunks.used, value.shape[1]), value.dtype))
+        pieces.append(jnp.zeros((chunks.width - chunks.used, value.shape[1]), BF16))
     return jnp.concatenate(pieces, axis=0)
 
 
@@ -179,26 +178,21 @@
     return me ^ d if parts & (parts - 1) == 0 else (me + d) % parts
 
 
-def rolled(ref, parts):
-    me = lax.axis_index("lon")
-    return jnp.concatenate([ref[partner(me, d, parts)] for d in range(parts)], axis=0)
-
-
 def scores_kernel(chunks, near, first, last, *refs):
     pieces, refs = refs[:near], refs[near:]
-    gain_ref, inproj, outproj, bias_t, perm, queries, *refs = refs
+    gain_ref, inproj, outproj, bias_t, perm, *refs = refs
     weights = split(inproj)
     before = None
     if not first:
         before, *refs = refs
-    standard_out, scale_out, keys_out, query_out, up_out, p_out, ds_out, *totals = refs
+    standard_out, scale_out, keys_out, query_out, up_out, p_out, ds_out, *totals, turn = refs
     parts, width = chunks.parts, chunks.width
     channels = outproj.shape[0]
     scaling = (channels // chunks.heads) ** (-0.5)
     lanes, rest_mask = head_masks(chunks, channels)
     lanes = [mask.astype(F32).astype(BF16) for mask in lanes]
     rest_mask = rest_mask.astype(BF16) if chunks.rest else None
-    choose = rolled(queries, parts)
+    me = lax.axis_index("lon")
     level_windows = pieces[0].shape[0]
     tile = channels // LANES * LANES
     from_tile = jnp.concatenate([jnp.zeros((channels, channels - tile), BF16), outproj[...]], axis=1)
@@ -206,7 +200,7 @@
     for a in range(level_windows):
         moved = dot(perm[...], jnp.concatenate([piece[a] for piece in pieces], axis=0))
         ts.append(moved[:, :channels])
-        us.append(dot_nt(moved[:, tile:].astype(BF16), from_tile).astype(BF16))
+        us.append(dot_nt(moved[:, tile:].astype(BF16), from_tile))
     t = jnp.concatenate(ts, axis=0)
     centred = t - jnp.mean(t, axis=-1, keepdims=True)
     inverse_rms = lax.rsqrt(jnp.mean(centred * centred, axis=-1, keepdims=True) + epsilon)
@@ -214,16 +208,15 @@
     standard_out[...] = standard
     scale_out[...] = jnp.broadcast_to(inverse_rms, scale_out.shape)
     normed = (standard * gain_ref[...]).astype(BF16)
-    q = dot(normed, weights[0]).astype(BF16)
+    q = dot(normed, weights[0])
+    query_out[...] = q
     k = dot(normed, weights[1]).astype(BF16)
     v = dot(normed, weights[2]).astype(BF16)
     keys_out[...] = k
     for a in range(level_windows):
         cut = slice(a * WT, (a + 1) * WT)
-        query = dot(choose, q[cut]).astype(BF16)
-        up = dot(choose, us[a]).astype(BF16)
-        query_out[a] = query
-        up_out[a] = up
+        query, up = q[cut], us[a]
+        up_out[cut] = up
         for d in range(parts):
             at = slice(d * width, (d + 1) * width)
             s = dot_nt(k[cut], stack_heads(chunks, query, d, lanes, rest_mask))
@@ -236,13 +229,16 @@
             if not first:
                 ds += before[a, d]
             if last:
-                totals[d][a] = ds.astype(BF16)
+                turn[d] = ds.astype(BF16)
             else:
                 totals[0][a, d] = ds
+        if last:
+            for d in range(parts):
+                totals[d][a] = turn[partner(me, d, parts)]
 
 
 def tokens_kernel(chunks, near, first, *refs):
-    standard_in, scale_in, keys, queries_in, ups, p_in, ds_in, gain_ref, inproj, perm_t, queries, *refs = refs
+    standard_in, scale_in, keys, queries_in, ups, p_in, ds_in, gain_ref, inproj, perm_t, *refs = refs
     weights = split(inproj)
     before = None
     if not first:
@@ -255,11 +251,11 @@
     lanes, rest_mask = head_masks(chunks, channels)
     low_lanes = [mask.astype(F32).astype(BF16) for mask in lanes]
     low_rest = rest_mask.astype(BF16) if chunks.rest else None
-    choose_t = jnp.transpose(rolled(queries, parts).astype(F32)).astype(BF16)
     level_windows = p_in.shape[0]
     dqs, dks, dvs = [], [], []
     for a in range(level_windows):
-        query, up = queries_in[a], ups[a]
+        cut = slice(a * WT, (a + 1) * WT)
+        query, up = queries_in[cut], ups[cut]
         qs = jnp.concatenate(
             [stack_heads(chunks, query, d, low_lanes, low_rest) for d in range(parts)], axis=0
         )
@@ -296,9 +292,12 @@
             if chunks.main:
                 rows.append(jnp.concatenate([tiles[d] for tiles in main], axis=1))
             if chunks.rest:
-                rows.append(left[d * chunks.rest_rows : (d + 1) * chunks.rest_rows] * rest_mask)
-        picked = (jnp.concatenate(rows, axis=0) * scaling).astype(BF16)
-        dqs.append(dot(choose_t, picked).astype(BF16))
+                some = left[d * chunks.rest_rows : (d + 1) * chunks.rest_rows] * rest_mask
+                total = some[: chunks.rest]
+                for h in range(1, chunks.heads):
+                    total += some[h * chunks.rest : (h + 1) * chunks.rest]
+                rows.append(total)
+        dqs.append((jnp.concatenate(rows, axis=0) * scaling).astype(BF16))
     dq, dk, dv = (jnp.concatenate(parts_of, axis=0) for parts_of in (dqs, dks, dvs))
     scaled = (dot_nt(dq, weights[0]) + dot_nt(dk, weights[1]) + dot_nt(dv, weights[2])) * gain_ref[...]
     standard = standard_in[...]
@@ -370,12 +369,13 @@
     return [pl.BlockSpec(memory_space=pltpu.VMEM)] * count
 
 
-def call(kernel, outs, args, flops=0):
+def call(kernel, outs, args, flops=0, scratch=()):
     return pl.pallas_call(
         kernel,
         out_shape=outs,
         in_specs=vmem(len(args)),
         out_specs=vmem(len(outs)),
+        scratch_shapes=list(scratch),
         compiler_params=pltpu.CompilerParams(vmem_limit_bytes=40 * 2**20),
         cost_estimate=pl.CostEstimate(flops=flops, bytes_accessed=0, transcendentals=0),
     )(*args)
@@ -400,14 +400,13 @@
     struct = jax.ShapeDtypeStruct
     half, side = WZ * HALF_ROWS * cols, WZ * HALF_ROWS * SIDE
     gain = norm_gain.reshape(1, channels)
-    queries = jnp.asarray(chunks.queries(), BF16)
 
     bias = bias.reshape(level_windows, heads, WT, WT)
     both = jnp.concatenate([tokens, cotangent], axis=-1)
     narrow = round_up(WZ * HALF_ROWS * (cols - HALF_COLS), 16)
-    inner, below, right, corner = call(
+    inner, below, right, corner, tail = call(
         send_kernel,
-        [struct((level_windows, size, 2 * channels), BF16) for size in (half, narrow, side, side)],
+        [struct((level_windows, size, 2 * channels), BF16) for size in (half, narrow, side, side, side)],
         (both,),
     )
     below = shift(below, -1, 0)
@@ -422,7 +421,7 @@
     total = []
     for c in range(windows):
         last = c == windows - 1
-        pieces = (inner, below) + ((right, corner) if last else ())
+        pieces = (tail, below, right, corner) if last else (inner, below)
         if last:
             sums = [struct((level_windows, WT, chunks.width), BF16)] * lon_count
         else:
@@ -434,14 +433,15 @@
                 struct((level_windows * WT, channels), F32),
                 struct((level_windows * WT, LANES), F32),
                 struct((level_windows * WT, channels), BF16),
-                struct((level_windows, lon_count * chunks.rows, channels), BF16),
-                struct((level_windows, lon_count * chunks.rows, channels), BF16),
+                struct((level_windows * WT, channels), F32),
+                struct((level_windows * WT, channels), F32),
                 struct((level_windows, WT, lon_count * chunks.width), BF16),
                 struct((level_windows, WT, lon_count * chunks.width), BF16),
             ]
             + sums,
-            (*pieces, gain, inproj_weight, outproj_weight, bias_t, order, queries, *total),
+            (*pieces, gain, inproj_weight, outproj_weight, bias_t, order, *total),
             flops=10**9,
+            scratch=[pltpu.VMEM((lon_count, WT, chunks.width), BF16)],
         )
         per_window.append(results[:7])
         total = results[7:]
@@ -458,7 +458,7 @@
         results = call(
             functools.partial(tokens_kernel, chunks, 2, last),
             [wide, wide, thin, thin] if last else [wide, struct((half, level_windows * channels), BF16)],
-            (*per_window[c], gain, inproj_weight, order, queries, *grads),
+            (*per_window[c], gain, inproj_weight, order, *grads),
         )
         grads = results[:2]
         if last:

time: 30.8 us -> 29.9 us (0.971)
  Pallas kernels: 9.29 us -> 8.24 us
    pallas_call x8, Pallas kernels: 9.29 us -> 8.24 us  [call(): pl.pallas_call(kernel, out_shape=outs, in_specs=vmem(len(args)), out_spec...]
    ppermute x3, waiting for transfers between devices: 2.97 us -> 3.44 us  [local(): arrived.append(lax.ppermute(total[d], 'lon', pairs))]
    ppermute x6, waiting for transfers between devices: 1.77 us -> 1.33 us  [shift(): return lax.ppermute(value, ('lat', 'lon'), pairs)]
    unnamed x18 -> x16, local copies, waits for them, and re-layouts: 2.03 us -> 1.97 us
  transfers between devices with their start and end apart: 9 -> 9, of which waited for: 2 -> 2; matrix products, arithmetic and copies ran while one was open for 0% -> 0% of each run, Pallas kernels for 21% -> 19%
where the time goes in v2:
time: 29.9 us; the launch traced here: 29.7 us
  starting transfers between devices  12.8 us (43%)
  Pallas kernels  8.24 us (28%)
  waiting for transfers between devices  4.78 us (16%)
  local copies, waits for them, and re-layouts  1.97 us (7%)
  other arithmetic  1.21 us (4%)
  between operations  0.74 us (2%)
    ppermute x6, starting transfers between devices, shift(): return lax.ppermute(value, ('lat', 'lon'), pairs)  9.22 us
    pallas_call x8, Pallas kernels, call(): pl.pallas_call(kernel, out_shape=outs, in_specs=vmem(len(args)), out_spec...  8.24 us
    ppermute x3, starting transfers between devices, local(): arrived.append(lax.ppermute(total[d], 'lon', pairs))  3.55 us
    ppermute x3, waiting for transfers between devices, local(): arrived.append(lax.ppermute(total[d], 'lon', pairs))  3.44 us
    unnamed x16, local copies, waits for them, and re-layouts  1.97 us
    ppermute x6, waiting for transfers between devices, shift(): return lax.ppermute(value, ('lat', 'lon'), pairs)  1.33 us
    concatenate x1, other arithmetic, local(): both = jnp.concatenate([tokens, cotangent], axis=-1)  1.21 us
  transfers between devices with their start and end apart: 9, of which 2 were waited for; matrix products, arithmetic and copies ran while one was open for 0% of the time, Pallas kernels for 19%

profile of v2, /device:TPU:0, one launch (start us, length us, event | category | flops | bytes accessed | tf_op | source)
XLA Modules:
  0.0 29.7 jit_solution(5701104861343732995)
XLA Ops:
  0.6 1.2 %pad_maximum_fusion.both = bf16[4,6,24,384]{3,2,1,0:T(8,128)(2,1)S(1)} fusion(bf16[4,6,24,192]{3,2,1,0:T(8,128)(2,1)} %param.11, bf16[4,6,24,192]{3,2,1,0:T(8,128)(2,1)} %param.10), kind=kLoop, calls=%fused_computation | loop fusion | flops 884736 | bytes 884736 | tf_op jit(solution)/shard_map/concatenate | solution.py:405
  1.8 0.2 shard_map.113
  2.1 4.5 %collective-permute-start = (bf16[2,112,384]{2,1,0:T(8,128)(2,1)S(1)}, bf16[2,112,384]{2,1,0:T(8,128)(2,1)S(1)}, u32[]{:S(2)}, u32[]{:S(2)}) collective-permute-start(bf16[2,112,384]{2,1,0:T(8,128)(2,1)S(1)} %get-tuple-element.35), channel_id=1, source_target_pairs={{0,28},{1,29},{2,30},{3,31},{4,0},{5,1},{6,2},{7,3},{8,4},{9,5},{1... | collective-permute-start | bytes 516104 | tf_op jit(solution)/shard_map/ppermute | solution.py:391
  6.6 2.4 %collective-permute-start.1 = (bf16[2,48,384]{2,1,0:T(8,128)(2,1)S(1)}, bf16[2,48,384]{2,1,0:T(8,128)(2,1)S(1)}, u32[]{:S(2)}, u32[]{:S(2)}) collective-permute-start(bf16[2,48,384]{2,1,0:T(8,128)(2,1)S(1)} %get-tuple-element.36), channel_id=1, source_target_pairs={{0,3},{1,0},{2,1},{3,2},{4,7},{5,4},{6,5},{7,6},{8,11},{9,8},{10,9... | collective-permute-start | bytes 221192 | tf_op jit(solution)/shard_map/ppermute | solution.py:391
  9.1 0.4 %collective-permute-start.2 = (bf16[2,48,384]{2,1,0:T(8,128)(2,1)S(1)}, bf16[2,48,384]{2,1,0:T(8,128)(2,1)S(1)}, u32[]{:S(2)}, u32[]{:S(2)}) collective-permute-start(bf16[2,48,384]{2,1,0:T(8,128)(2,1)S(1)} %get-tuple-element.37), channel_id=1, source_target_pairs={{0,31},{1,28},{2,29},{3,30},{4,3},{5,0},{6,1},{7,2},{8,7},{9,4},{1... | collective-permute-start | bytes 221192 | tf_op jit(solution)/shard_map/ppermute | solution.py:391
  9.4 0.0 copy-start
  9.4 1.5 %copy-done = f32[2,1,6,144,144]{4,3,2,1,0:T(8,128)S(1)} copy-done((f32[2,1,6,144,144]{4,3,2,1,0:T(8,128)S(1)}, f32[2,1,6,144,144]{4,3,2,1,0:T(8,128)}, u32[]{:S(2)}) %copy-start) | copy-done | bytes 995352
  10.9 0.0 copy-start.1
  10.9 0.0 copy-start.4
  10.9 0.0 copy-start.5
  10.9 0.0 copy-start.7
  10.9 0.6 %shard_map.114.refs_5_.refs_7_ = f32[2,4,144,256]{3,2,1,0:T(8,128)S(1)} custom-call(f32[2,6,144,144]{3,2,1,0:T(8,128)S(1)} %bitcast.3), custom_call_target="tpu_custom_call" | custom-call | tf_op jit(solution)/shard_map/pallas_call | solution.py:373
  11.5 0.0 collective-permute-done.refs_1_
  11.5 0.3 %copy-done.1 = bf16[192,576]{1,0:T(8,128)(2,1)S(1)} copy-done((bf16[192,576]{1,0:T(8,128)(2,1)S(1)}, bf16[192,576]{1,0:T(8,128)(2,1)}, u32[]{:S(2)}) %copy-start.1) | copy-done | bytes 221208
  11.8 0.0 copy-done.4
  11.8 0.1 copy-done.5
  11.9 0.0 copy-done.7
  12.0 0.0 copy-start.6
  12.0 1.4 %shard_map.115 = (f32[288,192]{1,0:T(8,128)S(1)}, f32[288,128]{1,0:T(8,128)S(1)}, bf16[288,192]{1,0:T(8,128)(2,1)S(1)}, f32[288,192]{1,0:T(8,128)S(1)}, f32[288,...) custom-call(bf16[2,144,384]{2,1,0:T(8,128)(2,1)S(1)} %get-tuple-elem, ...), custom_call_target="tpu_custom_call" | custom-call | flops 1000000000 | tf_op jit(solution)/shard_map/pallas_call | solution.py:373
  13.4 0.0 collective-permute-done.1.refs_2_
  13.4 0.0 collective-permute-done.2.refs_3_
  13.4 0.0 copy-done.6
  13.4 0.0 copy-start.2
  13.4 1.5 %shard_map.116 = (f32[288,192]{1,0:T(8,128)S(1)}, f32[288,128]{1,0:T(8,128)S(1)}, bf16[288,192]{1,0:T(8,128)(2,1)S(1)}, f32[288,192]{1,0:T(8,128)S(1)}, f32[288,...) custom-call(bf16[2,48,384]{2,1,0:T(8,128)(2,1)S(1)} %get-tuple-eleme, ...), custom_call_target="tpu_custom_call" | custom-call | flops 1000000000 | tf_op jit(solution)/shard_map/pallas_call | solution.py:373
  14.9 1.6 %collective-permute-start.6 = (bf16[2,144,256]{2,1,0:T(8,128)(2,1)S(1)}, bf16[2,144,256]{2,1,0:T(8,128)(2,1)S(1)}, u32[]{:S(2)}, u32[]{:S(2)}) collective-permute-start(bf16[2,144,256]{2,1,0:T(8,128)(2,1)S(1)} %get-tuple-element.61), channel_id=1, source_target_pairs={{0,1},{1,0},{2,3},{3,2},{4,5},{5,4},{6,7},{7,6},{8,9},{9,8},{10,11... | collective-permute-start | bytes 442376 | tf_op jit(solution)/shard_map/ppermute | solution.py:451
  16.5 0.7 %collective-permute-start.7 = (bf16[2,144,256]{2,1,0:T(8,128)(2,1)S(1)}, bf16[2,144,256]{2,1,0:T(8,128)(2,1)S(1)}, u32[]{:S(2)}, u32[]{:S(2)}) collective-permute-start(bf16[2,144,256]{2,1,0:T(8,128)(2,1)S(1)} %get-tuple-element.62), channel_id=1, source_target_pairs={{0,2},{1,3},{2,0},{3,1},{4,6},{5,7},{6,4},{7,5},{8,10},{9,11},{10,... | collective-permute-start | bytes 442376 | tf_op jit(solution)/shard_map/ppermute | solution.py:451
  17.2 1.3 %collective-permute-start.8 = (bf16[2,144,256]{2,1,0:T(8,128)(2,1)S(1)}, bf16[2,144,256]{2,1,0:T(8,128)(2,1)S(1)}, u32[]{:S(2)}, u32[]{:S(2)}) collective-permute-start(bf16[2,144,256]{2,1,0:T(8,128)(2,1)S(1)} %get-tuple-element.63), channel_id=1, source_target_pairs={{0,3},{1,2},{2,1},{3,0},{4,7},{5,6},{6,5},{7,4},{8,11},{9,10},{10,... | collective-permute-start | bytes 442376 | tf_op jit(solution)/shard_map/ppermute | solution.py:451
  18.5 0.0 copy-done.2
  18.5 0.0 copy-start.3
  18.5 1.4 %shard_map.117 = (bf16[2,144,192]{2,1,0:T(8,128)(2,1)S(1)}, bf16[2,144,192]{2,1,0:T(8,128)(2,1)S(1)}, bf16[2,48,192]{2,1,0:T(8,128)(2,1)S(1)}, bf16[2,48,192]{2,1,0:T(8,128)(2,1)S(1)}) custom-call(f32[288,192]{1,0:T(8,128)S(1)} %get-tuple-element.40.refs_0_, f32[288,128]{1,0:T(8,128)S(1)} %get-tuple-element.41.refs_1_, ...), custom_call_target="tpu_custom_call" | custom-call | tf_op jit(solution)/shard_map/pallas_call | solution.py:373
  19.8 0.0 copy-done.3
  19.8 1.4 %shard_map.118 = (bf16[2,144,192]{2,1,0:T(8,128)(2,1)S(1)}, bf16[144,384]{1,0:T(8,128)(2,1)S(1)}) custom-call(f32[288,192]{1,0:T(8,128)S(1)} %get-tuple-element.48.refs_0_, f32[288,128]{1,0:T(8,128)S(1)} %get-tuple-element.49.refs_1_, bf16[288,192]{1,0:T(8,128)(2,1)S(1)} %get-tuple-element.50.refs_2_, f32[288,192]{1,0:T(8,128)S(1)} %get-tuple-element.51.refs_3_, ...), custom_call_target="tpu_custom_call" | custom-call | tf_op jit(solution)/shard_map/pallas_call | solution.py:373
  21.3 0.1 collective-permute-start.4
  21.3 0.6 %collective-permute-start.3 = (bf16[2,48,192]{2,1,0:T(8,128)(2,1)S(1)}, bf16[2,48,192]{2,1,0:T(8,128)(2,1)S(1)}, u32[]{:S(2)}, u32[]{:S(2)}) collective-permute-start(bf16[2,48,192]{2,1,0:T(8,128)(2,1)S(1)} %get-tuple-element.47), channel_id=1, source_target_pairs={{0,5},{1,6},{2,7},{3,4},{4,9},{5,10},{6,11},{7,8},{8,13},{9,14},{1... | collective-permute-start | bytes 110600 | tf_op jit(solution)/shard_map/ppermute | solution.py:391
  21.9 0.0 collective-permute-done.6.refs_1_
  21.9 1.2 %collective-permute-start.5 = (bf16[2,48,192]{2,1,0:T(8,128)(2,1)S(1)}, bf16[2,48,192]{2,1,0:T(8,128)(2,1)S(1)}, u32[]{:S(2)}, u32[]{:S(2)}) collective-permute-start(bf16[2,48,192]{2,1,0:T(8,128)(2,1)S(1)} %get-tuple-element.58), channel_id=1, source_target_pairs={{0,1},{1,2},{2,3},{3,0},{4,5},{5,6},{6,7},{7,4},{8,9},{9,10},{10,1... | collective-permute-start | bytes 110600 | tf_op jit(solution)/shard_map/ppermute | solution.py:391
  23.1 3.4 %collective-permute-done.7.refs_2_ = bf16[2,144,256]{2,1,0:T(8,128)(2,1)S(1)} collective-permute-done((bf16[2,144,256]{2,1,0:T(8,128)(2,1)S(1)}, bf16[2,144,256]{2,1,0:T(8,128)(2,1)S(1)}, u32[]{:S(2)}, u32[]{:S(2)}) %collective-permute-start.7) | collective-permute-done | bytes 147488 | tf_op jit(solution)/shard_map/ppermute | solution.py:451
  26.6 0.0 collective-permute-done.8.refs_3_
  26.6 1.0 %shard_map.119 = (f32[432,1,144]{2,1,0:T(1,128)}, f32[8,128]{1,0:T(8,128)S(1)}) custom-call(bf16[2,144,256]{2,1,0:T(8,128)(2,1)S(1)} %get-tuple-element.60.refs_0_, bf16[2,144,256]{2,1,0:T(8,128)(2,1)S(1)} %collective-permute-done.6.refs_1_, bf16[2,144,256]{2,1,0:T(8,128)(2,1)S(1)} %collective-permute-done.7.refs_2_, ...), custom_call_target="tpu_custom_call" | custom-call | tf_op jit(solution)/shard_map/pallas_call | solution.py:373
  27.6 1.3 %collective-permute-done.3.corner = bf16[2,48,192]{2,1,0:T(8,128)(2,1)S(1)} collective-permute-done((bf16[2,48,192]{2,1,0:T(8,128)(2,1)S(1)}, bf16[2,48,192]{2,1,0:T(8,128)(2,1)S(1)}, u32[]{:S(2)}, u32[]{:S(2)}) %collective-permute-start.3) | collective-permute-done | bytes 36896 | tf_op jit(solution)/shard_map/ppermute | solution.py:391
  28.9 0.0 collective-permute-done.5.right
  28.9 0.0 collective-permute-done.4.below
  28.9 0.8 %shard_map.120 = bf16[4,6,24,192]{3,2,1,0:T(8,128)(2,1)} custom-call(bf16[2,48,192]{2,1,0:T(8,128)(2,1)S(1)} %collective-permute-done.3.corner, bf16[144,384]{1,0:T(8,128)(2,1)S(1)} %collective-permute-done.4.below, bf16[2,48,192]{2,1,0:T(8,128)(2,1)S(1)} %collective-permute-done.5.right, bf16[2,144,192]{2,1,0:T(8,128)(2,1)S(1)} %get-tuple-element.59.inner, ...), custom_call_target="tpu_custom_call" | custom-call | tf_op jit(solution)/shard_map/pallas_call | solution.py:373
Async XLA Ops:
  2.1 9.4 %collective-permute-start = (bf16[2,112,384]{2,1,0:T(8,128)(2,1)S(1)}, bf16[2,112,384]{2,1,0:T(8,128)(2,1)S(1)}, u32[]{:S(2)}, u32[]{:S(2)}) collective-permute-start(bf16[2,112,384]{2,1,0:T(8,128)(2,1)S(1)} %get-tuple-element.35), channel_id=1, source_target_pairs={{0,28},{1,29},{2,30},{3,31},{4,0},{5,1},{6,2},{7,3},{8,4},{9,5},{1... | collective-permute-start | bytes 516104 | tf_op jit(solution)/shard_map/ppermute | solution.py:391
  6.6 6.8 %collective-permute-start.1 = (bf16[2,48,384]{2,1,0:T(8,128)(2,1)S(1)}, bf16[2,48,384]{2,1,0:T(8,128)(2,1)S(1)}, u32[]{:S(2)}, u32[]{:S(2)}) collective-permute-start(bf16[2,48,384]{2,1,0:T(8,128)(2,1)S(1)} %get-tuple-element.36), channel_id=1, source_target_pairs={{0,3},{1,0},{2,1},{3,2},{4,7},{5,4},{6,5},{7,6},{8,11},{9,8},{10,9... | collective-permute-start | bytes 221192 | tf_op jit(solution)/shard_map/ppermute | solution.py:391
  9.1 4.3 %collective-permute-start.2 = (bf16[2,48,384]{2,1,0:T(8,128)(2,1)S(1)}, bf16[2,48,384]{2,1,0:T(8,128)(2,1)S(1)}, u32[]{:S(2)}, u32[]{:S(2)}) collective-permute-start(bf16[2,48,384]{2,1,0:T(8,128)(2,1)S(1)} %get-tuple-element.37), channel_id=1, source_target_pairs={{0,31},{1,28},{2,29},{3,30},{4,3},{5,0},{6,1},{7,2},{8,7},{9,4},{1... | collective-permute-start | bytes 221192 | tf_op jit(solution)/shard_map/ppermute | solution.py:391
  9.4 1.5 %copy-start = (f32[2,1,6,144,144]{4,3,2,1,0:T(8,128)S(1)}, f32[2,1,6,144,144]{4,3,2,1,0:T(8,128)}, u32[]{:S(2)}) copy-start(f32[2,1,6,144,144]{4,3,2,1,0:T(8,128)} %param.15) | copy-start | bytes 2985988
  10.9 0.9 %copy-start.1 = (bf16[192,576]{1,0:T(8,128)(2,1)S(1)}, bf16[192,576]{1,0:T(8,128)(2,1)}, u32[]{:S(2)}) copy-start(bf16[192,576]{1,0:T(8,128)(2,1)} %refs_8_.4) | copy-start | bytes 663556
  10.9 0.9 %copy-start.4 = (f32[192]{0:T(256)S(1)}, f32[192]{0:T(256)}, u32[]{:S(2)}) copy-start(f32[192]{0:T(256)} %param.12) | copy-start | bytes 2308
  10.9 1.0 %copy-start.5 = (bf16[192,192]{1,0:T(8,128)(2,1)S(1)}, bf16[192,192]{1,0:T(8,128)(2,1)}, u32[]{:S(2)}) copy-start(bf16[192,192]{1,0:T(8,128)(2,1)} %refs_6_.2) | copy-start | bytes 221188
  10.9 1.1 %copy-start.7 = (bf16[144,256]{1,0:T(8,128)(2,1)S(1)}, bf16[144,256]{1,0:T(8,128)(2,1)}, u32[]{:S(2)}) copy-start(bf16[144,256]{1,0:T(8,128)(2,1)} %constant.8.clone.refs_6_) | copy-start | bytes 221188
  12.0 1.4 %copy-start.6 = (bf16[144,256]{1,0:T(8,128)(2,1)S(1)}, bf16[144,256]{1,0:T(8,128)(2,1)}, u32[]{:S(2)}) copy-start(bf16[144,256]{1,0:T(8,128)(2,1)} %constant.9.clone.refs_8_) | copy-start | bytes 221188
  13.4 5.1 %copy-start.2 = (bf16[384,144]{1,0:T(8,128)(2,1)S(1)}, bf16[384,144]{1,0:T(8,128)(2,1)}, u32[]{:S(2)}) copy-start(bf16[384,144]{1,0:T(8,128)(2,1)} %constant.10.clone.refs_9_) | copy-start | bytes 331780
  14.9 7.0 %collective-permute-start.6 = (bf16[2,144,256]{2,1,0:T(8,128)(2,1)S(1)}, bf16[2,144,256]{2,1,0:T(8,128)(2,1)S(1)}, u32[]{:S(2)}, u32[]{:S(2)}) collective-permute-start(bf16[2,144,256]{2,1,0:T(8,128)(2,1)S(1)} %get-tuple-element.61), channel_id=1, source_target_pairs={{0,1},{1,0},{2,3},{3,2},{4,5},{5,4},{6,7},{7,6},{8,9},{9,8},{10,11... | collective-permute-start | bytes 442376 | tf_op jit(solution)/shard_map/ppermute | solution.py:451
  16.5 10.1 %collective-permute-start.7 = (bf16[2,144,256]{2,1,0:T(8,128)(2,1)S(1)}, bf16[2,144,256]{2,1,0:T(8,128)(2,1)S(1)}, u32[]{:S(2)}, u32[]{:S(2)}) collective-permute-start(bf16[2,144,256]{2,1,0:T(8,128)(2,1)S(1)} %get-tuple-element.62), channel_id=1, source_target_pairs={{0,2},{1,3},{2,0},{3,1},{4,6},{5,7},{6,4},{7,5},{8,10},{9,11},{10,... | collective-permute-start | bytes 442376 | tf_op jit(solution)/shard_map/ppermute | solution.py:451
  17.2 9.4 %collective-permute-start.8 = (bf16[2,144,256]{2,1,0:T(8,128)(2,1)S(1)}, bf16[2,144,256]{2,1,0:T(8,128)(2,1)S(1)}, u32[]{:S(2)}, u32[]{:S(2)}) collective-permute-start(bf16[2,144,256]{2,1,0:T(8,128)(2,1)S(1)} %get-tuple-element.63), channel_id=1, source_target_pairs={{0,3},{1,2},{2,1},{3,0},{4,7},{5,6},{6,5},{7,4},{8,11},{9,10},{10,... | collective-permute-start | bytes 442376 | tf_op jit(solution)/shard_map/ppermute | solution.py:451
  18.5 1.4 %copy-start.3 = (bf16[288,144]{1,0:T(8,128)(2,1)S(1)}, bf16[288,144]{1,0:T(8,128)(2,1)}, u32[]{:S(2)}) copy-start(bf16[288,144]{1,0:T(8,128)(2,1)} %constant.11.clone.refs_9_) | copy-start | bytes 248836
  21.3 7.6 %collective-permute-start.4 = (bf16[144,384]{1,0:T(8,128)(2,1)S(1)}, bf16[144,384]{1,0:T(8,128)(2,1)S(1)}, u32[]{:S(2)}, u32[]{:S(2)}) collective-permute-start(bf16[144,384]{1,0:T(8,128)(2,1)S(1)} %get-tuple-element.57), channel_id=1, source_target_pairs={{0,4},{1,5},{2,6},{3,7},{4,8},{5,9},{6,10},{7,11},{8,12},{9,13},{1... | collective-permute-start | bytes 331784 | tf_op jit(solution)/shard_map/ppermute | solution.py:391
  21.3 7.6 %collective-permute-start.3 = (bf16[2,48,192]{2,1,0:T(8,128)(2,1)S(1)}, bf16[2,48,192]{2,1,0:T(8,128)(2,1)S(1)}, u32[]{:S(2)}, u32[]{:S(2)}) collective-permute-start(bf16[2,48,192]{2,1,0:T(8,128)(2,1)S(1)} %get-tuple-element.47), channel_id=1, source_target_pairs={{0,5},{1,6},{2,7},{3,4},{4,9},{5,10},{6,11},{7,8},{8,13},{9,14},{1... | collective-permute-start | bytes 110600 | tf_op jit(solution)/shard_map/ppermute | solution.py:391
  21.9 7.0 %collective-permute-start.5 = (bf16[2,48,192]{2,1,0:T(8,128)(2,1)S(1)}, bf16[2,48,192]{2,1,0:T(8,128)(2,1)S(1)}, u32[]{:S(2)}, u32[]{:S(2)}) collective-permute-start(bf16[2,48,192]{2,1,0:T(8,128)(2,1)S(1)} %get-tuple-element.58), channel_id=1, source_target_pairs={{0,1},{1,2},{2,3},{3,0},{4,5},{5,6},{6,7},{7,4},{8,9},{9,10},{10,1... | collective-permute-start | bytes 110600 | tf_op jit(solution)/shard_map/ppermute | solution.py:391

commit v3 on v2

--- a/solution.py
+++ b/solution.py
@@ -172,6 +172,37 @@
 def split(inproj):
     channels = inproj.shape[0]
     return [inproj[:, part * channels : (part + 1) * channels] for part in range(3)]
+
+
+def pack(columns):
+    used = columns[0].shape[1]
+    whole = used // LANES * LANES
+    tiles = [part[:, i : i + LANES] for part in columns for i in range(0, whole, LANES)]
+    left = jnp.concatenate([part[:, whole:] for part in columns], axis=1)
+    while left.shape[1] >= LANES:
+        tiles.append(left[:, :LANES])
+        left = left[:, LANES:]
+    if left.shape[1]:
+        tiles.append(jnp.concatenate([left[: WT // 2, : LANES // 2], left[WT // 2 :, : LANES // 2]], axis=1))
+    return jnp.concatenate(tiles, axis=0)
+
+
+def unpack(rows, many, used):
+    whole = used // LANES
+    tiles = [rows[i * WT : (i + 1) * WT] for i in range(rows.shape[0] // WT)]
+    left = tiles[many * whole :]
+    if rows.shape[0] % WT:
+        last = rows[len(tiles) * WT :]
+        left.append(jnp.concatenate([last[:, : LANES // 2], last[:, LANES // 2 :]], axis=0))
+    left = jnp.concatenate(left, axis=1) if left else None
+    rest = used - whole * LANES
+    columns = []
+    for a in range(many):
+        part = tiles[a * whole : (a + 1) * whole]
+        if rest:
+            part.append(left[:, a * rest : (a + 1) * rest])
+        columns.append(jnp.concatenate(part, axis=1))
+    return columns
 
 
 def partner(me, d, parts):
@@ -229,15 +260,17 @@
             if not first:
                 ds += before[a, d]
             if last:
-                turn[d] = ds.astype(BF16)
+                turn[a, d] = ds
             else:
                 totals[0][a, d] = ds
-        if last:
-            for d in range(parts):
-                totals[d][a] = turn[partner(me, d, parts)]
-
-
-def tokens_kernel(chunks, near, first, *refs):
+    if last:
+        for d in range(parts):
+            j = partner(me, d, parts)
+            columns = [turn[a, j][:, : chunks.used] for a in range(level_windows)]
+            totals[d][...] = pack(columns).astype(BF16)
+
+
+def tokens_kernel(chunks, first, *refs):
     standard_in, scale_in, keys, queries_in, ups, p_in, ds_in, gain_ref, inproj, perm_t, *refs = refs
     weights = split(inproj)
     before = None
@@ -327,6 +360,19 @@
         outs[1][...] = jnp.concatenate(packed, axis=1).astype(BF16)
 
 
+def stage_kernel(chunks, windows, *refs):
+    per_window, refs = refs[: 7 * windows], refs[7 * windows :]
+    gain_ref, inproj, *refs = refs
+    orders, refs = refs[:windows], refs[windows:]
+    g_inner, g_below, right, corner, *partial = refs
+    for i in range(windows):
+        ins = (*per_window[7 * i : 7 * (i + 1)], gain_ref, inproj, orders[i])
+        if i == 0:
+            tokens_kernel(chunks, True, *ins, *partial, right, corner)
+        else:
+            tokens_kernel(chunks, False, *ins, *partial, g_inner, g_below)
+
+
 def join_kernel(corner, below, right, inner, after, grad_input):
     levels, _, cols, channels = grad_input.shape
     level_windows = levels // WZ
@@ -351,11 +397,12 @@
     *arrived, bias_grad, after = refs
     after[...] = jnp.zeros(after.shape, F32)
     main, rest, heads = chunks.main, chunks.rest, chunks.heads
-    for a in range(arrived[0].shape[0]):
-        total = arrived[0][a].astype(F32)
-        for other in arrived[1:]:
-            total += other[a].astype(F32)
-        turned = jnp.transpose(total)
+    total = arrived[0][...].astype(F32)
+    for other in arrived[1:]:
+        total += other[...].astype(F32)
+    many = bias_grad.shape[0] // (heads * chunks.size)
+    for a, columns in enumerate(unpack(total, many, chunks.used)):
+        turned = jnp.transpose(columns)
         for h in range(heads):
             at = (a * heads + h) * chunks.size
             if main:
@@ -417,13 +464,14 @@
         [struct((level_windows, lon_count, WT, chunks.width), F32)],
         (bias,),
     )
+    packed = level_windows * chunks.used * WT // LANES
     per_window = []
     total = []
     for c in range(windows):
         last = c == windows - 1
         pieces = (tail, below, right, corner) if last else (inner, below)
         if last:
-            sums = [struct((level_windows, WT, chunks.width), BF16)] * lon_count
+            sums = [struct((packed, LANES), BF16)] * lon_count
         else:
             sums = [struct((level_windows, lon_count, WT, chunks.width), F32)]
         order = jnp.asarray(window_order(cols, c, True), BF16)
@@ -441,7 +489,7 @@
             + sums,
             (*pieces, gain, inproj_weight, outproj_weight, bias_t, order, *total),
             flops=10**9,
-            scratch=[pltpu.VMEM((lon_count, WT, chunks.width), BF16)],
+            scratch=[pltpu.VMEM((level_windows, lon_count, WT, chunks.width), F32)],
         )
         per_window.append(results[:7])
         total = results[7:]
@@ -451,25 +499,22 @@
         arrived.append(lax.ppermute(total[d], "lon", pairs))
     wide = struct((level_windows, half, channels), BF16)
     thin = struct((level_windows, side, channels), BF16)
-    grads = []
-    for c in reversed(range(windows)):
-        last = c == windows - 1
-        order = jnp.asarray(window_order(cols, c, False).T, BF16)
-        results = call(
-            functools.partial(tokens_kernel, chunks, 2, last),
-            [wide, wide, thin, thin] if last else [wide, struct((half, level_windows * channels), BF16)],
-            (*per_window[c], gain, inproj_weight, order, *grads),
-        )
-        grads = results[:2]
-        if last:
-            left, corner = shift(results[2], 0, 1), shift(results[3], 1, 1)
-    above = shift(grads[1], 1, 0)
+    back = list(reversed(range(windows)))
+    g_inner, above, left, corner = call(
+        functools.partial(stage_kernel, chunks, windows),
+        [wide, struct((half, level_windows * channels), BF16), thin, thin],
+        [ref for c in back for ref in per_window[c]]
+        + [gain, inproj_weight]
+        + [jnp.asarray(window_order(cols, c, False).T, BF16) for c in back],
+        scratch=[pltpu.VMEM(wide.shape, BF16)] * 2,
+    )
+    left, corner, above = shift(left, 0, 1), shift(corner, 1, 1), shift(above, 1, 0)
     bias_grad, after = call(
         functools.partial(bias_kernel, chunks),
         [struct((level_windows * heads * chunks.size, 1, WT), F32), struct((8, LANES), F32)],
         arrived,
     )
-    (grad_input,) = call(join_kernel, [struct(tokens.shape, BF16)], (corner, above, left, grads[0], after))
+    (grad_input,) = call(join_kernel, [struct(tokens.shape, BF16)], (corner, above, left, g_inner, after))
     bias_grad = bias_grad.reshape(level_windows, heads, chunks.size, 1, WT)
     return grad_input, jnp.transpose(bias_grad, (0, 3, 1, 2, 4))
 

time: 29.9 us -> 29.9 us (level)
    ppermute x6, waiting for transfers between devices: 1.33 us -> 3.12 us  [shift(): return lax.ppermute(value, ('lat', 'lon'), pairs)]
    ppermute x3, waiting for transfers between devices: 3.44 us -> 1.76 us  [local(): arrived.append(lax.ppermute(total[d], 'lon', pairs))]
    pallas_call x8 -> x7, Pallas kernels: 8.24 us -> 8.31 us  [call(): pl.pallas_call(kernel, out_shape=outs, in_specs=vmem(len(args)), out_spec...]
where the time goes in v3:
time: 29.9 us; the launch traced here: 29.7 us
  starting transfers between devices  12.6 us (42%)
  Pallas kernels  8.31 us (28%)
  waiting for transfers between devices  4.88 us (16%)
  local copies, waits for them, and re-layouts  1.97 us (7%)
  other arithmetic  1.21 us (4%)
  between operations  0.73 us (2%)
    ppermute x6, starting transfers between devices, shift(): return lax.ppermute(value, ('lat', 'lon'), pairs)  9.05 us
    pallas_call x7, Pallas kernels, call(): pl.pallas_call(kernel, out_shape=outs, in_specs=vmem(len(args)), out_spec...  8.31 us
    ppermute x3, starting transfers between devices, local(): arrived.append(lax.ppermute(total[d], 'lon', pairs))  3.55 us
    ppermute x6, waiting for transfers between devices, shift(): return lax.ppermute(value, ('lat', 'lon'), pairs)  3.12 us
    unnamed x16, local copies, waits for them, and re-layouts  1.97 us
    ppermute x3, waiting for transfers between devices, local(): arrived.append(lax.ppermute(total[d], 'lon', pairs))  1.76 us
    concatenate x1, other arithmetic, local(): both = jnp.concatenate([tokens, cotangent], axis=-1)  1.21 us
  transfers between devices with their start and end apart: 9, of which 2 were waited for; matrix products, arithmetic and copies ran while one was open for 0% of the time, Pallas kernels for 19%

profile of v3, /device:TPU:0, one launch (start us, length us, event | category | flops | bytes accessed | tf_op | source)
XLA Modules:
  0.0 29.7 jit_solution(8320301374998610514)
XLA Ops:
  0.6 1.2 %pad_maximum_fusion.both = bf16[4,6,24,384]{3,2,1,0:T(8,128)(2,1)S(1)} fusion(bf16[4,6,24,192]{3,2,1,0:T(8,128)(2,1)} %param.11, bf16[4,6,24,192]{3,2,1,0:T(8,128)(2,1)} %param.10), kind=kLoop, calls=%fused_computation | loop fusion | flops 884736 | bytes 884736 | tf_op jit(solution)/shard_map/concatenate | solution.py:452
  1.8 0.2 shard_map.113
  2.1 4.5 %collective-permute-start = (bf16[2,112,384]{2,1,0:T(8,128)(2,1)S(1)}, bf16[2,112,384]{2,1,0:T(8,128)(2,1)S(1)}, u32[]{:S(2)}, u32[]{:S(2)}) collective-permute-start(bf16[2,112,384]{2,1,0:T(8,128)(2,1)S(1)} %get-tuple-element.33), channel_id=1, source_target_pairs={{0,28},{1,29},{2,30},{3,31},{4,0},{5,1},{6,2},{7,3},{8,4},{9,5},{1... | collective-permute-start | bytes 516104 | tf_op jit(solution)/shard_map/ppermute | solution.py:438
  6.6 2.4 %collective-permute-start.1 = (bf16[2,48,384]{2,1,0:T(8,128)(2,1)S(1)}, bf16[2,48,384]{2,1,0:T(8,128)(2,1)S(1)}, u32[]{:S(2)}, u32[]{:S(2)}) collective-permute-start(bf16[2,48,384]{2,1,0:T(8,128)(2,1)S(1)} %get-tuple-element.34), channel_id=1, source_target_pairs={{0,3},{1,0},{2,1},{3,2},{4,7},{5,4},{6,5},{7,6},{8,11},{9,8},{10,9... | collective-permute-start | bytes 221192 | tf_op jit(solution)/shard_map/ppermute | solution.py:438
  9.1 0.4 %collective-permute-start.2 = (bf16[2,48,384]{2,1,0:T(8,128)(2,1)S(1)}, bf16[2,48,384]{2,1,0:T(8,128)(2,1)S(1)}, u32[]{:S(2)}, u32[]{:S(2)}) collective-permute-start(bf16[2,48,384]{2,1,0:T(8,128)(2,1)S(1)} %get-tuple-element.35), channel_id=1, source_target_pairs={{0,31},{1,28},{2,29},{3,30},{4,3},{5,0},{6,1},{7,2},{8,7},{9,4},{1... | collective-permute-start | bytes 221192 | tf_op jit(solution)/shard_map/ppermute | solution.py:438
  9.4 0.0 copy-start
  9.4 1.5 %copy-done = f32[2,1,6,144,144]{4,3,2,1,0:T(8,128)S(1)} copy-done((f32[2,1,6,144,144]{4,3,2,1,0:T(8,128)S(1)}, f32[2,1,6,144,144]{4,3,2,1,0:T(8,128)}, u32[]{:S(2)}) %copy-start) | copy-done | bytes 995352
  10.9 0.0 copy-start.1
  10.9 0.0 copy-start.4
  10.9 0.0 copy-start.5
  10.9 0.0 copy-start.7
  10.9 0.6 %shard_map.114.refs_5_.refs_7_ = f32[2,4,144,256]{3,2,1,0:T(8,128)S(1)} custom-call(f32[2,6,144,144]{3,2,1,0:T(8,128)S(1)} %bitcast.3), custom_call_target="tpu_custom_call" | custom-call | tf_op jit(solution)/shard_map/pallas_call | solution.py:420
  11.5 0.0 collective-permute-done.refs_1_
  11.5 0.3 %copy-done.1 = bf16[192,576]{1,0:T(8,128)(2,1)S(1)} copy-done((bf16[192,576]{1,0:T(8,128)(2,1)S(1)}, bf16[192,576]{1,0:T(8,128)(2,1)}, u32[]{:S(2)}) %copy-start.1) | copy-done | bytes 221208
  11.8 0.0 copy-done.4
  11.8 0.1 copy-done.5
  11.9 0.0 copy-done.7
  12.0 0.0 copy-start.6
  12.0 1.4 %shard_map.115 = (f32[288,192]{1,0:T(8,128)S(1)}, f32[288,128]{1,0:T(8,128)S(1)}, bf16[288,192]{1,0:T(8,128)(2,1)S(1)}, f32[288,192]{1,0:T(8,128)S(1)}, f32[288,...) custom-call(bf16[2,144,384]{2,1,0:T(8,128)(2,1)S(1)} %get-tuple-elem, ...), custom_call_target="tpu_custom_call" | custom-call | flops 1000000000 | tf_op jit(solution)/shard_map/pallas_call | solution.py:420
  13.4 0.0 collective-permute-done.1.refs_2_
  13.4 0.0 collective-permute-done.2.refs_3_
  13.4 0.0 copy-done.6
  13.4 0.0 copy-start.2
  13.4 0.0 copy-start.3
  13.4 1.6 %shard_map.116 = (f32[288,192]{1,0:T(8,128)S(1)}, f32[288,128]{1,0:T(8,128)S(1)}, bf16[288,192]{1,0:T(8,128)(2,1)S(1)}, f32[288,192]{1,0:T(8,128)S(1)}, f32[288,...) custom-call(bf16[2,48,384]{2,1,0:T(8,128)(2,1)S(1)} %get-tuple-eleme, ...), custom_call_target="tpu_custom_call" | custom-call | flops 1000000000 | tf_op jit(solution)/shard_map/pallas_call | solution.py:420
  15.0 1.6 %collective-permute-start.6 = (bf16[504,128]{1,0:T(8,128)(2,1)S(1)}, bf16[504,128]{1,0:T(8,128)(2,1)S(1)}, u32[]{:S(2)}, u32[]{:S(2)}) collective-permute-start(bf16[504,128]{1,0:T(8,128)(2,1)S(1)} %get-tuple-element.57), channel_id=1, source_target_pairs={{0,1},{1,0},{2,3},{3,2},{4,5},{5,4},{6,7},{7,6},{8,9},{9,8},{10,11... | collective-permute-start | bytes 387080 | tf_op jit(solution)/shard_map/ppermute | solution.py:499
  16.6 0.7 %collective-permute-start.7 = (bf16[504,128]{1,0:T(8,128)(2,1)S(1)}, bf16[504,128]{1,0:T(8,128)(2,1)S(1)}, u32[]{:S(2)}, u32[]{:S(2)}) collective-permute-start(bf16[504,128]{1,0:T(8,128)(2,1)S(1)} %get-tuple-element.58), channel_id=1, source_target_pairs={{0,2},{1,3},{2,0},{3,1},{4,6},{5,7},{6,4},{7,5},{8,10},{9,11},{10,... | collective-permute-start | bytes 387080 | tf_op jit(solution)/shard_map/ppermute | solution.py:499
  17.3 1.3 %collective-permute-start.8 = (bf16[504,128]{1,0:T(8,128)(2,1)S(1)}, bf16[504,128]{1,0:T(8,128)(2,1)S(1)}, u32[]{:S(2)}, u32[]{:S(2)}) collective-permute-start(bf16[504,128]{1,0:T(8,128)(2,1)S(1)} %get-tuple-element.59), channel_id=1, source_target_pairs={{0,3},{1,2},{2,1},{3,0},{4,7},{5,6},{6,5},{7,4},{8,11},{9,10},{10,... | collective-permute-start | bytes 387080 | tf_op jit(solution)/shard_map/ppermute | solution.py:499
  18.6 0.0 copy-done.2
  18.6 0.0 copy-done.3
  18.6 2.7 %shard_map.117 = (bf16[2,144,192]{2,1,0:T(8,128)(2,1)S(1)}, bf16[144,384]{1,0:T(8,128)(2,1)S(1)}, bf16[2,48,192]{2,1,0:T(8,128)(2,1)S(1)}, bf16[2,48,192]{2,1,0:T(8,128)(2,1)S(1)}) custom-call(f32[288,192]{1,0:T(8,128)S(1)} %get-tuple-element.38.refs_0_, f32[288,128]{1,0:T(8,128)S(1)} %get-tuple-element.39.refs_1_, ...), custom_call_target="tpu_custom_call" | custom-call | tf_op jit(solution)/shard_map/pallas_call | solution.py:420
  21.3 0.1 collective-permute-start.4
  21.3 0.6 %collective-permute-start.3 = (bf16[2,48,192]{2,1,0:T(8,128)(2,1)S(1)}, bf16[2,48,192]{2,1,0:T(8,128)(2,1)S(1)}, u32[]{:S(2)}, u32[]{:S(2)}) collective-permute-start(bf16[2,48,192]{2,1,0:T(8,128)(2,1)S(1)} %get-tuple-element.52), channel_id=1, source_target_pairs={{0,5},{1,6},{2,7},{3,4},{4,9},{5,10},{6,11},{7,8},{8,13},{9,14},{1... | collective-permute-start | bytes 110600 | tf_op jit(solution)/shard_map/ppermute | solution.py:438
  21.9 0.0 collective-permute-done.6.refs_1_
  21.9 1.0 %collective-permute-start.5 = (bf16[2,48,192]{2,1,0:T(8,128)(2,1)S(1)}, bf16[2,48,192]{2,1,0:T(8,128)(2,1)S(1)}, u32[]{:S(2)}, u32[]{:S(2)}) collective-permute-start(bf16[2,48,192]{2,1,0:T(8,128)(2,1)S(1)} %get-tuple-element.54), channel_id=1, source_target_pairs={{0,1},{1,2},{2,3},{3,0},{4,5},{5,6},{6,7},{7,4},{8,9},{9,10},{10,1... | collective-permute-start | bytes 110600 | tf_op jit(solution)/shard_map/ppermute | solution.py:438
  23.0 1.8 %collective-permute-done.7.refs_2_ = bf16[504,128]{1,0:T(8,128)(2,1)S(1)} collective-permute-done((bf16[504,128]{1,0:T(8,128)(2,1)S(1)}, bf16[504,128]{1,0:T(8,128)(2,1)S(1)}, u32[]{:S(2)}, u32[]{:S(2)}) %collective-permute-start.7) | collective-permute-done | bytes 129056 | tf_op jit(solution)/shard_map/ppermute | solution.py:499
  24.7 0.0 collective-permute-done.8.refs_3_
  24.7 1.1 %shard_map.118 = (f32[432,1,144]{2,1,0:T(1,128)}, f32[8,128]{1,0:T(8,128)S(1)}) custom-call(bf16[504,128]{1,0:T(8,128)(2,1)S(1)} %get-tuple-element.56.refs_0_, bf16[504,128]{1,0:T(8,128)(2,1)S(1)} %collective-permute-done.6.refs_1_, bf16[504,128]{1,0:T(8,128)(2,1)S(1)} %collective-permute-done.7.refs_2_, bf16[504,128]{1,0:T(8,128)(2,1)S(1)} %collective-permute-done.8.refs_3_), custom_call_target="tpu_custom_call" | custom-call | tf_op jit(solution)/shard_map/pallas_call | solution.py:420
  25.8 3.1 %collective-permute-done.3.corner = bf16[2,48,192]{2,1,0:T(8,128)(2,1)S(1)} collective-permute-done((bf16[2,48,192]{2,1,0:T(8,128)(2,1)S(1)}, bf16[2,48,192]{2,1,0:T(8,128)(2,1)S(1)}, u32[]{:S(2)}, u32[]{:S(2)}) %collective-permute-start.3) | collective-permute-done | bytes 36896 | tf_op jit(solution)/shard_map/ppermute | solution.py:438
  28.9 0.0 collective-permute-done.5.right
  28.9 0.0 collective-permute-done.4.below
  28.9 0.8 %shard_map.119 = bf16[4,6,24,192]{3,2,1,0:T(8,128)(2,1)} custom-call(bf16[2,48,192]{2,1,0:T(8,128)(2,1)S(1)} %collective-permute-done.3.corner, bf16[144,384]{1,0:T(8,128)(2,1)S(1)} %collective-permute-done.4.below, bf16[2,48,192]{2,1,0:T(8,128)(2,1)S(1)} %collective-permute-done.5.right, bf16[2,144,192]{2,1,0:T(8,128)(2,1)S(1)} %get-tuple-element.55.inner, ...), custom_call_target="tpu_custom_call" | custom-call | tf_op jit(solution)/shard_map/pallas_call | solution.py:420
Async XLA Ops:
  2.1 9.4 %collective-permute-start = (bf16[2,112,384]{2,1,0:T(8,128)(2,1)S(1)}, bf16[2,112,384]{2,1,0:T(8,128)(2,1)S(1)}, u32[]{:S(2)}, u32[]{:S(2)}) collective-permute-start(bf16[2,112,384]{2,1,0:T(8,128)(2,1)S(1)} %get-tuple-element.33), channel_id=1, source_target_pairs={{0,28},{1,29},{2,30},{3,31},{4,0},{5,1},{6,2},{7,3},{8,4},{9,5},{1... | collective-permute-start | bytes 516104 | tf_op jit(solution)/shard_map/ppermute | solution.py:438
  6.6 6.8 %collective-permute-start.1 = (bf16[2,48,384]{2,1,0:T(8,128)(2,1)S(1)}, bf16[2,48,384]{2,1,0:T(8,128)(2,1)S(1)}, u32[]{:S(2)}, u32[]{:S(2)}) collective-permute-start(bf16[2,48,384]{2,1,0:T(8,128)(2,1)S(1)} %get-tuple-element.34), channel_id=1, source_target_pairs={{0,3},{1,0},{2,1},{3,2},{4,7},{5,4},{6,5},{7,6},{8,11},{9,8},{10,9... | collective-permute-start | bytes 221192 | tf_op jit(solution)/shard_map/ppermute | solution.py:438
  9.1 4.3 %collective-permute-start.2 = (bf16[2,48,384]{2,1,0:T(8,128)(2,1)S(1)}, bf16[2,48,384]{2,1,0:T(8,128)(2,1)S(1)}, u32[]{:S(2)}, u32[]{:S(2)}) collective-permute-start(bf16[2,48,384]{2,1,0:T(8,128)(2,1)S(1)} %get-tuple-element.35), channel_id=1, source_target_pairs={{0,31},{1,28},{2,29},{3,30},{4,3},{5,0},{6,1},{7,2},{8,7},{9,4},{1... | collective-permute-start | bytes 221192 | tf_op jit(solution)/shard_map/ppermute | solution.py:438
  9.4 1.5 %copy-start = (f32[2,1,6,144,144]{4,3,2,1,0:T(8,128)S(1)}, f32[2,1,6,144,144]{4,3,2,1,0:T(8,128)}, u32[]{:S(2)}) copy-start(f32[2,1,6,144,144]{4,3,2,1,0:T(8,128)} %param.15) | copy-start | bytes 2985988
  10.9 0.9 %copy-start.1 = (bf16[192,576]{1,0:T(8,128)(2,1)S(1)}, bf16[192,576]{1,0:T(8,128)(2,1)}, u32[]{:S(2)}) copy-start(bf16[192,576]{1,0:T(8,128)(2,1)} %refs_15_.1) | copy-start | bytes 663556
  10.9 0.9 %copy-start.4 = (f32[192]{0:T(256)S(1)}, f32[192]{0:T(256)}, u32[]{:S(2)}) copy-start(f32[192]{0:T(256)} %param.12) | copy-start | bytes 2308
  10.9 1.0 %copy-start.5 = (bf16[192,192]{1,0:T(8,128)(2,1)S(1)}, bf16[192,192]{1,0:T(8,128)(2,1)}, u32[]{:S(2)}) copy-start(bf16[192,192]{1,0:T(8,128)(2,1)} %refs_6_.2) | copy-start | bytes 221188
  10.9 1.1 %copy-start.7 = (bf16[144,256]{1,0:T(8,128)(2,1)S(1)}, bf16[144,256]{1,0:T(8,128)(2,1)}, u32[]{:S(2)}) copy-start(bf16[144,256]{1,0:T(8,128)(2,1)} %constant.8.clone.refs_6_) | copy-start | bytes 221188
  12.0 1.4 %copy-start.6 = (bf16[144,256]{1,0:T(8,128)(2,1)S(1)}, bf16[144,256]{1,0:T(8,128)(2,1)}, u32[]{:S(2)}) copy-start(bf16[144,256]{1,0:T(8,128)(2,1)} %constant.9.clone.refs_8_) | copy-start | bytes 221188
  13.4 5.2 %copy-start.2 = (bf16[384,144]{1,0:T(8,128)(2,1)S(1)}, bf16[384,144]{1,0:T(8,128)(2,1)}, u32[]{:S(2)}) copy-start(bf16[384,144]{1,0:T(8,128)(2,1)} %constant.10.clone.refs_16_) | copy-start | bytes 331780
  13.4 5.2 %copy-start.3 = (bf16[288,144]{1,0:T(8,128)(2,1)S(1)}, bf16[288,144]{1,0:T(8,128)(2,1)}, u32[]{:S(2)}) copy-start(bf16[288,144]{1,0:T(8,128)(2,1)} %constant.11.clone.refs_17_) | copy-start | bytes 248836
  15.0 6.9 %collective-permute-start.6 = (bf16[504,128]{1,0:T(8,128)(2,1)S(1)}, bf16[504,128]{1,0:T(8,128)(2,1)S(1)}, u32[]{:S(2)}, u32[]{:S(2)}) collective-permute-start(bf16[504,128]{1,0:T(8,128)(2,1)S(1)} %get-tuple-element.57), channel_id=1, source_target_pairs={{0,1},{1,0},{2,3},{3,2},{4,5},{5,4},{6,7},{7,6},{8,9},{9,8},{10,11... | collective-permute-start | bytes 387080 | tf_op jit(solution)/shard_map/ppermute | solution.py:499
  16.6 8.1 %collective-permute-start.7 = (bf16[504,128]{1,0:T(8,128)(2,1)S(1)}, bf16[504,128]{1,0:T(8,128)(2,1)S(1)}, u32[]{:S(2)}, u32[]{:S(2)}) collective-permute-start(bf16[504,128]{1,0:T(8,128)(2,1)S(1)} %get-tuple-element.58), channel_id=1, source_target_pairs={{0,2},{1,3},{2,0},{3,1},{4,6},{5,7},{6,4},{7,5},{8,10},{9,11},{10,... | collective-permute-start | bytes 387080 | tf_op jit(solution)/shard_map/ppermute | solution.py:499
  17.3 7.4 %collective-permute-start.8 = (bf16[504,128]{1,0:T(8,128)(2,1)S(1)}, bf16[504,128]{1,0:T(8,128)(2,1)S(1)}, u32[]{:S(2)}, u32[]{:S(2)}) collective-permute-start(bf16[504,128]{1,0:T(8,128)(2,1)S(1)} %get-tuple-element.59), channel_id=1, source_target_pairs={{0,3},{1,2},{2,1},{3,0},{4,7},{5,6},{6,5},{7,4},{8,11},{9,10},{10,... | collective-permute-start | bytes 387080 | tf_op jit(solution)/shard_map/ppermute | solution.py:499
  21.3 7.7 %collective-permute-start.4 = (bf16[144,384]{1,0:T(8,128)(2,1)S(1)}, bf16[144,384]{1,0:T(8,128)(2,1)S(1)}, u32[]{:S(2)}, u32[]{:S(2)}) collective-permute-start(bf16[144,384]{1,0:T(8,128)(2,1)S(1)} %get-tuple-element.53), channel_id=1, source_target_pairs={{0,4},{1,5},{2,6},{3,7},{4,8},{5,9},{6,10},{7,11},{8,12},{9,13},{1... | collective-permute-start | bytes 331784 | tf_op jit(solution)/shard_map/ppermute | solution.py:438
  21.3 7.6 %collective-permute-start.3 = (bf16[2,48,192]{2,1,0:T(8,128)(2,1)S(1)}, bf16[2,48,192]{2,1,0:T(8,128)(2,1)S(1)}, u32[]{:S(2)}, u32[]{:S(2)}) collective-permute-start(bf16[2,48,192]{2,1,0:T(8,128)(2,1)S(1)} %get-tuple-element.52), channel_id=1, source_target_pairs={{0,5},{1,6},{2,7},{3,4},{4,9},{5,10},{6,11},{7,8},{8,13},{9,14},{1... | collective-permute-start | bytes 110600 | tf_op jit(solution)/shard_map/ppermute | solution.py:438
  21.9 7.0 %collective-permute-start.5 = (bf16[2,48,192]{2,1,0:T(8,128)(2,1)S(1)}, bf16[2,48,192]{2,1,0:T(8,128)(2,1)S(1)}, u32[]{:S(2)}, u32[]{:S(2)}) collective-permute-start(bf16[2,48,192]{2,1,0:T(8,128)(2,1)S(1)} %get-tuple-element.54), channel_id=1, source_target_pairs={{0,1},{1,2},{2,3},{3,0},{4,5},{5,6},{6,7},{7,4},{8,9},{9,10},{10,1... | collective-permute-start | bytes 110600 | tf_op jit(solution)/shard_map/ppermute | solution.py:438

commit v4 on v3

--- a/solution.py
+++ b/solution.py
@@ -57,20 +57,34 @@
         return j * self.size + jnp.where(lane < low, main, left)
 
 
-def window_order(cols, c, narrow):
+def side_order(cols):
+    part = HALF_ROWS * cols
+    table = np.zeros((round_up(WZ * WH * HALF_COLS, 16), 2 * WZ * part), np.float32)
+    for z in range(WZ):
+        for r in range(WH):
+            low, row = divmod(r, HALF_ROWS)
+            for w in range(HALF_COLS):
+                table[(z * WH + r) * HALF_COLS + w, (low * WZ + z) * part + row * cols + w] = 1.0
+    return table
+
+
+def window_order(cols, c, out):
     last = c == cols // WW - 1
     part, side = HALF_ROWS * cols, HALF_ROWS * SIDE
-    kept = cols - HALF_COLS if narrow else cols
-    tail = narrow and last
+    kept = cols if out else cols - HALF_COLS
+    tail = last and not out
     inner = WZ * (side if tail else part)
     near = inner + round_up(WZ * HALF_ROWS * kept, 16)
-    table = np.zeros((WT, near + last * 2 * WZ * side), np.float32)
+    extra = round_up(WZ * WH * HALF_COLS, 16) if out else 2 * WZ * side
+    table = np.zeros((WT, near + last * extra), np.float32)
     for z in range(WZ):
         for r in range(WH):
             for w in range(WW):
                 col = c * WW + w + HALF_COLS
                 low, row = divmod(r, HALF_ROWS)
-                if col >= cols:
+                if col >= cols and out:
+                    at = near + (z * WH + r) * HALF_COLS + col - cols
+                elif col >= cols:
                     at = near + (low * WZ + z) * side + row * SIDE + col - cols
                 elif low:
                     at = inner + (z * HALF_ROWS + row) * kept + col - (cols - kept)
@@ -216,7 +230,7 @@
     before = None
     if not first:
         before, *refs = refs
-    standard_out, scale_out, keys_out, query_out, up_out, p_out, ds_out, *totals, turn = refs
+    standard_out, scale_out, keys_out, query_out, up_out, p_out, ds_out, total_out = refs
     parts, width = chunks.parts, chunks.width
     channels = outproj.shape[0]
     scaling = (channels // chunks.heads) ** (-0.5)
@@ -260,14 +274,9 @@
             if not first:
                 ds += before[a, d]
             if last:
-                turn[a, d] = ds
+                total_out[a, d] = ds
             else:
-                totals[0][a, d] = ds
-    if last:
-        for d in range(parts):
-            j = partner(me, d, parts)
-            columns = [turn[a, j][:, : chunks.used] for a in range(level_windows)]
-            totals[d][...] = pack(columns).astype(BF16)
+                total_out[a, d] = ds
 
 
 def tokens_kernel(chunks, first, *refs):
@@ -341,39 +350,41 @@
         - standard * jnp.mean(scaled * standard, axis=-1, keepdims=True)
     )
     grad = grad.astype(BF16)
-    lows = []
     for a in range(level_windows):
         spread = dot(perm_t[...], grad[a * WT : (a + 1) * WT])
         base = 0
         for i, out in enumerate(outs):
-            rows = out.shape[-2]
+            rows = out.shape[1]
             part = spread[base : base + rows]
             if not first and i < 2:
                 part += before[i][a].astype(F32)
-            if not first and i == 1:
-                lows.append(part)
-            else:
-                out[a] = part.astype(BF16)
+            out[a] = part.astype(BF16)
             base += rows
-    if not first:
-        packed = [low[:, :LANES] for low in lows] + [low[:, LANES:] for low in lows]
-        outs[1][...] = jnp.concatenate(packed, axis=1).astype(BF16)
-
-
-def stage_kernel(chunks, windows, *refs):
-    per_window, refs = refs[: 7 * windows], refs[7 * windows :]
-    gain_ref, inproj, *refs = refs
-    orders, refs = refs[:windows], refs[windows:]
-    g_inner, g_below, right, corner, *partial = refs
-    for i in range(windows):
-        ins = (*per_window[7 * i : 7 * (i + 1)], gain_ref, inproj, orders[i])
-        if i == 0:
-            tokens_kernel(chunks, True, *ins, *partial, right, corner)
-        else:
-            tokens_kernel(chunks, False, *ins, *partial, g_inner, g_below)
-
-
-def join_kernel(corner, below, right, inner, after, grad_input):
+
+
+def first_kernel(chunks, *refs):
+    *ins, total, inner, below, side = refs[:14]
+    messages = refs[14:]
+    me = lax.axis_index("lon")
+    for d, message in enumerate(messages):
+        j = partner(me, d, chunks.parts)
+        columns = [total[a, j][:, : chunks.used] for a in range(total.shape[0])]
+        message[...] = pack(columns).astype(BF16)
+    tokens_kernel(chunks, True, *ins, inner, below, side)
+
+
+def merge_kernel(inner_in, below_in, side, order_t, inner, below):
+    half = inner.shape[1]
+    lows = []
+    for a in range(inner.shape[0]):
+        spread = dot(order_t[...], side[a])
+        inner[a] = (inner_in[a].astype(F32) + spread[:half]).astype(BF16)
+        lows.append(below_in[a].astype(F32) + spread[half:])
+    packed = [low[:, :LANES] for low in lows] + [low[:, LANES:] for low in lows]
+    below[...] = jnp.concatenate(packed, axis=1).astype(BF16)
+
+
+def join_kernel(inner, below, after, grad_input):
     levels, _, cols, channels = grad_input.shape
     level_windows = levels // WZ
     whole = below[...].astype(F32)
@@ -382,15 +393,13 @@
         low = jnp.concatenate(
             [whole[:, a * LANES : (a + 1) * LANES], whole[:, rest_at : rest_at + channels - LANES]], axis=1
         )
-        parts = ((low, corner[a].astype(F32), 0), (inner[a].astype(F32), right[a].astype(F32), HALF_ROWS))
+        high = inner[a].astype(F32)
         for z in range(WZ):
             level = (a * WZ + WZ // 2 + z) % levels
             for row in range(HALF_ROWS):
-                at = z * HALF_ROWS + row
-                for wide, side, base in parts:
-                    first = wide[at * cols : at * cols + SIDE] + side[at * SIDE : (at + 1) * SIDE]
-                    rest = wide[at * cols + SIDE : (at + 1) * cols]
-                    grad_input[level, base + row] = jnp.concatenate([first, rest], axis=0).astype(BF16)
+                at = slice((z * HALF_ROWS + row) * cols, (z * HALF_ROWS + row + 1) * cols)
+                grad_input[level, row] = low[at].astype(BF16)
+                grad_input[level, HALF_ROWS + row] = high[at].astype(BF16)
 
 
 def bias_kernel(chunks, *refs):
@@ -447,6 +456,7 @@
     struct = jax.ShapeDtypeStruct
     half, side = WZ * HALF_ROWS * cols, WZ * HALF_ROWS * SIDE
     gain = norm_gain.reshape(1, channels)
+    side_table = side_order(cols)
 
     bias = bias.reshape(level_windows, heads, WT, WT)
     both = jnp.concatenate([tokens, cotangent], axis=-1)
@@ -470,11 +480,8 @@
     for c in range(windows):
         last = c == windows - 1
         pieces = (tail, below, right, corner) if last else (inner, below)
-        if last:
-            sums = [struct((packed, LANES), BF16)] * lon_count
-        else:
-            sums = [struct((level_windows, lon_count, WT, chunks.width), F32)]
-        order = jnp.asarray(window_order(cols, c, True), BF16)
+        sums = [struct((level_windows, lon_count, WT, chunks.width), F32)]
+        order = jnp.asarray(window_order(cols, c, False), BF16)
         results = call(
             functools.partial(scores_kernel, chunks, len(pieces), c == 0, last),
             [
@@ -489,32 +496,41 @@
             + sums,
             (*pieces, gain, inproj_weight, outproj_weight, bias_t, order, *total),
             flops=10**9,
-            scratch=[pltpu.VMEM((level_windows, lon_count, WT, chunks.width), F32)],
         )
         per_window.append(results[:7])
         total = results[7:]
-    arrived = [total[0]]
-    for d in range(1, lon_count):
-        pairs = [(i, partner(i, d, lon_count)) for i in range(lon_count)]
-        arrived.append(lax.ppermute(total[d], "lon", pairs))
     wide = struct((level_windows, half, channels), BF16)
-    thin = struct((level_windows, side, channels), BF16)
-    back = list(reversed(range(windows)))
-    g_inner, above, left, corner = call(
-        functools.partial(stage_kernel, chunks, windows),
-        [wide, struct((half, level_windows * channels), BF16), thin, thin],
-        [ref for c in back for ref in per_window[c]]
-        + [gain, inproj_weight]
-        + [jnp.asarray(window_order(cols, c, False).T, BF16) for c in back],
-        scratch=[pltpu.VMEM(wide.shape, BF16)] * 2,
-    )
-    left, corner, above = shift(left, 0, 1), shift(corner, 1, 1), shift(above, 1, 0)
+    grads = []
+    for c in reversed(range(windows)):
+        order = jnp.asarray(window_order(cols, c, True).T, BF16)
+        ins = (*per_window[c], gain, inproj_weight, order)
+        if c == windows - 1:
+            results = call(
+                functools.partial(first_kernel, chunks),
+                [wide, wide, struct((level_windows, side_table.shape[0], channels), BF16)]
+                + [struct((packed, LANES), BF16)] * lon_count,
+                (*ins, *total),
+            )
+            left = shift(results[2], 0, 1)
+            arrived = [results[3]]
+            for d in range(1, lon_count):
+                pairs = [(i, partner(i, d, lon_count)) for i in range(lon_count)]
+                arrived.append(lax.ppermute(results[3 + d], "lon", pairs))
+        else:
+            results = call(functools.partial(tokens_kernel, chunks, False), [wide] * 2, (*ins, *grads))
+        grads = results[:2]
+    g_inner, g_below = call(
+        merge_kernel,
+        [wide, struct((half, level_windows * channels), BF16)],
+        (*grads, left, jnp.asarray(side_table.T, BF16)),
+    )
+    above = shift(g_below, 1, 0)
     bias_grad, after = call(
         functools.partial(bias_kernel, chunks),
         [struct((level_windows * heads * chunks.size, 1, WT), F32), struct((8, LANES), F32)],
         arrived,
     )
-    (grad_input,) = call(join_kernel, [struct(tokens.shape, BF16)], (corner, above, left, g_inner, after))
+    (grad_input,) = call(join_kernel, [struct(tokens.shape, BF16)], (g_inner, above, after))
     bias_grad = bias_grad.reshape(level_windows, heads, chunks.size, 1, WT)
     return grad_input, jnp.transpose(bias_grad, (0, 3, 1, 2, 4))
 

time: 29.9 us -> 30 us (level)
    ppermute x3, waiting for transfers between devices: 1.76 us -> 4.35 us  [local(): arrived.append(lax.ppermute(results[3 + d], 'lon', pairs))]
    ppermute x6 -> x5, waiting for transfers between devices: 3.12 us -> 0.54 us  [shift(): return lax.ppermute(value, ('lat', 'lon'), pairs)]
    pallas_call x7 -> x9, Pallas kernels: 8.31 us -> 8.5 us  [call(): pl.pallas_call(kernel, out_shape=outs, in_specs=vmem(len(args)), out_spec...]
    ppermute x6 -> x5, starting transfers between devices: 9.05 us -> 8.95 us  [shift(): return lax.ppermute(value, ('lat', 'lon'), pairs)]
    unnamed x16 -> x18, local copies, waits for them, and re-layouts: 1.97 us -> 1.98 us
  transfers between devices with their start and end apart: 9 -> 8, of which waited for: 2 -> 4; matrix products, arithmetic and copies ran while one was open for 0% -> 0% of each run, Pallas kernels for 19% -> 16%
where the time goes in v4:
time: 30 us; the launch traced here: 29.8 us
  starting transfers between devices  12.4 us (41%)
  Pallas kernels  8.5 us (28%)
  waiting for transfers between devices  4.89 us (16%)
  local copies, waits for them, and re-layouts  1.98 us (7%)
  other arithmetic  1.21 us (4%)
  between operations  0.77 us (3%)
    ppermute x5, starting transfers between devices, shift(): return lax.ppermute(value, ('lat', 'lon'), pairs)  8.95 us
    pallas_call x9, Pallas kernels, call(): pl.pallas_call(kernel, out_shape=outs, in_specs=vmem(len(args)), out_spec...  8.5 us
    ppermute x3, waiting for transfers between devices, local(): arrived.append(lax.ppermute(results[3 + d], 'lon', pairs))  4.35 us
    ppermute x3, starting transfers between devices, local(): arrived.append(lax.ppermute(results[3 + d], 'lon', pairs))  3.49 us
    unnamed x18, local copies, waits for them, and re-layouts  1.98 us
    concatenate x1, other arithmetic, local(): both = jnp.concatenate([tokens, cotangent], axis=-1)  1.21 us
  transfers between devices with their start and end apart: 8, of which 4 were waited for; matrix products, arithmetic and copies ran while one was open for 0% of the time, Pallas kernels for 16%

profile of v4, /device:TPU:0, one launch (start us, length us, event | category | flops | bytes accessed | tf_op | source)
XLA Modules:
  0.0 29.8 jit_solution(4682435914206919495)
XLA Ops:
  0.6 1.2 %pad_maximum_fusion.both = bf16[4,6,24,384]{3,2,1,0:T(8,128)(2,1)S(1)} fusion(bf16[4,6,24,192]{3,2,1,0:T(8,128)(2,1)} %param.12, bf16[4,6,24,192]{3,2,1,0:T(8,128)(2,1)} %param.11), kind=kLoop, calls=%fused_computation | loop fusion | flops 884736 | bytes 884736 | tf_op jit(solution)/shard_map/concatenate | solution.py:462
  1.8 0.2 shard_map.122
  2.1 4.5 %collective-permute-start = (bf16[2,112,384]{2,1,0:T(8,128)(2,1)S(1)}, bf16[2,112,384]{2,1,0:T(8,128)(2,1)S(1)}, u32[]{:S(2)}, u32[]{:S(2)}) collective-permute-start(bf16[2,112,384]{2,1,0:T(8,128)(2,1)S(1)} %get-tuple-element.37), channel_id=1, source_target_pairs={{0,28},{1,29},{2,30},{3,31},{4,0},{5,1},{6,2},{7,3},{8,4},{9,5},{1... | collective-permute-start | bytes 516104 | tf_op jit(solution)/shard_map/ppermute | solution.py:447
  6.6 2.4 %collective-permute-start.1 = (bf16[2,48,384]{2,1,0:T(8,128)(2,1)S(1)}, bf16[2,48,384]{2,1,0:T(8,128)(2,1)S(1)}, u32[]{:S(2)}, u32[]{:S(2)}) collective-permute-start(bf16[2,48,384]{2,1,0:T(8,128)(2,1)S(1)} %get-tuple-element.46), channel_id=1, source_target_pairs={{0,3},{1,0},{2,1},{3,2},{4,7},{5,4},{6,5},{7,6},{8,11},{9,8},{10,9... | collective-permute-start | bytes 221192 | tf_op jit(solution)/shard_map/ppermute | solution.py:447
  9.1 0.4 %collective-permute-start.2 = (bf16[2,48,384]{2,1,0:T(8,128)(2,1)S(1)}, bf16[2,48,384]{2,1,0:T(8,128)(2,1)S(1)}, u32[]{:S(2)}, u32[]{:S(2)}) collective-permute-start(bf16[2,48,384]{2,1,0:T(8,128)(2,1)S(1)} %get-tuple-element.47), channel_id=1, source_target_pairs={{0,31},{1,28},{2,29},{3,30},{4,3},{5,0},{6,1},{7,2},{8,7},{9,4},{1... | collective-permute-start | bytes 221192 | tf_op jit(solution)/shard_map/ppermute | solution.py:447
  9.4 0.0 copy-start
  9.4 1.5 %copy-done = f32[2,1,6,144,144]{4,3,2,1,0:T(8,128)S(1)} copy-done((f32[2,1,6,144,144]{4,3,2,1,0:T(8,128)S(1)}, f32[2,1,6,144,144]{4,3,2,1,0:T(8,128)}, u32[]{:S(2)}) %copy-start) | copy-done | bytes 995352
  10.9 0.0 copy-start.1
  10.9 0.0 copy-start.5
  10.9 0.0 copy-start.6
  10.9 0.0 copy-start.8
  10.9 0.6 %shard_map.123.refs_5_.refs_7_ = f32[2,4,144,256]{3,2,1,0:T(8,128)S(1)} custom-call(f32[2,6,144,144]{3,2,1,0:T(8,128)S(1)} %bitcast.3), custom_call_target="tpu_custom_call" | custom-call | tf_op jit(solution)/shard_map/pallas_call | solution.py:429
  11.5 0.0 collective-permute-done.refs_1_
  11.5 0.3 %copy-done.1 = bf16[192,576]{1,0:T(8,128)(2,1)S(1)} copy-done((bf16[192,576]{1,0:T(8,128)(2,1)S(1)}, bf16[192,576]{1,0:T(8,128)(2,1)}, u32[]{:S(2)}) %copy-start.1) | copy-done | bytes 221208
  11.8 0.0 copy-done.5
  11.8 0.1 copy-done.6
  11.9 0.0 copy-done.8
  12.0 0.0 copy-start.7
  12.0 1.4 %shard_map.124 = (f32[288,192]{1,0:T(8,128)S(1)}, f32[288,128]{1,0:T(8,128)S(1)}, bf16[288,192]{1,0:T(8,128)(2,1)S(1)}, f32[288,192]{1,0:T(8,128)S(1)}, f32[288,...) custom-call(bf16[2,144,384]{2,1,0:T(8,128)(2,1)S(1)} %get-tuple-elem, ...), custom_call_target="tpu_custom_call" | custom-call | flops 1000000000 | tf_op jit(solution)/shard_map/pallas_call | solution.py:429
  13.4 0.0 collective-permute-done.1.refs_2_
  13.4 0.0 collective-permute-done.2.refs_3_
  13.4 0.0 copy-done.7
  13.4 0.0 copy-start.2
  13.4 1.4 %shard_map.125 = (f32[288,192]{1,0:T(8,128)S(1)}, f32[288,128]{1,0:T(8,128)S(1)}, bf16[288,192]{1,0:T(8,128)(2,1)S(1)}, f32[288,192]{1,0:T(8,128)S(1)}, f32[288,...) custom-call(bf16[2,48,384]{2,1,0:T(8,128)(2,1)S(1)} %get-tuple-eleme, ...), custom_call_target="tpu_custom_call" | custom-call | flops 1000000000 | tf_op jit(solution)/shard_map/pallas_call | solution.py:429
  14.9 0.0 copy-done.2
  14.9 0.0 copy-start.3
  14.9 1.4 %shard_map.126 = (bf16[2,144,192]{2,1,0:T(8,128)(2,1)S(1)}, bf16[2,144,192]{2,1,0:T(8,128)(2,1)S(1)}, bf16[2,80,192]{2,1,0:T(8,128)(2,1)S(1)}, bf16[504,128]{1,0...) custom-call(f32[288,192]{1,0:T(8,128)S(1)} %get-tuple-element.49.refs_0, ...), custom_call_target="tpu_custom_call" | custom-call | tf_op jit(solution)/shard_map/pallas_call | solution.py:429
  16.3 1.5 %collective-permute-start.3 = (bf16[2,80,192]{2,1,0:T(8,128)(2,1)S(1)}, bf16[2,80,192]{2,1,0:T(8,128)(2,1)S(1)}, u32[]{:S(2)}, u32[]{:S(2)}) collective-permute-start(bf16[2,80,192]{2,1,0:T(8,128)(2,1)S(1)} %get-tuple-element.61), channel_id=1, source_target_pairs={{0,1},{1,2},{2,3},{3,0},{4,5},{5,6},{6,7},{7,4},{8,9},{9,10},{10,1... | collective-permute-start | bytes 184328 | tf_op jit(solution)/shard_map/ppermute | solution.py:447
  17.8 0.5 %collective-permute-start.5 = (bf16[504,128]{1,0:T(8,128)(2,1)S(1)}, bf16[504,128]{1,0:T(8,128)(2,1)S(1)}, u32[]{:S(2)}, u32[]{:S(2)}) collective-permute-start(bf16[504,128]{1,0:T(8,128)(2,1)S(1)} %get-tuple-element.65), channel_id=1, source_target_pairs={{0,1},{1,0},{2,3},{3,2},{4,5},{5,4},{6,7},{7,6},{8,9},{9,8},{10,11... | collective-permute-start | bytes 387080 | tf_op jit(solution)/shard_map/ppermute | solution.py:518
  18.3 1.5 %collective-permute-start.6 = (bf16[504,128]{1,0:T(8,128)(2,1)S(1)}, bf16[504,128]{1,0:T(8,128)(2,1)S(1)}, u32[]{:S(2)}, u32[]{:S(2)}) collective-permute-start(bf16[504,128]{1,0:T(8,128)(2,1)S(1)} %get-tuple-element.66), channel_id=1, source_target_pairs={{0,2},{1,3},{2,0},{3,1},{4,6},{5,7},{6,4},{7,5},{8,10},{9,11},{10,... | collective-permute-start | bytes 387080 | tf_op jit(solution)/shard_map/ppermute | solution.py:518
  19.8 1.5 %collective-permute-start.7 = (bf16[504,128]{1,0:T(8,128)(2,1)S(1)}, bf16[504,128]{1,0:T(8,128)(2,1)S(1)}, u32[]{:S(2)}, u32[]{:S(2)}) collective-permute-start(bf16[504,128]{1,0:T(8,128)(2,1)S(1)} %get-tuple-element.67), channel_id=1, source_target_pairs={{0,3},{1,2},{2,1},{3,0},{4,7},{5,6},{6,5},{7,4},{8,11},{9,10},{10,... | collective-permute-start | bytes 387080 | tf_op jit(solution)/shard_map/ppermute | solution.py:518
  21.3 0.0 copy-done.3
  21.3 0.0 copy-start.4
  21.3 1.4 %shard_map.127 = (bf16[2,144,192]{2,1,0:T(8,128)(2,1)S(1)}, bf16[2,144,192]{2,1,0:T(8,128)(2,1)S(1)}) custom-call(f32[288,192]{1,0:T(8,128)S(1)} %get-tuple-element.38.refs_0_, f32[288,128]{1,0:T(8,128)S(1)} %get-tuple-element.39.refs_1_, bf16[288,192]{1,0:T(8,128)(2,1)S(1)} %get-tuple-element.40.refs_2_, f32[288,192]{1,0:T(8,128)S(1)} %get-tuple-element.41.refs_3_, ...), custom_call_target="tpu_custom_call" | custom-call | tf_op jit(solution)/shard_map/pallas_call | solution.py:429
  22.7 0.0 collective-permute-done.3.side
  22.7 0.0 copy-done.4
  22.7 0.3 shard_map.128
  23.0 0.1 collective-permute-start.4
  23.0 1.2 %collective-permute-done.5.refs_1_ = bf16[504,128]{1,0:T(8,128)(2,1)S(1)} collective-permute-done((bf16[504,128]{1,0:T(8,128)(2,1)S(1)}, bf16[504,128]{1,0:T(8,128)(2,1)S(1)}, u32[]{:S(2)}, u32[]{:S(2)}) %collective-permute-start.5) | collective-permute-done | bytes 129056 | tf_op jit(solution)/shard_map/ppermute | solution.py:518
  24.2 1.0 %collective-permute-done.6.refs_2_ = bf16[504,128]{1,0:T(8,128)(2,1)S(1)} collective-permute-done((bf16[504,128]{1,0:T(8,128)(2,1)S(1)}, bf16[504,128]{1,0:T(8,128)(2,1)S(1)}, u32[]{:S(2)}, u32[]{:S(2)}) %collective-permute-start.6) | collective-permute-done | bytes 129056 | tf_op jit(solution)/shard_map/ppermute | solution.py:518
  25.3 2.1 %collective-permute-done.7.refs_3_ = bf16[504,128]{1,0:T(8,128)(2,1)S(1)} collective-permute-done((bf16[504,128]{1,0:T(8,128)(2,1)S(1)}, bf16[504,128]{1,0:T(8,128)(2,1)S(1)}, u32[]{:S(2)}, u32[]{:S(2)}) %collective-permute-start.7) | collective-permute-done | bytes 129056 | tf_op jit(solution)/shard_map/ppermute | solution.py:518
  27.4 1.1 %shard_map.129 = (f32[432,1,144]{2,1,0:T(1,128)}, f32[8,128]{1,0:T(8,128)S(1)}) custom-call(bf16[504,128]{1,0:T(8,128)(2,1)S(1)} %get-tuple-element.64.refs_0_, bf16[504,128]{1,0:T(8,128)(2,1)S(1)} %collective-permute-done.5.refs_1_, bf16[504,128]{1,0:T(8,128)(2,1)S(1)} %collective-permute-done.6.refs_2_, bf16[504,128]{1,0:T(8,128)(2,1)S(1)} %collective-permute-done.7.refs_3_), custom_call_target="tpu_custom_call" | custom-call | tf_op jit(solution)/shard_map/pallas_call | solution.py:429
  28.5 0.5 %collective-permute-done.4.below = bf16[144,384]{1,0:T(8,128)(2,1)S(1)} collective-permute-done((bf16[144,384]{1,0:T(8,128)(2,1)S(1)}, bf16[144,384]{1,0:T(8,128)(2,1)S(1)}, u32[]{:S(2)}, u32[]{:S(2)}) %collective-permute-start.4) | collective-permute-done | bytes 110624 | tf_op jit(solution)/shard_map/ppermute | solution.py:447
  29.0 0.8 %shard_map.130 = bf16[4,6,24,192]{3,2,1,0:T(8,128)(2,1)} custom-call(bf16[2,144,192]{2,1,0:T(8,128)(2,1)S(1)} %get-tuple-element.62.inner, bf16[144,384]{1,0:T(8,128)(2,1)S(1)} %collective-permute-done.4.below, f32[8,128]{1,0:T(8,128)S(1)} %get-tuple-element.68.after), custom_call_target="tpu_custom_call" | custom-call | tf_op jit(solution)/shard_map/pallas_call | solution.py:429
Async XLA Ops:
  2.1 9.4 %collective-permute-start = (bf16[2,112,384]{2,1,0:T(8,128)(2,1)S(1)}, bf16[2,112,384]{2,1,0:T(8,128)(2,1)S(1)}, u32[]{:S(2)}, u32[]{:S(2)}) collective-permute-start(bf16[2,112,384]{2,1,0:T(8,128)(2,1)S(1)} %get-tuple-element.37), channel_id=1, source_target_pairs={{0,28},{1,29},{2,30},{3,31},{4,0},{5,1},{6,2},{7,3},{8,4},{9,5},{1... | collective-permute-start | bytes 516104 | tf_op jit(solution)/shard_map/ppermute | solution.py:447
  6.6 6.8 %collective-permute-start.1 = (bf16[2,48,384]{2,1,0:T(8,128)(2,1)S(1)}, bf16[2,48,384]{2,1,0:T(8,128)(2,1)S(1)}, u32[]{:S(2)}, u32[]{:S(2)}) collective-permute-start(bf16[2,48,384]{2,1,0:T(8,128)(2,1)S(1)} %get-tuple-element.46), channel_id=1, source_target_pairs={{0,3},{1,0},{2,1},{3,2},{4,7},{5,4},{6,5},{7,6},{8,11},{9,8},{10,9... | collective-permute-start | bytes 221192 | tf_op jit(solution)/shard_map/ppermute | solution.py:447
  9.1 4.3 %collective-permute-start.2 = (bf16[2,48,384]{2,1,0:T(8,128)(2,1)S(1)}, bf16[2,48,384]{2,1,0:T(8,128)(2,1)S(1)}, u32[]{:S(2)}, u32[]{:S(2)}) collective-permute-start(bf16[2,48,384]{2,1,0:T(8,128)(2,1)S(1)} %get-tuple-element.47), channel_id=1, source_target_pairs={{0,31},{1,28},{2,29},{3,30},{4,3},{5,0},{6,1},{7,2},{8,7},{9,4},{1... | collective-permute-start | bytes 221192 | tf_op jit(solution)/shard_map/ppermute | solution.py:447
  9.4 1.5 %copy-start = (f32[2,1,6,144,144]{4,3,2,1,0:T(8,128)S(1)}, f32[2,1,6,144,144]{4,3,2,1,0:T(8,128)}, u32[]{:S(2)}) copy-start(f32[2,1,6,144,144]{4,3,2,1,0:T(8,128)} %param.16) | copy-start | bytes 2985988
  10.9 0.9 %copy-start.1 = (bf16[192,576]{1,0:T(8,128)(2,1)S(1)}, bf16[192,576]{1,0:T(8,128)(2,1)}, u32[]{:S(2)}) copy-start(bf16[192,576]{1,0:T(8,128)(2,1)} %refs_8_.4) | copy-start | bytes 663556
  10.9 0.9 %copy-start.5 = (f32[192]{0:T(256)S(1)}, f32[192]{0:T(256)}, u32[]{:S(2)}) copy-start(f32[192]{0:T(256)} %param.13) | copy-start | bytes 2308
  10.9 1.0 %copy-start.6 = (bf16[192,192]{1,0:T(8,128)(2,1)S(1)}, bf16[192,192]{1,0:T(8,128)(2,1)}, u32[]{:S(2)}) copy-start(bf16[192,192]{1,0:T(8,128)(2,1)} %refs_6_.2) | copy-start | bytes 221188
  10.9 1.1 %copy-start.8 = (bf16[144,256]{1,0:T(8,128)(2,1)S(1)}, bf16[144,256]{1,0:T(8,128)(2,1)}, u32[]{:S(2)}) copy-start(bf16[144,256]{1,0:T(8,128)(2,1)} %constant.10.clone.refs_6_) | copy-start | bytes 221188
  12.0 1.4 %copy-start.7 = (bf16[144,256]{1,0:T(8,128)(2,1)S(1)}, bf16[144,256]{1,0:T(8,128)(2,1)}, u32[]{:S(2)}) copy-start(bf16[144,256]{1,0:T(8,128)(2,1)} %constant.11.clone.refs_8_) | copy-start | bytes 221188
  13.4 1.5 %copy-start.2 = (bf16[368,144]{1,0:T(8,128)(2,1)S(1)}, bf16[368,144]{1,0:T(8,128)(2,1)}, u32[]{:S(2)}) copy-start(bf16[368,144]{1,0:T(8,128)(2,1)} %constant.12.clone.refs_9_) | copy-start | bytes 317956
  14.9 6.4 %copy-start.3 = (bf16[288,144]{1,0:T(8,128)(2,1)S(1)}, bf16[288,144]{1,0:T(8,128)(2,1)}, u32[]{:S(2)}) copy-start(bf16[288,144]{1,0:T(8,128)(2,1)} %constant.13.clone.refs_9_) | copy-start | bytes 248836
  16.3 6.4 %collective-permute-start.3 = (bf16[2,80,192]{2,1,0:T(8,128)(2,1)S(1)}, bf16[2,80,192]{2,1,0:T(8,128)(2,1)S(1)}, u32[]{:S(2)}, u32[]{:S(2)}) collective-permute-start(bf16[2,80,192]{2,1,0:T(8,128)(2,1)S(1)} %get-tuple-element.61), channel_id=1, source_target_pairs={{0,1},{1,2},{2,3},{3,0},{4,5},{5,6},{6,7},{7,4},{8,9},{9,10},{10,1... | collective-permute-start | bytes 184328 | tf_op jit(solution)/shard_map/ppermute | solution.py:447
  17.8 6.4 %collective-permute-start.5 = (bf16[504,128]{1,0:T(8,128)(2,1)S(1)}, bf16[504,128]{1,0:T(8,128)(2,1)S(1)}, u32[]{:S(2)}, u32[]{:S(2)}) collective-permute-start(bf16[504,128]{1,0:T(8,128)(2,1)S(1)} %get-tuple-element.65), channel_id=1, source_target_pairs={{0,1},{1,0},{2,3},{3,2},{4,5},{5,4},{6,7},{7,6},{8,9},{9,8},{10,11... | collective-permute-start | bytes 387080 | tf_op jit(solution)/shard_map/ppermute | solution.py:518
  18.3 7.0 %collective-permute-start.6 = (bf16[504,128]{1,0:T(8,128)(2,1)S(1)}, bf16[504,128]{1,0:T(8,128)(2,1)S(1)}, u32[]{:S(2)}, u32[]{:S(2)}) collective-permute-start(bf16[504,128]{1,0:T(8,128)(2,1)S(1)} %get-tuple-element.66), channel_id=1, source_target_pairs={{0,2},{1,3},{2,0},{3,1},{4,6},{5,7},{6,4},{7,5},{8,10},{9,11},{10,... | collective-permute-start | bytes 387080 | tf_op jit(solution)/shard_map/ppermute | solution.py:518
  19.8 7.6 %collective-permute-start.7 = (bf16[504,128]{1,0:T(8,128)(2,1)S(1)}, bf16[504,128]{1,0:T(8,128)(2,1)S(1)}, u32[]{:S(2)}, u32[]{:S(2)}) collective-permute-start(bf16[504,128]{1,0:T(8,128)(2,1)S(1)} %get-tuple-element.67), channel_id=1, source_target_pairs={{0,3},{1,2},{2,1},{3,0},{4,7},{5,6},{6,5},{7,4},{8,11},{9,10},{10,... | collective-permute-start | bytes 387080 | tf_op jit(solution)/shard_map/ppermute | solution.py:518
  21.3 1.4 %copy-start.4 = (bf16[288,80]{1,0:T(8,128)(2,1)S(1)}, bf16[288,80]{1,0:T(8,128)(2,1)}, u32[]{:S(2)}) copy-start(bf16[288,80]{1,0:T(8,128)(2,1)} %constant.14.clone.order_t) | copy-start | bytes 138244
  23.0 6.0 %collective-permute-start.4 = (bf16[144,384]{1,0:T(8,128)(2,1)S(1)}, bf16[144,384]{1,0:T(8,128)(2,1)S(1)}, u32[]{:S(2)}, u32[]{:S(2)}) collective-permute-start(bf16[144,384]{1,0:T(8,128)(2,1)S(1)} %get-tuple-element.63), channel_id=1, source_target_pairs={{0,4},{1,5},{2,6},{3,7},{4,8},{5,9},{6,10},{7,11},{8,12},{9,13},{1... | collective-permute-start | bytes 331784 | tf_op jit(solution)/shard_map/ppermute | solution.py:447

commit v5 on v4

--- a/solution.py
+++ b/solution.py
@@ -384,26 +384,41 @@
     below[...] = jnp.concatenate(packed, axis=1).astype(BF16)
 
 
-def join_kernel(inner, below, after, grad_input):
-    levels, _, cols, channels = grad_input.shape
-    level_windows = levels // WZ
+def put_rows(level_window, a, rows):
+    levels, many, cols, _ = rows.shape
+    for z in range(WZ):
+        level = (a * WZ + WZ // 2 + z) % levels
+        for row in range(many):
+            at = (z * many + row) * cols
+            rows[level, row] = level_window[at : at + cols].astype(BF16)
+
+
+def upper_kernel(inner, grad_input, done, rows, sem):
+    for a in range(inner.shape[0]):
+        put_rows(inner[a].astype(F32), a, rows)
+    copy = pltpu.make_async_copy(rows, grad_input.at[:, HALF_ROWS:], sem)
+    copy.start()
+    done[...] = jnp.zeros(done.shape, F32)
+    copy.wait()
+
+
+def lower_kernel(below, after, upper, grad_input, rows, sem):
+    level_windows = rows.shape[0] // WZ
+    channels = rows.shape[3]
     whole = below[...].astype(F32)
     for a in range(level_windows):
         rest_at = level_windows * LANES + a * (channels - LANES)
         low = jnp.concatenate(
             [whole[:, a * LANES : (a + 1) * LANES], whole[:, rest_at : rest_at + channels - LANES]], axis=1
         )
-        high = inner[a].astype(F32)
-        for z in range(WZ):
-            level = (a * WZ + WZ // 2 + z) % levels
-            for row in range(HALF_ROWS):
-                at = slice((z * HALF_ROWS + row) * cols, (z * HALF_ROWS + row + 1) * cols)
-                grad_input[level, row] = low[at].astype(BF16)
-                grad_input[level, HALF_ROWS + row] = high[at].astype(BF16)
+        put_rows(low, a, rows)
+    copy = pltpu.make_async_copy(rows, grad_input.at[:, :HALF_ROWS], sem)
+    copy.start()
+    copy.wait()
 
 
 def bias_kernel(chunks, *refs):
-    *arrived, bias_grad, after = refs
+    *arrived, _, bias_grad, after = refs
     after[...] = jnp.zeros(after.shape, F32)
     main, rest, heads = chunks.main, chunks.rest, chunks.heads
     total = arrived[0][...].astype(F32)
@@ -425,12 +440,13 @@
     return [pl.BlockSpec(memory_space=pltpu.VMEM)] * count
 
 
-def call(kernel, outs, args, flops=0, scratch=()):
+def call(kernel, outs, args, flops=0, scratch=(), ins=None, specs=None, aliases=None):
     return pl.pallas_call(
         kernel,
         out_shape=outs,
-        in_specs=vmem(len(args)),
-        out_specs=vmem(len(outs)),
+        in_specs=ins or vmem(len(args)),
+        out_specs=specs or vmem(len(outs)),
+        input_output_aliases=aliases or {},
         scratch_shapes=list(scratch),
         compiler_params=pltpu.CompilerParams(vmem_limit_bytes=40 * 2**20),
         cost_estimate=pl.CostEstimate(flops=flops, bytes_accessed=0, transcendentals=0),
@@ -525,12 +541,26 @@
         (*grads, left, jnp.asarray(side_table.T, BF16)),
     )
     above = shift(g_below, 1, 0)
+    anywhere = [pl.BlockSpec(memory_space=pl.ANY)]
+    rows_scratch = [pltpu.VMEM((levels, HALF_ROWS, cols, channels), BF16), pltpu.SemaphoreType.DMA(())]
+    token = struct((8, LANES), F32)
+    grad_input, done = call(
+        upper_kernel, [struct(tokens.shape, BF16), token], (g_inner,), scratch=rows_scratch, specs=anywhere + vmem(1)
+    )
     bias_grad, after = call(
         functools.partial(bias_kernel, chunks),
-        [struct((level_windows * heads * chunks.size, 1, WT), F32), struct((8, LANES), F32)],
-        arrived,
-    )
-    (grad_input,) = call(join_kernel, [struct(tokens.shape, BF16)], (g_inner, above, after))
+        [struct((level_windows * heads * chunks.size, 1, WT), F32), token],
+        arrived + [done],
+    )
+    (grad_input,) = call(
+        lower_kernel,
+        [struct(tokens.shape, BF16)],
+        (above, after, grad_input),
+        scratch=rows_scratch,
+        ins=vmem(2) + anywhere,
+        specs=anywhere,
+        aliases={2: 0},
+    )
     bias_grad = bias_grad.reshape(level_windows, heads, chunks.size, 1, WT)
     return grad_input, jnp.transpose(bias_grad, (0, 3, 1, 2, 4))
 

time: 30 us -> 29.9 us (level)
  waiting for transfers between devices: 4.89 us -> 4.2 us
  Pallas kernels: 8.5 us -> 9.13 us
    ppermute x3, waiting for transfers between devices: 4.35 us -> 3.67 us  [local(): arrived.append(lax.ppermute(results[3 + d], 'lon', pairs))]
    pallas_call x9 -> x10, Pallas kernels: 8.5 us -> 9.13 us  [call(): pl.pallas_call(kernel, out_shape=outs, in_specs=ins or vmem(len(args)), o...]
  transfers between devices with their start and end apart: 8 -> 8, of which waited for: 4 -> 4; matrix products, arithmetic and copies ran while one was open for 0% -> 0% of each run, Pallas kernels for 16% -> 18%
where the time goes in v5:
time: 29.9 us; the launch traced here: 29.7 us
  starting transfers between devices  12.4 us (41%)
  Pallas kernels  9.13 us (31%)
  waiting for transfers between devices  4.2 us (14%)
  local copies, waits for them, and re-layouts  1.98 us (7%)
  other arithmetic  1.21 us (4%)
  between operations  0.78 us (3%)
    pallas_call x10, Pallas kernels, call(): pl.pallas_call(kernel, out_shape=outs, in_specs=ins or vmem(len(args)), o...  9.13 us
    ppermute x5, starting transfers between devices, shift(): return lax.ppermute(value, ('lat', 'lon'), pairs)  8.95 us
    ppermute x3, waiting for transfers between devices, local(): arrived.append(lax.ppermute(results[3 + d], 'lon', pairs))  3.67 us
    ppermute x3, starting transfers between devices, local(): arrived.append(lax.ppermute(results[3 + d], 'lon', pairs))  3.49 us
    unnamed x18, local copies, waits for them, and re-layouts  1.98 us
    concatenate x1, other arithmetic, local(): both = jnp.concatenate([tokens, cotangent], axis=-1)  1.21 us
  transfers between devices with their start and end apart: 8, of which 4 were waited for; matrix products, arithmetic and copies ran while one was open for 0% of the time, Pallas kernels for 18%

profile of v5, /device:TPU:0, one launch (start us, length us, event | category | flops | bytes accessed | tf_op | source)
XLA Modules:
  0.0 29.7 jit_solution(14011469727394255745)
XLA Ops:
  0.6 1.2 %pad_maximum_fusion.both = bf16[4,6,24,384]{3,2,1,0:T(8,128)(2,1)S(1)} fusion(bf16[4,6,24,192]{3,2,1,0:T(8,128)(2,1)} %param.12, bf16[4,6,24,192]{3,2,1,0:T(8,128)(2,1)} %param.11), kind=kLoop, calls=%fused_computation | loop fusion | flops 884736 | bytes 884736 | tf_op jit(solution)/shard_map/concatenate | solution.py:478
  1.8 0.2 shard_map.122
  2.1 4.5 %collective-permute-start = (bf16[2,112,384]{2,1,0:T(8,128)(2,1)S(1)}, bf16[2,112,384]{2,1,0:T(8,128)(2,1)S(1)}, u32[]{:S(2)}, u32[]{:S(2)}) collective-permute-start(bf16[2,112,384]{2,1,0:T(8,128)(2,1)S(1)} %get-tuple-element.39), channel_id=1, source_target_pairs={{0,28},{1,29},{2,30},{3,31},{4,0},{5,1},{6,2},{7,3},{8,4},{9,5},{1... | collective-permute-start | bytes 516104 | tf_op jit(solution)/shard_map/ppermute | solution.py:463
  6.6 2.4 %collective-permute-start.1 = (bf16[2,48,384]{2,1,0:T(8,128)(2,1)S(1)}, bf16[2,48,384]{2,1,0:T(8,128)(2,1)S(1)}, u32[]{:S(2)}, u32[]{:S(2)}) collective-permute-start(bf16[2,48,384]{2,1,0:T(8,128)(2,1)S(1)} %get-tuple-element.48), channel_id=1, source_target_pairs={{0,3},{1,0},{2,1},{3,2},{4,7},{5,4},{6,5},{7,6},{8,11},{9,8},{10,9... | collective-permute-start | bytes 221192 | tf_op jit(solution)/shard_map/ppermute | solution.py:463
  9.1 0.4 %collective-permute-start.2 = (bf16[2,48,384]{2,1,0:T(8,128)(2,1)S(1)}, bf16[2,48,384]{2,1,0:T(8,128)(2,1)S(1)}, u32[]{:S(2)}, u32[]{:S(2)}) collective-permute-start(bf16[2,48,384]{2,1,0:T(8,128)(2,1)S(1)} %get-tuple-element.49), channel_id=1, source_target_pairs={{0,31},{1,28},{2,29},{3,30},{4,3},{5,0},{6,1},{7,2},{8,7},{9,4},{1... | collective-permute-start | bytes 221192 | tf_op jit(solution)/shard_map/ppermute | solution.py:463
  9.4 0.0 copy-start
  9.4 1.5 %copy-done = f32[2,1,6,144,144]{4,3,2,1,0:T(8,128)S(1)} copy-done((f32[2,1,6,144,144]{4,3,2,1,0:T(8,128)S(1)}, f32[2,1,6,144,144]{4,3,2,1,0:T(8,128)}, u32[]{:S(2)}) %copy-start) | copy-done | bytes 995352
  10.9 0.0 copy-start.1
  10.9 0.0 copy-start.5
  10.9 0.0 copy-start.6
  10.9 0.0 copy-start.8
  10.9 0.6 %shard_map.123.refs_5_.refs_7_ = f32[2,4,144,256]{3,2,1,0:T(8,128)S(1)} custom-call(f32[2,6,144,144]{3,2,1,0:T(8,128)S(1)} %bitcast.3), custom_call_target="tpu_custom_call" | custom-call | tf_op jit(solution)/shard_map/pallas_call | solution.py:444
  11.5 0.0 collective-permute-done.refs_1_
  11.5 0.3 %copy-done.1 = bf16[192,576]{1,0:T(8,128)(2,1)S(1)} copy-done((bf16[192,576]{1,0:T(8,128)(2,1)S(1)}, bf16[192,576]{1,0:T(8,128)(2,1)}, u32[]{:S(2)}) %copy-start.1) | copy-done | bytes 221208
  11.8 0.0 copy-done.5
  11.8 0.1 copy-done.6
  11.9 0.0 copy-done.8
  12.0 0.0 copy-start.7
  12.0 1.4 %shard_map.124 = (f32[288,192]{1,0:T(8,128)S(1)}, f32[288,128]{1,0:T(8,128)S(1)}, bf16[288,192]{1,0:T(8,128)(2,1)S(1)}, f32[288,192]{1,0:T(8,128)S(1)}, f32[288,...) custom-call(bf16[2,144,384]{2,1,0:T(8,128)(2,1)S(1)} %get-tuple-elem, ...), custom_call_target="tpu_custom_call" | custom-call | flops 1000000000 | tf_op jit(solution)/shard_map/pallas_call | solution.py:444
  13.4 0.0 collective-permute-done.1.refs_2_
  13.4 0.0 collective-permute-done.2.refs_3_
  13.4 0.0 copy-done.7
  13.4 0.0 copy-start.2
  13.4 1.4 %shard_map.125 = (f32[288,192]{1,0:T(8,128)S(1)}, f32[288,128]{1,0:T(8,128)S(1)}, bf16[288,192]{1,0:T(8,128)(2,1)S(1)}, f32[288,192]{1,0:T(8,128)S(1)}, f32[288,...) custom-call(bf16[2,48,384]{2,1,0:T(8,128)(2,1)S(1)} %get-tuple-eleme, ...), custom_call_target="tpu_custom_call" | custom-call | flops 1000000000 | tf_op jit(solution)/shard_map/pallas_call | solution.py:444
  14.9 0.0 copy-done.2
  14.9 0.0 copy-start.3
  14.9 1.4 %shard_map.126 = (bf16[2,144,192]{2,1,0:T(8,128)(2,1)S(1)}, bf16[2,144,192]{2,1,0:T(8,128)(2,1)S(1)}, bf16[2,80,192]{2,1,0:T(8,128)(2,1)S(1)}, bf16[504,128]{1,0...) custom-call(f32[288,192]{1,0:T(8,128)S(1)} %get-tuple-element.51.refs_0, ...), custom_call_target="tpu_custom_call" | custom-call | tf_op jit(solution)/shard_map/pallas_call | solution.py:444
  16.3 1.5 %collective-permute-start.3 = (bf16[2,80,192]{2,1,0:T(8,128)(2,1)S(1)}, bf16[2,80,192]{2,1,0:T(8,128)(2,1)S(1)}, u32[]{:S(2)}, u32[]{:S(2)}) collective-permute-start(bf16[2,80,192]{2,1,0:T(8,128)(2,1)S(1)} %get-tuple-element.63), channel_id=1, source_target_pairs={{0,1},{1,2},{2,3},{3,0},{4,5},{5,6},{6,7},{7,4},{8,9},{9,10},{10,1... | collective-permute-start | bytes 184328 | tf_op jit(solution)/shard_map/ppermute | solution.py:463
  17.8 0.5 %collective-permute-start.5 = (bf16[504,128]{1,0:T(8,128)(2,1)S(1)}, bf16[504,128]{1,0:T(8,128)(2,1)S(1)}, u32[]{:S(2)}, u32[]{:S(2)}) collective-permute-start(bf16[504,128]{1,0:T(8,128)(2,1)S(1)} %get-tuple-element.66), channel_id=1, source_target_pairs={{0,1},{1,0},{2,3},{3,2},{4,5},{5,4},{6,7},{7,6},{8,9},{9,8},{10,11... | collective-permute-start | bytes 387080 | tf_op jit(solution)/shard_map/ppermute | solution.py:534
  18.3 1.5 %collective-permute-start.6 = (bf16[504,128]{1,0:T(8,128)(2,1)S(1)}, bf16[504,128]{1,0:T(8,128)(2,1)S(1)}, u32[]{:S(2)}, u32[]{:S(2)}) collective-permute-start(bf16[504,128]{1,0:T(8,128)(2,1)S(1)} %get-tuple-element.67), channel_id=1, source_target_pairs={{0,2},{1,3},{2,0},{3,1},{4,6},{5,7},{6,4},{7,5},{8,10},{9,11},{10,... | collective-permute-start | bytes 387080 | tf_op jit(solution)/shard_map/ppermute | solution.py:534
  19.8 1.5 %collective-permute-start.7 = (bf16[504,128]{1,0:T(8,128)(2,1)S(1)}, bf16[504,128]{1,0:T(8,128)(2,1)S(1)}, u32[]{:S(2)}, u32[]{:S(2)}) collective-permute-start(bf16[504,128]{1,0:T(8,128)(2,1)S(1)} %get-tuple-element.68), channel_id=1, source_target_pairs={{0,3},{1,2},{2,1},{3,0},{4,7},{5,6},{6,5},{7,4},{8,11},{9,10},{10,... | collective-permute-start | bytes 387080 | tf_op jit(solution)/shard_map/ppermute | solution.py:534
  21.3 0.0 copy-done.3
  21.3 0.0 copy-start.4
  21.3 1.4 %shard_map.127 = (bf16[2,144,192]{2,1,0:T(8,128)(2,1)S(1)}, bf16[2,144,192]{2,1,0:T(8,128)(2,1)S(1)}) custom-call(f32[288,192]{1,0:T(8,128)S(1)} %get-tuple-element.40.refs_0_, f32[288,128]{1,0:T(8,128)S(1)} %get-tuple-element.41.refs_1_, bf16[288,192]{1,0:T(8,128)(2,1)S(1)} %get-tuple-element.42.refs_2_, f32[288,192]{1,0:T(8,128)S(1)} %get-tuple-element.43.refs_3_, ...), custom_call_target="tpu_custom_call" | custom-call | tf_op jit(solution)/shard_map/pallas_call | solution.py:444
  22.7 0.0 collective-permute-done.3.side
  22.7 0.0 copy-done.4
  22.7 0.3 shard_map.128
  23.0 0.1 collective-permute-start.4
  23.0 0.7 %shard_map.129 = (bf16[4,6,24,192]{3,2,1,0:T(8,128)(2,1)}, f32[8,128]{1,0:T(8,128)S(1)}) custom-call(bf16[2,144,192]{2,1,0:T(8,128)(2,1)S(1)} %get-tuple-element.69.inner), custom_call_target="tpu_custom_call" | custom-call | tf_op jit(solution)/shard_map/pallas_call | solution.py:444
  23.7 0.5 %collective-permute-done.5.refs_1_ = bf16[504,128]{1,0:T(8,128)(2,1)S(1)} collective-permute-done((bf16[504,128]{1,0:T(8,128)(2,1)S(1)}, bf16[504,128]{1,0:T(8,128)(2,1)S(1)}, u32[]{:S(2)}, u32[]{:S(2)}) %collective-permute-start.5) | collective-permute-done | bytes 129056 | tf_op jit(solution)/shard_map/ppermute | solution.py:534
  24.2 1.0 %collective-permute-done.6.refs_2_ = bf16[504,128]{1,0:T(8,128)(2,1)S(1)} collective-permute-done((bf16[504,128]{1,0:T(8,128)(2,1)S(1)}, bf16[504,128]{1,0:T(8,128)(2,1)S(1)}, u32[]{:S(2)}, u32[]{:S(2)}) %collective-permute-start.6) | collective-permute-done | bytes 129056 | tf_op jit(solution)/shard_map/ppermute | solution.py:534
  25.3 2.1 %collective-permute-done.7.refs_3_ = bf16[504,128]{1,0:T(8,128)(2,1)S(1)} collective-permute-done((bf16[504,128]{1,0:T(8,128)(2,1)S(1)}, bf16[504,128]{1,0:T(8,128)(2,1)S(1)}, u32[]{:S(2)}, u32[]{:S(2)}) %collective-permute-start.7) | collective-permute-done | bytes 129056 | tf_op jit(solution)/shard_map/ppermute | solution.py:534
  27.4 1.1 %shard_map.130 = (f32[432,1,144]{2,1,0:T(1,128)}, f32[8,128]{1,0:T(8,128)S(1)}) custom-call(bf16[504,128]{1,0:T(8,128)(2,1)S(1)} %get-tuple-element.65.refs_0_, bf16[504,128]{1,0:T(8,128)(2,1)S(1)} %collective-permute-done.5.refs_1_, bf16[504,128]{1,0:T(8,128)(2,1)S(1)} %collective-permute-done.6.refs_2_, ...), custom_call_target="tpu_custom_call" | custom-call | tf_op jit(solution)/shard_map/pallas_call | solution.py:444
  28.5 0.5 %collective-permute-done.4.below = bf16[144,384]{1,0:T(8,128)(2,1)S(1)} collective-permute-done((bf16[144,384]{1,0:T(8,128)(2,1)S(1)}, bf16[144,384]{1,0:T(8,128)(2,1)S(1)}, u32[]{:S(2)}, u32[]{:S(2)}) %collective-permute-start.4) | collective-permute-done | bytes 110624 | tf_op jit(solution)/shard_map/ppermute | solution.py:463
  29.0 0.8 %shard_map.131 = bf16[4,6,24,192]{3,2,1,0:T(8,128)(2,1)} custom-call(bf16[144,384]{1,0:T(8,128)(2,1)S(1)} %collective-permute-done.4.below, f32[8,128]{1,0:T(8,128)S(1)} %get-tuple-element.71.after, bf16[4,6,24,192]{3,2,1,0:T(8,128)(2,1)} %get-tuple-element.72.upper), custom_call_target="tpu_custom_call", output_to_operand_aliasing={{}: (2, {})} | custom-call | tf_op jit(solution)/shard_map/pallas_call | solution.py:444
Async XLA Ops:
  2.1 9.4 %collective-permute-start = (bf16[2,112,384]{2,1,0:T(8,128)(2,1)S(1)}, bf16[2,112,384]{2,1,0:T(8,128)(2,1)S(1)}, u32[]{:S(2)}, u32[]{:S(2)}) collective-permute-start(bf16[2,112,384]{2,1,0:T(8,128)(2,1)S(1)} %get-tuple-element.39), channel_id=1, source_target_pairs={{0,28},{1,29},{2,30},{3,31},{4,0},{5,1},{6,2},{7,3},{8,4},{9,5},{1... | collective-permute-start | bytes 516104 | tf_op jit(solution)/shard_map/ppermute | solution.py:463
  6.6 6.8 %collective-permute-start.1 = (bf16[2,48,384]{2,1,0:T(8,128)(2,1)S(1)}, bf16[2,48,384]{2,1,0:T(8,128)(2,1)S(1)}, u32[]{:S(2)}, u32[]{:S(2)}) collective-permute-start(bf16[2,48,384]{2,1,0:T(8,128)(2,1)S(1)} %get-tuple-element.48), channel_id=1, source_target_pairs={{0,3},{1,0},{2,1},{3,2},{4,7},{5,4},{6,5},{7,6},{8,11},{9,8},{10,9... | collective-permute-start | bytes 221192 | tf_op jit(solution)/shard_map/ppermute | solution.py:463
  9.1 4.3 %collective-permute-start.2 = (bf16[2,48,384]{2,1,0:T(8,128)(2,1)S(1)}, bf16[2,48,384]{2,1,0:T(8,128)(2,1)S(1)}, u32[]{:S(2)}, u32[]{:S(2)}) collective-permute-start(bf16[2,48,384]{2,1,0:T(8,128)(2,1)S(1)} %get-tuple-element.49), channel_id=1, source_target_pairs={{0,31},{1,28},{2,29},{3,30},{4,3},{5,0},{6,1},{7,2},{8,7},{9,4},{1... | collective-permute-start | bytes 221192 | tf_op jit(solution)/shard_map/ppermute | solution.py:463
  9.4 1.5 %copy-start = (f32[2,1,6,144,144]{4,3,2,1,0:T(8,128)S(1)}, f32[2,1,6,144,144]{4,3,2,1,0:T(8,128)}, u32[]{:S(2)}) copy-start(f32[2,1,6,144,144]{4,3,2,1,0:T(8,128)} %param.16) | copy-start | bytes 2985988
  10.9 0.9 %copy-start.1 = (bf16[192,576]{1,0:T(8,128)(2,1)S(1)}, bf16[192,576]{1,0:T(8,128)(2,1)}, u32[]{:S(2)}) copy-start(bf16[192,576]{1,0:T(8,128)(2,1)} %refs_8_.4) | copy-start | bytes 663556
  10.9 0.9 %copy-start.5 = (f32[192]{0:T(256)S(1)}, f32[192]{0:T(256)}, u32[]{:S(2)}) copy-start(f32[192]{0:T(256)} %param.13) | copy-start | bytes 2308
  10.9 1.0 %copy-start.6 = (bf16[192,192]{1,0:T(8,128)(2,1)S(1)}, bf16[192,192]{1,0:T(8,128)(2,1)}, u32[]{:S(2)}) copy-start(bf16[192,192]{1,0:T(8,128)(2,1)} %refs_6_.2) | copy-start | bytes 221188
  10.9 1.1 %copy-start.8 = (bf16[144,256]{1,0:T(8,128)(2,1)S(1)}, bf16[144,256]{1,0:T(8,128)(2,1)}, u32[]{:S(2)}) copy-start(bf16[144,256]{1,0:T(8,128)(2,1)} %constant.10.clone.refs_6_) | copy-start | bytes 221188
  12.0 1.4 %copy-start.7 = (bf16[144,256]{1,0:T(8,128)(2,1)S(1)}, bf16[144,256]{1,0:T(8,128)(2,1)}, u32[]{:S(2)}) copy-start(bf16[144,256]{1,0:T(8,128)(2,1)} %constant.11.clone.refs_8_) | copy-start | bytes 221188
  13.4 1.5 %copy-start.2 = (bf16[368,144]{1,0:T(8,128)(2,1)S(1)}, bf16[368,144]{1,0:T(8,128)(2,1)}, u32[]{:S(2)}) copy-start(bf16[368,144]{1,0:T(8,128)(2,1)} %constant.12.clone.refs_9_) | copy-start | bytes 317956
  14.9 6.4 %copy-start.3 = (bf16[288,144]{1,0:T(8,128)(2,1)S(1)}, bf16[288,144]{1,0:T(8,128)(2,1)}, u32[]{:S(2)}) copy-start(bf16[288,144]{1,0:T(8,128)(2,1)} %constant.13.clone.refs_9_) | copy-start | bytes 248836
  16.3 6.4 %collective-permute-start.3 = (bf16[2,80,192]{2,1,0:T(8,128)(2,1)S(1)}, bf16[2,80,192]{2,1,0:T(8,128)(2,1)S(1)}, u32[]{:S(2)}, u32[]{:S(2)}) collective-permute-start(bf16[2,80,192]{2,1,0:T(8,128)(2,1)S(1)} %get-tuple-element.63), channel_id=1, source_target_pairs={{0,1},{1,2},{2,3},{3,0},{4,5},{5,6},{6,7},{7,4},{8,9},{9,10},{10,1... | collective-permute-start | bytes 184328 | tf_op jit(solution)/shard_map/ppermute | solution.py:463
  17.8 6.4 %collective-permute-start.5 = (bf16[504,128]{1,0:T(8,128)(2,1)S(1)}, bf16[504,128]{1,0:T(8,128)(2,1)S(1)}, u32[]{:S(2)}, u32[]{:S(2)}) collective-permute-start(bf16[504,128]{1,0:T(8,128)(2,1)S(1)} %get-tuple-element.66), channel_id=1, source_target_pairs={{0,1},{1,0},{2,3},{3,2},{4,5},{5,4},{6,7},{7,6},{8,9},{9,8},{10,11... | collective-permute-start | bytes 387080 | tf_op jit(solution)/shard_map/ppermute | solution.py:534
  18.3 7.0 %collective-permute-start.6 = (bf16[504,128]{1,0:T(8,128)(2,1)S(1)}, bf16[504,128]{1,0:T(8,128)(2,1)S(1)}, u32[]{:S(2)}, u32[]{:S(2)}) collective-permute-start(bf16[504,128]{1,0:T(8,128)(2,1)S(1)} %get-tuple-element.67), channel_id=1, source_target_pairs={{0,2},{1,3},{2,0},{3,1},{4,6},{5,7},{6,4},{7,5},{8,10},{9,11},{10,... | collective-permute-start | bytes 387080 | tf_op jit(solution)/shard_map/ppermute | solution.py:534
  19.8 7.6 %collective-permute-start.7 = (bf16[504,128]{1,0:T(8,128)(2,1)S(1)}, bf16[504,128]{1,0:T(8,128)(2,1)S(1)}, u32[]{:S(2)}, u32[]{:S(2)}) collective-permute-start(bf16[504,128]{1,0:T(8,128)(2,1)S(1)} %get-tuple-element.68), channel_id=1, source_target_pairs={{0,3},{1,2},{2,1},{3,0},{4,7},{5,6},{6,5},{7,4},{8,11},{9,10},{10,... | collective-permute-start | bytes 387080 | tf_op jit(solution)/shard_map/ppermute | solution.py:534
  21.3 1.4 %copy-start.4 = (bf16[288,80]{1,0:T(8,128)(2,1)S(1)}, bf16[288,80]{1,0:T(8,128)(2,1)}, u32[]{:S(2)}) copy-start(bf16[288,80]{1,0:T(8,128)(2,1)} %constant.14.clone.order_t) | copy-start | bytes 138244
  23.0 6.0 %collective-permute-start.4 = (bf16[144,384]{1,0:T(8,128)(2,1)S(1)}, bf16[144,384]{1,0:T(8,128)(2,1)S(1)}, u32[]{:S(2)}, u32[]{:S(2)}) collective-permute-start(bf16[144,384]{1,0:T(8,128)(2,1)S(1)} %get-tuple-element.64), channel_id=1, source_target_pairs={{0,4},{1,5},{2,6},{3,7},{4,8},{5,9},{6,10},{7,11},{8,12},{9,13},{1... | collective-permute-start | bytes 331784 | tf_op jit(solution)/shard_map/ppermute | solution.py:463

commit v6 on v4

--- a/solution.py
+++ b/solution.py
@@ -513,7 +513,7 @@
             )
             left = shift(results[2], 0, 1)
             arrived = [results[3]]
-            for d in range(1, lon_count):
+            for d in sorted(range(1, lon_count), key=lambda d: -d.bit_count()):
                 pairs = [(i, partner(i, d, lon_count)) for i in range(lon_count)]
                 arrived.append(lax.ppermute(results[3 + d], "lon", pairs))
         else:

time: 30 us -> 30 us (level)
  no operation moved by 1% of the time
where the time goes in v6:
time: 30 us; the launch traced here: 29.8 us
  starting transfers between devices  12.4 us (41%)
  Pallas kernels  8.5 us (28%)
  waiting for transfers between devices  4.89 us (16%)
  local copies, waits for them, and re-layouts  1.98 us (7%)
  other arithmetic  1.21 us (4%)
  between operations  0.77 us (3%)
    ppermute x5, starting transfers between devices, shift(): return lax.ppermute(value, ('lat', 'lon'), pairs)  8.95 us
    pallas_call x9, Pallas kernels, call(): pl.pallas_call(kernel, out_shape=outs, in_specs=vmem(len(args)), out_spec...  8.5 us
    ppermute x3, waiting for transfers between devices, local(): arrived.append(lax.ppermute(results[3 + d], 'lon', pairs))  4.35 us
    ppermute x3, starting transfers between devices, local(): arrived.append(lax.ppermute(results[3 + d], 'lon', pairs))  3.49 us
    unnamed x18, local copies, waits for them, and re-layouts  1.98 us
    concatenate x1, other arithmetic, local(): both = jnp.concatenate([tokens, cotangent], axis=-1)  1.21 us
  transfers between devices with their start and end apart: 8, of which 4 were waited for; matrix products, arithmetic and copies ran while one was open for 0% of the time, Pallas kernels for 16%

profile of v6, /device:TPU:0, one launch (start us, length us, event | category | flops | bytes accessed | tf_op | source)
XLA Modules:
  0.0 29.8 jit_solution(792748090844019457)
XLA Ops:
  0.6 1.2 %pad_maximum_fusion.both = bf16[4,6,24,384]{3,2,1,0:T(8,128)(2,1)S(1)} fusion(bf16[4,6,24,192]{3,2,1,0:T(8,128)(2,1)} %param.12, bf16[4,6,24,192]{3,2,1,0:T(8,128)(2,1)} %param.11), kind=kLoop, calls=%fused_computation | loop fusion | flops 884736 | bytes 884736 | tf_op jit(solution)/shard_map/concatenate | solution.py:462
  1.8 0.2 shard_map.122
  2.1 4.5 %collective-permute-start = (bf16[2,112,384]{2,1,0:T(8,128)(2,1)S(1)}, bf16[2,112,384]{2,1,0:T(8,128)(2,1)S(1)}, u32[]{:S(2)}, u32[]{:S(2)}) collective-permute-start(bf16[2,112,384]{2,1,0:T(8,128)(2,1)S(1)} %get-tuple-element.37), channel_id=1, source_target_pairs={{0,28},{1,29},{2,30},{3,31},{4,0},{5,1},{6,2},{7,3},{8,4},{9,5},{1... | collective-permute-start | bytes 516104 | tf_op jit(solution)/shard_map/ppermute | solution.py:447
  6.6 2.4 %collective-permute-start.1 = (bf16[2,48,384]{2,1,0:T(8,128)(2,1)S(1)}, bf16[2,48,384]{2,1,0:T(8,128)(2,1)S(1)}, u32[]{:S(2)}, u32[]{:S(2)}) collective-permute-start(bf16[2,48,384]{2,1,0:T(8,128)(2,1)S(1)} %get-tuple-element.46), channel_id=1, source_target_pairs={{0,3},{1,0},{2,1},{3,2},{4,7},{5,4},{6,5},{7,6},{8,11},{9,8},{10,9... | collective-permute-start | bytes 221192 | tf_op jit(solution)/shard_map/ppermute | solution.py:447
  9.1 0.4 %collective-permute-start.2 = (bf16[2,48,384]{2,1,0:T(8,128)(2,1)S(1)}, bf16[2,48,384]{2,1,0:T(8,128)(2,1)S(1)}, u32[]{:S(2)}, u32[]{:S(2)}) collective-permute-start(bf16[2,48,384]{2,1,0:T(8,128)(2,1)S(1)} %get-tuple-element.47), channel_id=1, source_target_pairs={{0,31},{1,28},{2,29},{3,30},{4,3},{5,0},{6,1},{7,2},{8,7},{9,4},{1... | collective-permute-start | bytes 221192 | tf_op jit(solution)/shard_map/ppermute | solution.py:447
  9.4 0.0 copy-start
  9.4 1.5 %copy-done = f32[2,1,6,144,144]{4,3,2,1,0:T(8,128)S(1)} copy-done((f32[2,1,6,144,144]{4,3,2,1,0:T(8,128)S(1)}, f32[2,1,6,144,144]{4,3,2,1,0:T(8,128)}, u32[]{:S(2)}) %copy-start) | copy-done | bytes 995352
  10.9 0.0 copy-start.1
  10.9 0.0 copy-start.5
  10.9 0.0 copy-start.6
  10.9 0.0 copy-start.8
  10.9 0.6 %shard_map.123.refs_5_.refs_7_ = f32[2,4,144,256]{3,2,1,0:T(8,128)S(1)} custom-call(f32[2,6,144,144]{3,2,1,0:T(8,128)S(1)} %bitcast.3), custom_call_target="tpu_custom_call" | custom-call | tf_op jit(solution)/shard_map/pallas_call | solution.py:429
  11.5 0.0 collective-permute-done.refs_1_
  11.5 0.3 %copy-done.1 = bf16[192,576]{1,0:T(8,128)(2,1)S(1)} copy-done((bf16[192,576]{1,0:T(8,128)(2,1)S(1)}, bf16[192,576]{1,0:T(8,128)(2,1)}, u32[]{:S(2)}) %copy-start.1) | copy-done | bytes 221208
  11.8 0.0 copy-done.5
  11.8 0.1 copy-done.6
  11.9 0.0 copy-done.8
  12.0 0.0 copy-start.7
  12.0 1.4 %shard_map.124 = (f32[288,192]{1,0:T(8,128)S(1)}, f32[288,128]{1,0:T(8,128)S(1)}, bf16[288,192]{1,0:T(8,128)(2,1)S(1)}, f32[288,192]{1,0:T(8,128)S(1)}, f32[288,...) custom-call(bf16[2,144,384]{2,1,0:T(8,128)(2,1)S(1)} %get-tuple-elem, ...), custom_call_target="tpu_custom_call" | custom-call | flops 1000000000 | tf_op jit(solution)/shard_map/pallas_call | solution.py:429
  13.4 0.0 collective-permute-done.1.refs_2_
  13.4 0.0 collective-permute-done.2.refs_3_
  13.4 0.0 copy-done.7
  13.4 0.0 copy-start.2
  13.4 1.4 %shard_map.125 = (f32[288,192]{1,0:T(8,128)S(1)}, f32[288,128]{1,0:T(8,128)S(1)}, bf16[288,192]{1,0:T(8,128)(2,1)S(1)}, f32[288,192]{1,0:T(8,128)S(1)}, f32[288,...) custom-call(bf16[2,48,384]{2,1,0:T(8,128)(2,1)S(1)} %get-tuple-eleme, ...), custom_call_target="tpu_custom_call" | custom-call | flops 1000000000 | tf_op jit(solution)/shard_map/pallas_call | solution.py:429
  14.9 0.0 copy-done.2
  14.9 0.0 copy-start.3
  14.9 1.4 %shard_map.126 = (bf16[2,144,192]{2,1,0:T(8,128)(2,1)S(1)}, bf16[2,144,192]{2,1,0:T(8,128)(2,1)S(1)}, bf16[2,80,192]{2,1,0:T(8,128)(2,1)S(1)}, bf16[504,128]{1,0...) custom-call(f32[288,192]{1,0:T(8,128)S(1)} %get-tuple-element.49.refs_0, ...), custom_call_target="tpu_custom_call" | custom-call | tf_op jit(solution)/shard_map/pallas_call | solution.py:429
  16.3 1.5 %collective-permute-start.3 = (bf16[2,80,192]{2,1,0:T(8,128)(2,1)S(1)}, bf16[2,80,192]{2,1,0:T(8,128)(2,1)S(1)}, u32[]{:S(2)}, u32[]{:S(2)}) collective-permute-start(bf16[2,80,192]{2,1,0:T(8,128)(2,1)S(1)} %get-tuple-element.61), channel_id=1, source_target_pairs={{0,1},{1,2},{2,3},{3,0},{4,5},{5,6},{6,7},{7,4},{8,9},{9,10},{10,1... | collective-permute-start | bytes 184328 | tf_op jit(solution)/shard_map/ppermute | solution.py:447
  17.8 1.4 %collective-permute-start.5 = (bf16[504,128]{1,0:T(8,128)(2,1)S(1)}, bf16[504,128]{1,0:T(8,128)(2,1)S(1)}, u32[]{:S(2)}, u32[]{:S(2)}) collective-permute-start(bf16[504,128]{1,0:T(8,128)(2,1)S(1)} %get-tuple-element.65), channel_id=1, source_target_pairs={{0,3},{1,2},{2,1},{3,0},{4,7},{5,6},{6,5},{7,4},{8,11},{9,10},{10,... | collective-permute-start | bytes 387080 | tf_op jit(solution)/shard_map/ppermute | solution.py:518
  19.2 0.8 %collective-permute-start.6 = (bf16[504,128]{1,0:T(8,128)(2,1)S(1)}, bf16[504,128]{1,0:T(8,128)(2,1)S(1)}, u32[]{:S(2)}, u32[]{:S(2)}) collective-permute-start(bf16[504,128]{1,0:T(8,128)(2,1)S(1)} %get-tuple-element.66), channel_id=1, source_target_pairs={{0,1},{1,0},{2,3},{3,2},{4,5},{5,4},{6,7},{7,6},{8,9},{9,8},{10,11... | collective-permute-start | bytes 387080 | tf_op jit(solution)/shard_map/ppermute | solution.py:518
  20.0 1.3 %collective-permute-start.7 = (bf16[504,128]{1,0:T(8,128)(2,1)S(1)}, bf16[504,128]{1,0:T(8,128)(2,1)S(1)}, u32[]{:S(2)}, u32[]{:S(2)}) collective-permute-start(bf16[504,128]{1,0:T(8,128)(2,1)S(1)} %get-tuple-element.67), channel_id=1, source_target_pairs={{0,2},{1,3},{2,0},{3,1},{4,6},{5,7},{6,4},{7,5},{8,10},{9,11},{10,... | collective-permute-start | bytes 387080 | tf_op jit(solution)/shard_map/ppermute | solution.py:518
  21.3 0.0 copy-done.3
  21.3 0.0 copy-start.4
  21.3 1.4 %shard_map.127 = (bf16[2,144,192]{2,1,0:T(8,128)(2,1)S(1)}, bf16[2,144,192]{2,1,0:T(8,128)(2,1)S(1)}) custom-call(f32[288,192]{1,0:T(8,128)S(1)} %get-tuple-element.38.refs_0_, f32[288,128]{1,0:T(8,128)S(1)} %get-tuple-element.39.refs_1_, bf16[288,192]{1,0:T(8,128)(2,1)S(1)} %get-tuple-element.40.refs_2_, f32[288,192]{1,0:T(8,128)S(1)} %get-tuple-element.41.refs_3_, ...), custom_call_target="tpu_custom_call" | custom-call | tf_op jit(solution)/shard_map/pallas_call | solution.py:429
  22.7 0.0 collective-permute-done.3.side
  22.7 0.0 copy-done.4
  22.7 0.3 shard_map.128
  23.0 0.1 collective-permute-start.4
  23.0 2.2 %collective-permute-done.5.refs_1_ = bf16[504,128]{1,0:T(8,128)(2,1)S(1)} collective-permute-done((bf16[504,128]{1,0:T(8,128)(2,1)S(1)}, bf16[504,128]{1,0:T(8,128)(2,1)S(1)}, u32[]{:S(2)}, u32[]{:S(2)}) %collective-permute-start.5) | collective-permute-done | bytes 129056 | tf_op jit(solution)/shard_map/ppermute | solution.py:518
  25.2 1.2 %collective-permute-done.6.refs_2_ = bf16[504,128]{1,0:T(8,128)(2,1)S(1)} collective-permute-done((bf16[504,128]{1,0:T(8,128)(2,1)S(1)}, bf16[504,128]{1,0:T(8,128)(2,1)S(1)}, u32[]{:S(2)}, u32[]{:S(2)}) %collective-permute-start.6) | collective-permute-done | bytes 129056 | tf_op jit(solution)/shard_map/ppermute | solution.py:518
  26.4 1.0 %collective-permute-done.7.refs_3_ = bf16[504,128]{1,0:T(8,128)(2,1)S(1)} collective-permute-done((bf16[504,128]{1,0:T(8,128)(2,1)S(1)}, bf16[504,128]{1,0:T(8,128)(2,1)S(1)}, u32[]{:S(2)}, u32[]{:S(2)}) %collective-permute-start.7) | collective-permute-done | bytes 129056 | tf_op jit(solution)/shard_map/ppermute | solution.py:518
  27.4 1.1 %shard_map.129 = (f32[432,1,144]{2,1,0:T(1,128)}, f32[8,128]{1,0:T(8,128)S(1)}) custom-call(bf16[504,128]{1,0:T(8,128)(2,1)S(1)} %get-tuple-element.64.refs_0_, bf16[504,128]{1,0:T(8,128)(2,1)S(1)} %collective-permute-done.5.refs_1_, bf16[504,128]{1,0:T(8,128)(2,1)S(1)} %collective-permute-done.6.refs_2_, bf16[504,128]{1,0:T(8,128)(2,1)S(1)} %collective-permute-done.7.refs_3_), custom_call_target="tpu_custom_call" | custom-call | tf_op jit(solution)/shard_map/pallas_call | solution.py:429
  28.5 0.5 %collective-permute-done.4.below = bf16[144,384]{1,0:T(8,128)(2,1)S(1)} collective-permute-done((bf16[144,384]{1,0:T(8,128)(2,1)S(1)}, bf16[144,384]{1,0:T(8,128)(2,1)S(1)}, u32[]{:S(2)}, u32[]{:S(2)}) %collective-permute-start.4) | collective-permute-done | bytes 110624 | tf_op jit(solution)/shard_map/ppermute | solution.py:447
  29.0 0.8 %shard_map.130 = bf16[4,6,24,192]{3,2,1,0:T(8,128)(2,1)} custom-call(bf16[2,144,192]{2,1,0:T(8,128)(2,1)S(1)} %get-tuple-element.62.inner, bf16[144,384]{1,0:T(8,128)(2,1)S(1)} %collective-permute-done.4.below, f32[8,128]{1,0:T(8,128)S(1)} %get-tuple-element.68.after), custom_call_target="tpu_custom_call" | custom-call | tf_op jit(solution)/shard_map/pallas_call | solution.py:429
Async XLA Ops:
  2.1 9.4 %collective-permute-start = (bf16[2,112,384]{2,1,0:T(8,128)(2,1)S(1)}, bf16[2,112,384]{2,1,0:T(8,128)(2,1)S(1)}, u32[]{:S(2)}, u32[]{:S(2)}) collective-permute-start(bf16[2,112,384]{2,1,0:T(8,128)(2,1)S(1)} %get-tuple-element.37), channel_id=1, source_target_pairs={{0,28},{1,29},{2,30},{3,31},{4,0},{5,1},{6,2},{7,3},{8,4},{9,5},{1... | collective-permute-start | bytes 516104 | tf_op jit(solution)/shard_map/ppermute | solution.py:447
  6.6 6.8 %collective-permute-start.1 = (bf16[2,48,384]{2,1,0:T(8,128)(2,1)S(1)}, bf16[2,48,384]{2,1,0:T(8,128)(2,1)S(1)}, u32[]{:S(2)}, u32[]{:S(2)}) collective-permute-start(bf16[2,48,384]{2,1,0:T(8,128)(2,1)S(1)} %get-tuple-element.46), channel_id=1, source_target_pairs={{0,3},{1,0},{2,1},{3,2},{4,7},{5,4},{6,5},{7,6},{8,11},{9,8},{10,9... | collective-permute-start | bytes 221192 | tf_op jit(solution)/shard_map/ppermute | solution.py:447
  9.1 4.3 %collective-permute-start.2 = (bf16[2,48,384]{2,1,0:T(8,128)(2,1)S(1)}, bf16[2,48,384]{2,1,0:T(8,128)(2,1)S(1)}, u32[]{:S(2)}, u32[]{:S(2)}) collective-permute-start(bf16[2,48,384]{2,1,0:T(8,128)(2,1)S(1)} %get-tuple-element.47), channel_id=1, source_target_pairs={{0,31},{1,28},{2,29},{3,30},{4,3},{5,0},{6,1},{7,2},{8,7},{9,4},{1... | collective-permute-start | bytes 221192 | tf_op jit(solution)/shard_map/ppermute | solution.py:447
  9.4 1.5 %copy-start = (f32[2,1,6,144,144]{4,3,2,1,0:T(8,128)S(1)}, f32[2,1,6,144,144]{4,3,2,1,0:T(8,128)}, u32[]{:S(2)}) copy-start(f32[2,1,6,144,144]{4,3,2,1,0:T(8,128)} %param.16) | copy-start | bytes 2985988
  10.9 0.9 %copy-start.1 = (bf16[192,576]{1,0:T(8,128)(2,1)S(1)}, bf16[192,576]{1,0:T(8,128)(2,1)}, u32[]{:S(2)}) copy-start(bf16[192,576]{1,0:T(8,128)(2,1)} %refs_8_.4) | copy-start | bytes 663556
  10.9 0.9 %copy-start.5 = (f32[192]{0:T(256)S(1)}, f32[192]{0:T(256)}, u32[]{:S(2)}) copy-start(f32[192]{0:T(256)} %param.13) | copy-start | bytes 2308
  10.9 1.0 %copy-start.6 = (bf16[192,192]{1,0:T(8,128)(2,1)S(1)}, bf16[192,192]{1,0:T(8,128)(2,1)}, u32[]{:S(2)}) copy-start(bf16[192,192]{1,0:T(8,128)(2,1)} %refs_6_.2) | copy-start | bytes 221188
  10.9 1.1 %copy-start.8 = (bf16[144,256]{1,0:T(8,128)(2,1)S(1)}, bf16[144,256]{1,0:T(8,128)(2,1)}, u32[]{:S(2)}) copy-start(bf16[144,256]{1,0:T(8,128)(2,1)} %constant.10.clone.refs_6_) | copy-start | bytes 221188
  12.0 1.4 %copy-start.7 = (bf16[144,256]{1,0:T(8,128)(2,1)S(1)}, bf16[144,256]{1,0:T(8,128)(2,1)}, u32[]{:S(2)}) copy-start(bf16[144,256]{1,0:T(8,128)(2,1)} %constant.11.clone.refs_8_) | copy-start | bytes 221188
  13.4 1.5 %copy-start.2 = (bf16[368,144]{1,0:T(8,128)(2,1)S(1)}, bf16[368,144]{1,0:T(8,128)(2,1)}, u32[]{:S(2)}) copy-start(bf16[368,144]{1,0:T(8,128)(2,1)} %constant.12.clone.refs_9_) | copy-start | bytes 317956
  14.9 6.4 %copy-start.3 = (bf16[288,144]{1,0:T(8,128)(2,1)S(1)}, bf16[288,144]{1,0:T(8,128)(2,1)}, u32[]{:S(2)}) copy-start(bf16[288,144]{1,0:T(8,128)(2,1)} %constant.13.clone.refs_9_) | copy-start | bytes 248836
  16.3 6.4 %collective-permute-start.3 = (bf16[2,80,192]{2,1,0:T(8,128)(2,1)S(1)}, bf16[2,80,192]{2,1,0:T(8,128)(2,1)S(1)}, u32[]{:S(2)}, u32[]{:S(2)}) collective-permute-start(bf16[2,80,192]{2,1,0:T(8,128)(2,1)S(1)} %get-tuple-element.61), channel_id=1, source_target_pairs={{0,1},{1,2},{2,3},{3,0},{4,5},{5,6},{6,7},{7,4},{8,9},{9,10},{10,1... | collective-permute-start | bytes 184328 | tf_op jit(solution)/shard_map/ppermute | solution.py:447
  17.8 7.4 %collective-permute-start.5 = (bf16[504,128]{1,0:T(8,128)(2,1)S(1)}, bf16[504,128]{1,0:T(8,128)(2,1)S(1)}, u32[]{:S(2)}, u32[]{:S(2)}) collective-permute-start(bf16[504,128]{1,0:T(8,128)(2,1)S(1)} %get-tuple-element.65), channel_id=1, source_target_pairs={{0,3},{1,2},{2,1},{3,0},{4,7},{5,6},{6,5},{7,4},{8,11},{9,10},{10,... | collective-permute-start | bytes 387080 | tf_op jit(solution)/shard_map/ppermute | solution.py:518
  19.2 7.2 %collective-permute-start.6 = (bf16[504,128]{1,0:T(8,128)(2,1)S(1)}, bf16[504,128]{1,0:T(8,128)(2,1)S(1)}, u32[]{:S(2)}, u32[]{:S(2)}) collective-permute-start(bf16[504,128]{1,0:T(8,128)(2,1)S(1)} %get-tuple-element.66), channel_id=1, source_target_pairs={{0,1},{1,0},{2,3},{3,2},{4,5},{5,4},{6,7},{7,6},{8,9},{9,8},{10,11... | collective-permute-start | bytes 387080 | tf_op jit(solution)/shard_map/ppermute | solution.py:518
  20.0 7.4 %collective-permute-start.7 = (bf16[504,128]{1,0:T(8,128)(2,1)S(1)}, bf16[504,128]{1,0:T(8,128)(2,1)S(1)}, u32[]{:S(2)}, u32[]{:S(2)}) collective-permute-start(bf16[504,128]{1,0:T(8,128)(2,1)S(1)} %get-tuple-element.67), channel_id=1, source_target_pairs={{0,2},{1,3},{2,0},{3,1},{4,6},{5,7},{6,4},{7,5},{8,10},{9,11},{10,... | collective-permute-start | bytes 387080 | tf_op jit(solution)/shard_map/ppermute | solution.py:518
  21.3 1.4 %copy-start.4 = (bf16[288,80]{1,0:T(8,128)(2,1)S(1)}, bf16[288,80]{1,0:T(8,128)(2,1)}, u32[]{:S(2)}) copy-start(bf16[288,80]{1,0:T(8,128)(2,1)} %constant.14.clone.order_t) | copy-start | bytes 138244
  23.0 6.0 %collective-permute-start.4 = (bf16[144,384]{1,0:T(8,128)(2,1)S(1)}, bf16[144,384]{1,0:T(8,128)(2,1)S(1)}, u32[]{:S(2)}, u32[]{:S(2)}) collective-permute-start(bf16[144,384]{1,0:T(8,128)(2,1)S(1)} %get-tuple-element.63), channel_id=1, source_target_pairs={{0,4},{1,5},{2,6},{3,7},{4,8},{5,9},{6,10},{7,11},{8,12},{9,13},{1... | collective-permute-start | bytes 331784 | tf_op jit(solution)/shard_map/ppermute | solution.py:447

commit v7 on v4

--- a/solution.py
+++ b/solution.py
@@ -373,6 +373,14 @@
     tokens_kernel(chunks, True, *ins, inner, below, side)
 
 
+def last_kernel(chunks, near, *refs):
+    many = near + 6
+    ins, order, refs = refs[:many], refs[many], refs[many + 1 :]
+    outs, kept = refs[: 3 + chunks.parts], refs[3 + chunks.parts :]
+    scores_kernel(chunks, near, False, True, *ins, *kept)
+    first_kernel(chunks, *kept[:7], ins[near], ins[near + 1], order, kept[7], *outs)
+
+
 def merge_kernel(inner_in, below_in, side, order_t, inner, below):
     half = inner.shape[1]
     lows = []
@@ -482,8 +490,7 @@
         pieces = (tail, below, right, corner) if last else (inner, below)
         sums = [struct((level_windows, lon_count, WT, chunks.width), F32)]
         order = jnp.asarray(window_order(cols, c, False), BF16)
-        results = call(
-            functools.partial(scores_kernel, chunks, len(pieces), c == 0, last),
+        kept = (
             [
                 struct((level_windows * WT, channels), F32),
                 struct((level_windows * WT, LANES), F32),
@@ -493,9 +500,13 @@
                 struct((level_windows, WT, lon_count * chunks.width), BF16),
                 struct((level_windows, WT, lon_count * chunks.width), BF16),
             ]
-            + sums,
-            (*pieces, gain, inproj_weight, outproj_weight, bias_t, order, *total),
-            flops=10**9,
+            + sums
+        )
+        ins = (*pieces, gain, inproj_weight, outproj_weight, bias_t, order, *total)
+        if last:
+            break
+        results = call(
+            functools.partial(scores_kernel, chunks, len(pieces), c == 0, last), kept, ins, flops=10**9
         )
         per_window.append(results[:7])
         total = results[7:]
@@ -503,13 +514,13 @@
     grads = []
     for c in reversed(range(windows)):
         order = jnp.asarray(window_order(cols, c, True).T, BF16)
-        ins = (*per_window[c], gain, inproj_weight, order)
         if c == windows - 1:
             results = call(
-                functools.partial(first_kernel, chunks),
+                functools.partial(last_kernel, chunks, len(pieces)),
                 [wide, wide, struct((level_windows, side_table.shape[0], channels), BF16)]
                 + [struct((packed, LANES), BF16)] * lon_count,
-                (*ins, *total),
+                (*ins, order),
+                scratch=[pltpu.VMEM(part.shape, part.dtype) for part in kept],
             )
             left = shift(results[2], 0, 1)
             arrived = [results[3]]
@@ -517,6 +528,7 @@
                 pairs = [(i, partner(i, d, lon_count)) for i in range(lon_count)]
                 arrived.append(lax.ppermute(results[3 + d], "lon", pairs))
         else:
+            ins = (*per_window[c], gain, inproj_weight, order)
             results = call(functools.partial(tokens_kernel, chunks, False), [wide] * 2, (*ins, *grads))
         grads = results[:2]
     g_inner, g_below = call(

time: 30 us -> 29.7 us (0.990)
    pallas_call x9 -> x8, Pallas kernels: 8.5 us -> 8.27 us  [call(): pl.pallas_call(kernel, out_shape=outs, in_specs=vmem(len(args)), out_spec...]
where the time goes in v7:
time: 29.7 us; the launch traced here: 29.5 us
  starting transfers between devices  12.4 us (42%)
  Pallas kernels  8.27 us (28%)
  waiting for transfers between devices  4.89 us (16%)
  local copies, waits for them, and re-layouts  1.97 us (7%)
  other arithmetic  1.21 us (4%)
  between operations  0.76 us (3%)
    ppermute x5, starting transfers between devices, shift(): return lax.ppermute(value, ('lat', 'lon'), pairs)  8.96 us
    pallas_call x8, Pallas kernels, call(): pl.pallas_call(kernel, out_shape=outs, in_specs=vmem(len(args)), out_spec...  8.27 us
    ppermute x3, waiting for transfers between devices, local(): arrived.append(lax.ppermute(results[3 + d], 'lon', pairs))  4.33 us
    ppermute x3, starting transfers between devices, local(): arrived.append(lax.ppermute(results[3 + d], 'lon', pairs))  3.49 us
    unnamed x18, local copies, waits for them, and re-layouts  1.97 us
    concatenate x1, other arithmetic, local(): both = jnp.concatenate([tokens, cotangent], axis=-1)  1.21 us
  transfers between devices with their start and end apart: 8, of which 4 were waited for; matrix products, arithmetic and copies ran while one was open for 0% of the time, Pallas kernels for 16%

profile of v7, /device:TPU:0, one launch (start us, length us, event | category | flops | bytes accessed | tf_op | source)
XLA Modules:
  0.0 29.5 jit_solution(15616675520182784944)
XLA Ops:
  0.6 1.2 %pad_maximum_fusion.both = bf16[4,6,24,384]{3,2,1,0:T(8,128)(2,1)S(1)} fusion(bf16[4,6,24,192]{3,2,1,0:T(8,128)(2,1)} %param.12, bf16[4,6,24,192]{3,2,1,0:T(8,128)(2,1)} %param.11), kind=kLoop, calls=%fused_computation | loop fusion | flops 884736 | bytes 884736 | tf_op jit(solution)/shard_map/concatenate | solution.py:470
  1.8 0.2 shard_map.122
  2.1 4.5 %collective-permute-start = (bf16[2,112,384]{2,1,0:T(8,128)(2,1)S(1)}, bf16[2,112,384]{2,1,0:T(8,128)(2,1)S(1)}, u32[]{:S(2)}, u32[]{:S(2)}) collective-permute-start(bf16[2,112,384]{2,1,0:T(8,128)(2,1)S(1)} %get-tuple-element.29), channel_id=1, source_target_pairs={{0,28},{1,29},{2,30},{3,31},{4,0},{5,1},{6,2},{7,3},{8,4},{9,5},{1... | collective-permute-start | bytes 516104 | tf_op jit(solution)/shard_map/ppermute | solution.py:455
  6.6 2.4 %collective-permute-start.1 = (bf16[2,48,384]{2,1,0:T(8,128)(2,1)S(1)}, bf16[2,48,384]{2,1,0:T(8,128)(2,1)S(1)}, u32[]{:S(2)}, u32[]{:S(2)}) collective-permute-start(bf16[2,48,384]{2,1,0:T(8,128)(2,1)S(1)} %get-tuple-element.38), channel_id=1, source_target_pairs={{0,3},{1,0},{2,1},{3,2},{4,7},{5,4},{6,5},{7,6},{8,11},{9,8},{10,9... | collective-permute-start | bytes 221192 | tf_op jit(solution)/shard_map/ppermute | solution.py:455
  9.1 0.4 %collective-permute-start.2 = (bf16[2,48,384]{2,1,0:T(8,128)(2,1)S(1)}, bf16[2,48,384]{2,1,0:T(8,128)(2,1)S(1)}, u32[]{:S(2)}, u32[]{:S(2)}) collective-permute-start(bf16[2,48,384]{2,1,0:T(8,128)(2,1)S(1)} %get-tuple-element.39), channel_id=1, source_target_pairs={{0,31},{1,28},{2,29},{3,30},{4,3},{5,0},{6,1},{7,2},{8,7},{9,4},{1... | collective-permute-start | bytes 221192 | tf_op jit(solution)/shard_map/ppermute | solution.py:455
  9.4 0.0 copy-start
  9.4 1.5 %copy-done = f32[2,1,6,144,144]{4,3,2,1,0:T(8,128)S(1)} copy-done((f32[2,1,6,144,144]{4,3,2,1,0:T(8,128)S(1)}, f32[2,1,6,144,144]{4,3,2,1,0:T(8,128)}, u32[]{:S(2)}) %copy-start) | copy-done | bytes 995352
  10.9 0.0 copy-start.1
  10.9 0.0 copy-start.4
  10.9 0.0 copy-start.7
  10.9 0.0 copy-start.8
  10.9 0.6 %shard_map.123.refs_5_.refs_7_ = f32[2,4,144,256]{3,2,1,0:T(8,128)S(1)} custom-call(f32[2,6,144,144]{3,2,1,0:T(8,128)S(1)} %bitcast.3), custom_call_target="tpu_custom_call" | custom-call | tf_op jit(solution)/shard_map/pallas_call | solution.py:437
  11.5 0.0 collective-permute-done.refs_1_
  11.5 0.3 %copy-done.1 = bf16[192,576]{1,0:T(8,128)(2,1)S(1)} copy-done((bf16[192,576]{1,0:T(8,128)(2,1)S(1)}, bf16[192,576]{1,0:T(8,128)(2,1)}, u32[]{:S(2)}) %copy-start.1) | copy-done | bytes 221208
  11.8 0.1 copy-done.4
  11.9 0.0 copy-done.7
  11.9 0.1 copy-done.8
  12.0 0.0 copy-start.2
  12.0 0.0 copy-start.5
  12.0 1.4 %shard_map.124 = (f32[288,192]{1,0:T(8,128)S(1)}, f32[288,128]{1,0:T(8,128)S(1)}, bf16[288,192]{1,0:T(8,128)(2,1)S(1)}, f32[288,192]{1,0:T(8,128)S(1)}, f32[288,...) custom-call(bf16[2,144,384]{2,1,0:T(8,128)(2,1)S(1)} %get-tuple-elem, ...), custom_call_target="tpu_custom_call" | custom-call | flops 1000000000 | tf_op jit(solution)/shard_map/pallas_call | solution.py:437
  13.4 0.0 collective-permute-done.1.refs_2_
  13.4 0.0 collective-permute-done.2.refs_3_
  13.4 0.0 copy-done.2
  13.4 0.0 copy-done.5
  13.4 0.0 copy-start.3
  13.4 2.6 %shard_map.125 = (bf16[2,144,192]{2,1,0:T(8,128)(2,1)S(1)}, bf16[2,144,192]{2,1,0:T(8,128)(2,1)S(1)}, bf16[2,80,192]{2,1,0:T(8,128)(2,1)S(1)}, bf16[504,128]{1,0...) custom-call(bf16[2,48,384]{2,1,0:T(8,128)(2,1)S(1)} %get-tuple-element., ...), custom_call_target="tpu_custom_call" | custom-call | tf_op jit(solution)/shard_map/pallas_call | solution.py:437
  16.0 1.5 %collective-permute-start.3 = (bf16[2,80,192]{2,1,0:T(8,128)(2,1)S(1)}, bf16[2,80,192]{2,1,0:T(8,128)(2,1)S(1)}, u32[]{:S(2)}, u32[]{:S(2)}) collective-permute-start(bf16[2,80,192]{2,1,0:T(8,128)(2,1)S(1)} %get-tuple-element.45), channel_id=1, source_target_pairs={{0,1},{1,2},{2,3},{3,0},{4,5},{5,6},{6,7},{7,4},{8,9},{9,10},{10,1... | collective-permute-start | bytes 184328 | tf_op jit(solution)/shard_map/ppermute | solution.py:455
  17.6 0.5 %collective-permute-start.5 = (bf16[504,128]{1,0:T(8,128)(2,1)S(1)}, bf16[504,128]{1,0:T(8,128)(2,1)S(1)}, u32[]{:S(2)}, u32[]{:S(2)}) collective-permute-start(bf16[504,128]{1,0:T(8,128)(2,1)S(1)} %get-tuple-element.49), channel_id=1, source_target_pairs={{0,1},{1,0},{2,3},{3,2},{4,5},{5,4},{6,7},{7,6},{8,9},{9,8},{10,11... | collective-permute-start | bytes 387080 | tf_op jit(solution)/shard_map/ppermute | solution.py:529
  18.0 1.5 %collective-permute-start.6 = (bf16[504,128]{1,0:T(8,128)(2,1)S(1)}, bf16[504,128]{1,0:T(8,128)(2,1)S(1)}, u32[]{:S(2)}, u32[]{:S(2)}) collective-permute-start(bf16[504,128]{1,0:T(8,128)(2,1)S(1)} %get-tuple-element.50), channel_id=1, source_target_pairs={{0,2},{1,3},{2,0},{3,1},{4,6},{5,7},{6,4},{7,5},{8,10},{9,11},{10,... | collective-permute-start | bytes 387080 | tf_op jit(solution)/shard_map/ppermute | solution.py:529
  19.6 1.5 %collective-permute-start.7 = (bf16[504,128]{1,0:T(8,128)(2,1)S(1)}, bf16[504,128]{1,0:T(8,128)(2,1)S(1)}, u32[]{:S(2)}, u32[]{:S(2)}) collective-permute-start(bf16[504,128]{1,0:T(8,128)(2,1)S(1)} %get-tuple-element.51), channel_id=1, source_target_pairs={{0,3},{1,2},{2,1},{3,0},{4,7},{5,6},{6,5},{7,4},{8,11},{9,10},{10,... | collective-permute-start | bytes 387080 | tf_op jit(solution)/shard_map/ppermute | solution.py:529
  21.0 0.0 copy-done.3
  21.1 0.0 copy-start.6
  21.1 1.4 %shard_map.126 = (bf16[2,144,192]{2,1,0:T(8,128)(2,1)S(1)}, bf16[2,144,192]{2,1,0:T(8,128)(2,1)S(1)}) custom-call(f32[288,192]{1,0:T(8,128)S(1)} %get-tuple-element.30.refs_0_, f32[288,128]{1,0:T(8,128)S(1)} %get-tuple-element.31.refs_1_, bf16[288,192]{1,0:T(8,128)(2,1)S(1)} %get-tuple-element.32.refs_2_, f32[288,192]{1,0:T(8,128)S(1)} %get-tuple-element.33.refs_3_, ...), custom_call_target="tpu_custom_call" | custom-call | tf_op jit(solution)/shard_map/pallas_call | solution.py:437
  22.4 0.0 collective-permute-done.3.side
  22.4 0.0 copy-done.6
  22.4 0.3 shard_map.127
  22.7 0.1 collective-permute-start.4
  22.8 1.2 %collective-permute-done.5.refs_1_ = bf16[504,128]{1,0:T(8,128)(2,1)S(1)} collective-permute-done((bf16[504,128]{1,0:T(8,128)(2,1)S(1)}, bf16[504,128]{1,0:T(8,128)(2,1)S(1)}, u32[]{:S(2)}, u32[]{:S(2)}) %collective-permute-start.5) | collective-permute-done | bytes 129056 | tf_op jit(solution)/shard_map/ppermute | solution.py:529
  23.9 1.1 %collective-permute-done.6.refs_2_ = bf16[504,128]{1,0:T(8,128)(2,1)S(1)} collective-permute-done((bf16[504,128]{1,0:T(8,128)(2,1)S(1)}, bf16[504,128]{1,0:T(8,128)(2,1)S(1)}, u32[]{:S(2)}, u32[]{:S(2)}) %collective-permute-start.6) | collective-permute-done | bytes 129056 | tf_op jit(solution)/shard_map/ppermute | solution.py:529
  25.0 2.1 %collective-permute-done.7.refs_3_ = bf16[504,128]{1,0:T(8,128)(2,1)S(1)} collective-permute-done((bf16[504,128]{1,0:T(8,128)(2,1)S(1)}, bf16[504,128]{1,0:T(8,128)(2,1)S(1)}, u32[]{:S(2)}, u32[]{:S(2)}) %collective-permute-start.7) | collective-permute-done | bytes 129056 | tf_op jit(solution)/shard_map/ppermute | solution.py:529
  27.1 1.1 %shard_map.128 = (f32[432,1,144]{2,1,0:T(1,128)}, f32[8,128]{1,0:T(8,128)S(1)}) custom-call(bf16[504,128]{1,0:T(8,128)(2,1)S(1)} %get-tuple-element.48.refs_0_, bf16[504,128]{1,0:T(8,128)(2,1)S(1)} %collective-permute-done.5.refs_1_, bf16[504,128]{1,0:T(8,128)(2,1)S(1)} %collective-permute-done.6.refs_2_, bf16[504,128]{1,0:T(8,128)(2,1)S(1)} %collective-permute-done.7.refs_3_), custom_call_target="tpu_custom_call" | custom-call | tf_op jit(solution)/shard_map/pallas_call | solution.py:437
  28.2 0.5 %collective-permute-done.4.below = bf16[144,384]{1,0:T(8,128)(2,1)S(1)} collective-permute-done((bf16[144,384]{1,0:T(8,128)(2,1)S(1)}, bf16[144,384]{1,0:T(8,128)(2,1)S(1)}, u32[]{:S(2)}, u32[]{:S(2)}) %collective-permute-start.4) | collective-permute-done | bytes 110624 | tf_op jit(solution)/shard_map/ppermute | solution.py:455
  28.7 0.8 %shard_map.129 = bf16[4,6,24,192]{3,2,1,0:T(8,128)(2,1)} custom-call(bf16[2,144,192]{2,1,0:T(8,128)(2,1)S(1)} %get-tuple-element.46.inner, bf16[144,384]{1,0:T(8,128)(2,1)S(1)} %collective-permute-done.4.below, f32[8,128]{1,0:T(8,128)S(1)} %get-tuple-element.52.after), custom_call_target="tpu_custom_call" | custom-call | tf_op jit(solution)/shard_map/pallas_call | solution.py:437
Async XLA Ops:
  2.1 9.4 %collective-permute-start = (bf16[2,112,384]{2,1,0:T(8,128)(2,1)S(1)}, bf16[2,112,384]{2,1,0:T(8,128)(2,1)S(1)}, u32[]{:S(2)}, u32[]{:S(2)}) collective-permute-start(bf16[2,112,384]{2,1,0:T(8,128)(2,1)S(1)} %get-tuple-element.29), channel_id=1, source_target_pairs={{0,28},{1,29},{2,30},{3,31},{4,0},{5,1},{6,2},{7,3},{8,4},{9,5},{1... | collective-permute-start | bytes 516104 | tf_op jit(solution)/shard_map/ppermute | solution.py:455
  6.6 6.8 %collective-permute-start.1 = (bf16[2,48,384]{2,1,0:T(8,128)(2,1)S(1)}, bf16[2,48,384]{2,1,0:T(8,128)(2,1)S(1)}, u32[]{:S(2)}, u32[]{:S(2)}) collective-permute-start(bf16[2,48,384]{2,1,0:T(8,128)(2,1)S(1)} %get-tuple-element.38), channel_id=1, source_target_pairs={{0,3},{1,0},{2,1},{3,2},{4,7},{5,4},{6,5},{7,6},{8,11},{9,8},{10,9... | collective-permute-start | bytes 221192 | tf_op jit(solution)/shard_map/ppermute | solution.py:455
  9.1 4.3 %collective-permute-start.2 = (bf16[2,48,384]{2,1,0:T(8,128)(2,1)S(1)}, bf16[2,48,384]{2,1,0:T(8,128)(2,1)S(1)}, u32[]{:S(2)}, u32[]{:S(2)}) collective-permute-start(bf16[2,48,384]{2,1,0:T(8,128)(2,1)S(1)} %get-tuple-element.39), channel_id=1, source_target_pairs={{0,31},{1,28},{2,29},{3,30},{4,3},{5,0},{6,1},{7,2},{8,7},{9,4},{1... | collective-permute-start | bytes 221192 | tf_op jit(solution)/shard_map/ppermute | solution.py:455
  9.4 1.5 %copy-start = (f32[2,1,6,144,144]{4,3,2,1,0:T(8,128)S(1)}, f32[2,1,6,144,144]{4,3,2,1,0:T(8,128)}, u32[]{:S(2)}) copy-start(f32[2,1,6,144,144]{4,3,2,1,0:T(8,128)} %param.16) | copy-start | bytes 2985988
  10.9 0.9 %copy-start.1 = (bf16[192,576]{1,0:T(8,128)(2,1)S(1)}, bf16[192,576]{1,0:T(8,128)(2,1)}, u32[]{:S(2)}) copy-start(bf16[192,576]{1,0:T(8,128)(2,1)} %refs_8_.2) | copy-start | bytes 663556
  10.9 1.0 %copy-start.4 = (bf16[192,192]{1,0:T(8,128)(2,1)S(1)}, bf16[192,192]{1,0:T(8,128)(2,1)}, u32[]{:S(2)}) copy-start(bf16[192,192]{1,0:T(8,128)(2,1)} %refs_6_.2) | copy-start | bytes 221188
  10.9 1.0 %copy-start.7 = (f32[192]{0:T(256)S(1)}, f32[192]{0:T(256)}, u32[]{:S(2)}) copy-start(f32[192]{0:T(256)} %param.13) | copy-start | bytes 2308
  10.9 1.1 %copy-start.8 = (bf16[144,256]{1,0:T(8,128)(2,1)S(1)}, bf16[144,256]{1,0:T(8,128)(2,1)}, u32[]{:S(2)}) copy-start(bf16[144,256]{1,0:T(8,128)(2,1)} %constant.10.clone.refs_6_) | copy-start | bytes 221188
  12.0 1.4 %copy-start.2 = (bf16[368,144]{1,0:T(8,128)(2,1)S(1)}, bf16[368,144]{1,0:T(8,128)(2,1)}, u32[]{:S(2)}) copy-start(bf16[368,144]{1,0:T(8,128)(2,1)} %constant.12.clone.refs_10_) | copy-start | bytes 317956
  12.0 1.4 %copy-start.5 = (bf16[144,256]{1,0:T(8,128)(2,1)S(1)}, bf16[144,256]{1,0:T(8,128)(2,1)}, u32[]{:S(2)}) copy-start(bf16[144,256]{1,0:T(8,128)(2,1)} %constant.11.clone.refs_8_) | copy-start | bytes 221188
  13.4 7.6 %copy-start.3 = (bf16[288,144]{1,0:T(8,128)(2,1)S(1)}, bf16[288,144]{1,0:T(8,128)(2,1)}, u32[]{:S(2)}) copy-start(bf16[288,144]{1,0:T(8,128)(2,1)} %constant.13.clone.refs_9_) | copy-start | bytes 248836
  16.0 6.4 %collective-permute-start.3 = (bf16[2,80,192]{2,1,0:T(8,128)(2,1)S(1)}, bf16[2,80,192]{2,1,0:T(8,128)(2,1)S(1)}, u32[]{:S(2)}, u32[]{:S(2)}) collective-permute-start(bf16[2,80,192]{2,1,0:T(8,128)(2,1)S(1)} %get-tuple-element.45), channel_id=1, source_target_pairs={{0,1},{1,2},{2,3},{3,0},{4,5},{5,6},{6,7},{7,4},{8,9},{9,10},{10,1... | collective-permute-start | bytes 184328 | tf_op jit(solution)/shard_map/ppermute | solution.py:455
  17.6 6.4 %collective-permute-start.5 = (bf16[504,128]{1,0:T(8,128)(2,1)S(1)}, bf16[504,128]{1,0:T(8,128)(2,1)S(1)}, u32[]{:S(2)}, u32[]{:S(2)}) collective-permute-start(bf16[504,128]{1,0:T(8,128)(2,1)S(1)} %get-tuple-element.49), channel_id=1, source_target_pairs={{0,1},{1,0},{2,3},{3,2},{4,5},{5,4},{6,7},{7,6},{8,9},{9,8},{10,11... | collective-permute-start | bytes 387080 | tf_op jit(solution)/shard_map/ppermute | solution.py:529
  18.0 7.0 %collective-permute-start.6 = (bf16[504,128]{1,0:T(8,128)(2,1)S(1)}, bf16[504,128]{1,0:T(8,128)(2,1)S(1)}, u32[]{:S(2)}, u32[]{:S(2)}) collective-permute-start(bf16[504,128]{1,0:T(8,128)(2,1)S(1)} %get-tuple-element.50), channel_id=1, source_target_pairs={{0,2},{1,3},{2,0},{3,1},{4,6},{5,7},{6,4},{7,5},{8,10},{9,11},{10,... | collective-permute-start | bytes 387080 | tf_op jit(solution)/shard_map/ppermute | solution.py:529
  19.6 7.6 %collective-permute-start.7 = (bf16[504,128]{1,0:T(8,128)(2,1)S(1)}, bf16[504,128]{1,0:T(8,128)(2,1)S(1)}, u32[]{:S(2)}, u32[]{:S(2)}) collective-permute-start(bf16[504,128]{1,0:T(8,128)(2,1)S(1)} %get-tuple-element.51), channel_id=1, source_target_pairs={{0,3},{1,2},{2,1},{3,0},{4,7},{5,6},{6,5},{7,4},{8,11},{9,10},{10,... | collective-permute-start | bytes 387080 | tf_op jit(solution)/shard_map/ppermute | solution.py:529
  21.1 1.4 %copy-start.6 = (bf16[288,80]{1,0:T(8,128)(2,1)S(1)}, bf16[288,80]{1,0:T(8,128)(2,1)}, u32[]{:S(2)}) copy-start(bf16[288,80]{1,0:T(8,128)(2,1)} %constant.14.clone.order_t) | copy-start | bytes 138244
  22.7 6.0 %collective-permute-start.4 = (bf16[144,384]{1,0:T(8,128)(2,1)S(1)}, bf16[144,384]{1,0:T(8,128)(2,1)S(1)}, u32[]{:S(2)}, u32[]{:S(2)}) collective-permute-start(bf16[144,384]{1,0:T(8,128)(2,1)S(1)} %get-tuple-element.47), channel_id=1, source_target_pairs={{0,4},{1,5},{2,6},{3,7},{4,8},{5,9},{6,10},{7,11},{8,12},{9,13},{1... | collective-permute-start | bytes 331784 | tf_op jit(solution)/shard_map/ppermute | solution.py:455

commit v8 on v7

--- a/solution.py
+++ b/solution.py
@@ -106,7 +106,7 @@
     cols = both.shape[2]
     kept = cols - HALF_COLS
     shape = (below.shape[1], WZ * HALF_ROWS * cols)
-    row = lax.broadcasted_iota(jnp.int32, shape, 0)
+    row = lax.broadcasted_iota(jnp.int32, (shape[0], 1), 0)
     target = row + HALF_COLS
     for i in range(1, WZ * HALF_ROWS):
         target += jnp.where(row >= i * kept, HALF_COLS, 0)

time: 29.7 us -> 29.7 us (level)
  no operation moved by 1% of the time
where the time goes in v8:
time: 29.7 us; the launch traced here: 29.5 us
  starting transfers between devices  12.4 us (42%)
  Pallas kernels  8.27 us (28%)
  waiting for transfers between devices  4.89 us (16%)
  local copies, waits for them, and re-layouts  1.97 us (7%)
  other arithmetic  1.21 us (4%)
  between operations  0.76 us (3%)
    ppermute x5, starting transfers between devices, shift(): return lax.ppermute(value, ('lat', 'lon'), pairs)  8.96 us
    pallas_call x8, Pallas kernels, call(): pl.pallas_call(kernel, out_shape=outs, in_specs=vmem(len(args)), out_spec...  8.27 us
    ppermute x3, waiting for transfers between devices, local(): arrived.append(lax.ppermute(results[3 + d], 'lon', pairs))  4.33 us
    ppermute x3, starting transfers between devices, local(): arrived.append(lax.ppermute(results[3 + d], 'lon', pairs))  3.49 us
    unnamed x18, local copies, waits for them, and re-layouts  1.97 us
    concatenate x1, other arithmetic, local(): both = jnp.concatenate([tokens, cotangent], axis=-1)  1.21 us
  transfers between devices with their start and end apart: 8, of which 4 were waited for; matrix products, arithmetic and copies ran while one was open for 0% of the time, Pallas kernels for 16%

profile of v8, /device:TPU:0, one launch (start us, length us, event | category | flops | bytes accessed | tf_op | source)
XLA Modules:
  0.0 29.5 jit_solution(15616675520182784944)
XLA Ops:
  0.6 1.2 %pad_maximum_fusion.both = bf16[4,6,24,384]{3,2,1,0:T(8,128)(2,1)S(1)} fusion(bf16[4,6,24,192]{3,2,1,0:T(8,128)(2,1)} %param.12, bf16[4,6,24,192]{3,2,1,0:T(8,128)(2,1)} %param.11), kind=kLoop, calls=%fused_computation | loop fusion | flops 884736 | bytes 884736 | tf_op jit(solution)/shard_map/concatenate | solution.py:470
  1.8 0.2 shard_map.122
  2.1 4.5 %collective-permute-start = (bf16[2,112,384]{2,1,0:T(8,128)(2,1)S(1)}, bf16[2,112,384]{2,1,0:T(8,128)(2,1)S(1)}, u32[]{:S(2)}, u32[]{:S(2)}) collective-permute-start(bf16[2,112,384]{2,1,0:T(8,128)(2,1)S(1)} %get-tuple-element.29), channel_id=1, source_target_pairs={{0,28},{1,29},{2,30},{3,31},{4,0},{5,1},{6,2},{7,3},{8,4},{9,5},{1... | collective-permute-start | bytes 516104 | tf_op jit(solution)/shard_map/ppermute | solution.py:455
  6.6 2.4 %collective-permute-start.1 = (bf16[2,48,384]{2,1,0:T(8,128)(2,1)S(1)}, bf16[2,48,384]{2,1,0:T(8,128)(2,1)S(1)}, u32[]{:S(2)}, u32[]{:S(2)}) collective-permute-start(bf16[2,48,384]{2,1,0:T(8,128)(2,1)S(1)} %get-tuple-element.38), channel_id=1, source_target_pairs={{0,3},{1,0},{2,1},{3,2},{4,7},{5,4},{6,5},{7,6},{8,11},{9,8},{10,9... | collective-permute-start | bytes 221192 | tf_op jit(solution)/shard_map/ppermute | solution.py:455
  9.1 0.4 %collective-permute-start.2 = (bf16[2,48,384]{2,1,0:T(8,128)(2,1)S(1)}, bf16[2,48,384]{2,1,0:T(8,128)(2,1)S(1)}, u32[]{:S(2)}, u32[]{:S(2)}) collective-permute-start(bf16[2,48,384]{2,1,0:T(8,128)(2,1)S(1)} %get-tuple-element.39), channel_id=1, source_target_pairs={{0,31},{1,28},{2,29},{3,30},{4,3},{5,0},{6,1},{7,2},{8,7},{9,4},{1... | collective-permute-start | bytes 221192 | tf_op jit(solution)/shard_map/ppermute | solution.py:455
  9.4 0.0 copy-start
  9.4 1.5 %copy-done = f32[2,1,6,144,144]{4,3,2,1,0:T(8,128)S(1)} copy-done((f32[2,1,6,144,144]{4,3,2,1,0:T(8,128)S(1)}, f32[2,1,6,144,144]{4,3,2,1,0:T(8,128)}, u32[]{:S(2)}) %copy-start) | copy-done | bytes 995352
  10.9 0.0 copy-start.1
  10.9 0.0 copy-start.4
  10.9 0.0 copy-start.7
  10.9 0.0 copy-start.8
  10.9 0.6 %shard_map.123.refs_5_.refs_7_ = f32[2,4,144,256]{3,2,1,0:T(8,128)S(1)} custom-call(f32[2,6,144,144]{3,2,1,0:T(8,128)S(1)} %bitcast.3), custom_call_target="tpu_custom_call" | custom-call | tf_op jit(solution)/shard_map/pallas_call | solution.py:437
  11.5 0.0 collective-permute-done.refs_1_
  11.5 0.3 %copy-done.1 = bf16[192,576]{1,0:T(8,128)(2,1)S(1)} copy-done((bf16[192,576]{1,0:T(8,128)(2,1)S(1)}, bf16[192,576]{1,0:T(8,128)(2,1)}, u32[]{:S(2)}) %copy-start.1) | copy-done | bytes 221208
  11.8 0.1 copy-done.4
  11.9 0.0 copy-done.7
  11.9 0.1 copy-done.8
  12.0 0.0 copy-start.2
  12.0 0.0 copy-start.5
  12.0 1.4 %shard_map.124 = (f32[288,192]{1,0:T(8,128)S(1)}, f32[288,128]{1,0:T(8,128)S(1)}, bf16[288,192]{1,0:T(8,128)(2,1)S(1)}, f32[288,192]{1,0:T(8,128)S(1)}, f32[288,...) custom-call(bf16[2,144,384]{2,1,0:T(8,128)(2,1)S(1)} %get-tuple-elem, ...), custom_call_target="tpu_custom_call" | custom-call | flops 1000000000 | tf_op jit(solution)/shard_map/pallas_call | solution.py:437
  13.4 0.0 collective-permute-done.1.refs_2_
  13.4 0.0 collective-permute-done.2.refs_3_
  13.4 0.0 copy-done.2
  13.4 0.0 copy-done.5
  13.4 0.0 copy-start.3
  13.4 2.6 %shard_map.125 = (bf16[2,144,192]{2,1,0:T(8,128)(2,1)S(1)}, bf16[2,144,192]{2,1,0:T(8,128)(2,1)S(1)}, bf16[2,80,192]{2,1,0:T(8,128)(2,1)S(1)}, bf16[504,128]{1,0...) custom-call(bf16[2,48,384]{2,1,0:T(8,128)(2,1)S(1)} %get-tuple-element., ...), custom_call_target="tpu_custom_call" | custom-call | tf_op jit(solution)/shard_map/pallas_call | solution.py:437
  16.0 1.5 %collective-permute-start.3 = (bf16[2,80,192]{2,1,0:T(8,128)(2,1)S(1)}, bf16[2,80,192]{2,1,0:T(8,128)(2,1)S(1)}, u32[]{:S(2)}, u32[]{:S(2)}) collective-permute-start(bf16[2,80,192]{2,1,0:T(8,128)(2,1)S(1)} %get-tuple-element.45), channel_id=1, source_target_pairs={{0,1},{1,2},{2,3},{3,0},{4,5},{5,6},{6,7},{7,4},{8,9},{9,10},{10,1... | collective-permute-start | bytes 184328 | tf_op jit(solution)/shard_map/ppermute | solution.py:455
  17.6 0.5 %collective-permute-start.5 = (bf16[504,128]{1,0:T(8,128)(2,1)S(1)}, bf16[504,128]{1,0:T(8,128)(2,1)S(1)}, u32[]{:S(2)}, u32[]{:S(2)}) collective-permute-start(bf16[504,128]{1,0:T(8,128)(2,1)S(1)} %get-tuple-element.49), channel_id=1, source_target_pairs={{0,1},{1,0},{2,3},{3,2},{4,5},{5,4},{6,7},{7,6},{8,9},{9,8},{10,11... | collective-permute-start | bytes 387080 | tf_op jit(solution)/shard_map/ppermute | solution.py:529
  18.0 1.5 %collective-permute-start.6 = (bf16[504,128]{1,0:T(8,128)(2,1)S(1)}, bf16[504,128]{1,0:T(8,128)(2,1)S(1)}, u32[]{:S(2)}, u32[]{:S(2)}) collective-permute-start(bf16[504,128]{1,0:T(8,128)(2,1)S(1)} %get-tuple-element.50), channel_id=1, source_target_pairs={{0,2},{1,3},{2,0},{3,1},{4,6},{5,7},{6,4},{7,5},{8,10},{9,11},{10,... | collective-permute-start | bytes 387080 | tf_op jit(solution)/shard_map/ppermute | solution.py:529
  19.6 1.5 %collective-permute-start.7 = (bf16[504,128]{1,0:T(8,128)(2,1)S(1)}, bf16[504,128]{1,0:T(8,128)(2,1)S(1)}, u32[]{:S(2)}, u32[]{:S(2)}) collective-permute-start(bf16[504,128]{1,0:T(8,128)(2,1)S(1)} %get-tuple-element.51), channel_id=1, source_target_pairs={{0,3},{1,2},{2,1},{3,0},{4,7},{5,6},{6,5},{7,4},{8,11},{9,10},{10,... | collective-permute-start | bytes 387080 | tf_op jit(solution)/shard_map/ppermute | solution.py:529
  21.0 0.0 copy-done.3
  21.1 0.0 copy-start.6
  21.1 1.4 %shard_map.126 = (bf16[2,144,192]{2,1,0:T(8,128)(2,1)S(1)}, bf16[2,144,192]{2,1,0:T(8,128)(2,1)S(1)}) custom-call(f32[288,192]{1,0:T(8,128)S(1)} %get-tuple-element.30.refs_0_, f32[288,128]{1,0:T(8,128)S(1)} %get-tuple-element.31.refs_1_, bf16[288,192]{1,0:T(8,128)(2,1)S(1)} %get-tuple-element.32.refs_2_, f32[288,192]{1,0:T(8,128)S(1)} %get-tuple-element.33.refs_3_, ...), custom_call_target="tpu_custom_call" | custom-call | tf_op jit(solution)/shard_map/pallas_call | solution.py:437
  22.4 0.0 collective-permute-done.3.side
  22.4 0.0 copy-done.6
  22.4 0.3 shard_map.127
  22.7 0.1 collective-permute-start.4
  22.8 1.2 %collective-permute-done.5.refs_1_ = bf16[504,128]{1,0:T(8,128)(2,1)S(1)} collective-permute-done((bf16[504,128]{1,0:T(8,128)(2,1)S(1)}, bf16[504,128]{1,0:T(8,128)(2,1)S(1)}, u32[]{:S(2)}, u32[]{:S(2)}) %collective-permute-start.5) | collective-permute-done | bytes 129056 | tf_op jit(solution)/shard_map/ppermute | solution.py:529
  23.9 1.1 %collective-permute-done.6.refs_2_ = bf16[504,128]{1,0:T(8,128)(2,1)S(1)} collective-permute-done((bf16[504,128]{1,0:T(8,128)(2,1)S(1)}, bf16[504,128]{1,0:T(8,128)(2,1)S(1)}, u32[]{:S(2)}, u32[]{:S(2)}) %collective-permute-start.6) | collective-permute-done | bytes 129056 | tf_op jit(solution)/shard_map/ppermute | solution.py:529
  25.0 2.1 %collective-permute-done.7.refs_3_ = bf16[504,128]{1,0:T(8,128)(2,1)S(1)} collective-permute-done((bf16[504,128]{1,0:T(8,128)(2,1)S(1)}, bf16[504,128]{1,0:T(8,128)(2,1)S(1)}, u32[]{:S(2)}, u32[]{:S(2)}) %collective-permute-start.7) | collective-permute-done | bytes 129056 | tf_op jit(solution)/shard_map/ppermute | solution.py:529
  27.1 1.1 %shard_map.128 = (f32[432,1,144]{2,1,0:T(1,128)}, f32[8,128]{1,0:T(8,128)S(1)}) custom-call(bf16[504,128]{1,0:T(8,128)(2,1)S(1)} %get-tuple-element.48.refs_0_, bf16[504,128]{1,0:T(8,128)(2,1)S(1)} %collective-permute-done.5.refs_1_, bf16[504,128]{1,0:T(8,128)(2,1)S(1)} %collective-permute-done.6.refs_2_, bf16[504,128]{1,0:T(8,128)(2,1)S(1)} %collective-permute-done.7.refs_3_), custom_call_target="tpu_custom_call" | custom-call | tf_op jit(solution)/shard_map/pallas_call | solution.py:437
  28.2 0.5 %collective-permute-done.4.below = bf16[144,384]{1,0:T(8,128)(2,1)S(1)} collective-permute-done((bf16[144,384]{1,0:T(8,128)(2,1)S(1)}, bf16[144,384]{1,0:T(8,128)(2,1)S(1)}, u32[]{:S(2)}, u32[]{:S(2)}) %collective-permute-start.4) | collective-permute-done | bytes 110624 | tf_op jit(solution)/shard_map/ppermute | solution.py:455
  28.7 0.8 %shard_map.129 = bf16[4,6,24,192]{3,2,1,0:T(8,128)(2,1)} custom-call(bf16[2,144,192]{2,1,0:T(8,128)(2,1)S(1)} %get-tuple-element.46.inner, bf16[144,384]{1,0:T(8,128)(2,1)S(1)} %collective-permute-done.4.below, f32[8,128]{1,0:T(8,128)S(1)} %get-tuple-element.52.after), custom_call_target="tpu_custom_call" | custom-call | tf_op jit(solution)/shard_map/pallas_call | solution.py:437
Async XLA Ops:
  2.1 9.4 %collective-permute-start = (bf16[2,112,384]{2,1,0:T(8,128)(2,1)S(1)}, bf16[2,112,384]{2,1,0:T(8,128)(2,1)S(1)}, u32[]{:S(2)}, u32[]{:S(2)}) collective-permute-start(bf16[2,112,384]{2,1,0:T(8,128)(2,1)S(1)} %get-tuple-element.29), channel_id=1, source_target_pairs={{0,28},{1,29},{2,30},{3,31},{4,0},{5,1},{6,2},{7,3},{8,4},{9,5},{1... | collective-permute-start | bytes 516104 | tf_op jit(solution)/shard_map/ppermute | solution.py:455
  6.6 6.8 %collective-permute-start.1 = (bf16[2,48,384]{2,1,0:T(8,128)(2,1)S(1)}, bf16[2,48,384]{2,1,0:T(8,128)(2,1)S(1)}, u32[]{:S(2)}, u32[]{:S(2)}) collective-permute-start(bf16[2,48,384]{2,1,0:T(8,128)(2,1)S(1)} %get-tuple-element.38), channel_id=1, source_target_pairs={{0,3},{1,0},{2,1},{3,2},{4,7},{5,4},{6,5},{7,6},{8,11},{9,8},{10,9... | collective-permute-start | bytes 221192 | tf_op jit(solution)/shard_map/ppermute | solution.py:455
  9.1 4.3 %collective-permute-start.2 = (bf16[2,48,384]{2,1,0:T(8,128)(2,1)S(1)}, bf16[2,48,384]{2,1,0:T(8,128)(2,1)S(1)}, u32[]{:S(2)}, u32[]{:S(2)}) collective-permute-start(bf16[2,48,384]{2,1,0:T(8,128)(2,1)S(1)} %get-tuple-element.39), channel_id=1, source_target_pairs={{0,31},{1,28},{2,29},{3,30},{4,3},{5,0},{6,1},{7,2},{8,7},{9,4},{1... | collective-permute-start | bytes 221192 | tf_op jit(solution)/shard_map/ppermute | solution.py:455
  9.4 1.5 %copy-start = (f32[2,1,6,144,144]{4,3,2,1,0:T(8,128)S(1)}, f32[2,1,6,144,144]{4,3,2,1,0:T(8,128)}, u32[]{:S(2)}) copy-start(f32[2,1,6,144,144]{4,3,2,1,0:T(8,128)} %param.16) | copy-start | bytes 2985988
  10.9 0.9 %copy-start.1 = (bf16[192,576]{1,0:T(8,128)(2,1)S(1)}, bf16[192,576]{1,0:T(8,128)(2,1)}, u32[]{:S(2)}) copy-start(bf16[192,576]{1,0:T(8,128)(2,1)} %refs_8_.2) | copy-start | bytes 663556
  10.9 1.0 %copy-start.4 = (bf16[192,192]{1,0:T(8,128)(2,1)S(1)}, bf16[192,192]{1,0:T(8,128)(2,1)}, u32[]{:S(2)}) copy-start(bf16[192,192]{1,0:T(8,128)(2,1)} %refs_6_.2) | copy-start | bytes 221188
  10.9 1.0 %copy-start.7 = (f32[192]{0:T(256)S(1)}, f32[192]{0:T(256)}, u32[]{:S(2)}) copy-start(f32[192]{0:T(256)} %param.13) | copy-start | bytes 2308
  10.9 1.1 %copy-start.8 = (bf16[144,256]{1,0:T(8,128)(2,1)S(1)}, bf16[144,256]{1,0:T(8,128)(2,1)}, u32[]{:S(2)}) copy-start(bf16[144,256]{1,0:T(8,128)(2,1)} %constant.10.clone.refs_6_) | copy-start | bytes 221188
  12.0 1.4 %copy-start.2 = (bf16[368,144]{1,0:T(8,128)(2,1)S(1)}, bf16[368,144]{1,0:T(8,128)(2,1)}, u32[]{:S(2)}) copy-start(bf16[368,144]{1,0:T(8,128)(2,1)} %constant.12.clone.refs_10_) | copy-start | bytes 317956
  12.0 1.4 %copy-start.5 = (bf16[144,256]{1,0:T(8,128)(2,1)S(1)}, bf16[144,256]{1,0:T(8,128)(2,1)}, u32[]{:S(2)}) copy-start(bf16[144,256]{1,0:T(8,128)(2,1)} %constant.11.clone.refs_8_) | copy-start | bytes 221188
  13.4 7.6 %copy-start.3 = (bf16[288,144]{1,0:T(8,128)(2,1)S(1)}, bf16[288,144]{1,0:T(8,128)(2,1)}, u32[]{:S(2)}) copy-start(bf16[288,144]{1,0:T(8,128)(2,1)} %constant.13.clone.refs_9_) | copy-start | bytes 248836
  16.0 6.4 %collective-permute-start.3 = (bf16[2,80,192]{2,1,0:T(8,128)(2,1)S(1)}, bf16[2,80,192]{2,1,0:T(8,128)(2,1)S(1)}, u32[]{:S(2)}, u32[]{:S(2)}) collective-permute-start(bf16[2,80,192]{2,1,0:T(8,128)(2,1)S(1)} %get-tuple-element.45), channel_id=1, source_target_pairs={{0,1},{1,2},{2,3},{3,0},{4,5},{5,6},{6,7},{7,4},{8,9},{9,10},{10,1... | collective-permute-start | bytes 184328 | tf_op jit(solution)/shard_map/ppermute | solution.py:455
  17.6 6.4 %collective-permute-start.5 = (bf16[504,128]{1,0:T(8,128)(2,1)S(1)}, bf16[504,128]{1,0:T(8,128)(2,1)S(1)}, u32[]{:S(2)}, u32[]{:S(2)}) collective-permute-start(bf16[504,128]{1,0:T(8,128)(2,1)S(1)} %get-tuple-element.49), channel_id=1, source_target_pairs={{0,1},{1,0},{2,3},{3,2},{4,5},{5,4},{6,7},{7,6},{8,9},{9,8},{10,11... | collective-permute-start | bytes 387080 | tf_op jit(solution)/shard_map/ppermute | solution.py:529
  18.0 7.0 %collective-permute-start.6 = (bf16[504,128]{1,0:T(8,128)(2,1)S(1)}, bf16[504,128]{1,0:T(8,128)(2,1)S(1)}, u32[]{:S(2)}, u32[]{:S(2)}) collective-permute-start(bf16[504,128]{1,0:T(8,128)(2,1)S(1)} %get-tuple-element.50), channel_id=1, source_target_pairs={{0,2},{1,3},{2,0},{3,1},{4,6},{5,7},{6,4},{7,5},{8,10},{9,11},{10,... | collective-permute-start | bytes 387080 | tf_op jit(solution)/shard_map/ppermute | solution.py:529
  19.6 7.6 %collective-permute-start.7 = (bf16[504,128]{1,0:T(8,128)(2,1)S(1)}, bf16[504,128]{1,0:T(8,128)(2,1)S(1)}, u32[]{:S(2)}, u32[]{:S(2)}) collective-permute-start(bf16[504,128]{1,0:T(8,128)(2,1)S(1)} %get-tuple-element.51), channel_id=1, source_target_pairs={{0,3},{1,2},{2,1},{3,0},{4,7},{5,6},{6,5},{7,4},{8,11},{9,10},{10,... | collective-permute-start | bytes 387080 | tf_op jit(solution)/shard_map/ppermute | solution.py:529
  21.1 1.4 %copy-start.6 = (bf16[288,80]{1,0:T(8,128)(2,1)S(1)}, bf16[288,80]{1,0:T(8,128)(2,1)}, u32[]{:S(2)}) copy-start(bf16[288,80]{1,0:T(8,128)(2,1)} %constant.14.clone.order_t) | copy-start | bytes 138244
  22.7 6.0 %collective-permute-start.4 = (bf16[144,384]{1,0:T(8,128)(2,1)S(1)}, bf16[144,384]{1,0:T(8,128)(2,1)S(1)}, u32[]{:S(2)}, u32[]{:S(2)}) collective-permute-start(bf16[144,384]{1,0:T(8,128)(2,1)S(1)} %get-tuple-element.47), channel_id=1, source_target_pairs={{0,4},{1,5},{2,6},{3,7},{4,8},{5,9},{6,10},{7,11},{8,12},{9,13},{1... | collective-permute-start | bytes 331784 | tf_op jit(solution)/shard_map/ppermute | solution.py:455
